TPU v7x, 32 devices: a whole 2x2x4 slice. The times are simulated.
32 devices in a mesh: row: 4 (over y, core), col: 8 (over z, x).
Axes of the slice: x: 2, y: 2, z: 4, core: 2. Of those that a mesh axis runs over, the one named last changes fastest.
Arguments:
- a_window: bfloat16 [320, 1024], P('row', 'col'), may hold values from -60 to 60, as said below
- b_section: bfloat16 [4096, 8192], P('row', 'col'), may hold values from -60 to 60, as said below
- owners: int32 [4, 8, 10, 16, 1], P('row', 'col'), may hold values from 0 to 31; in each aligned block of 160 rows (0 to 159, 160 to 319, ..., all dimensions but the last counted through in order) at most 8 rows name the same one
- pos_rows: int32 [40, 128], P('row', 'col'), may hold values from 80 to 944
- pos_cols: int32 [40, 128], P('row', 'col'), may hold values from 80 to 944
- peaks: int32 [2, 40, 128], P(None, 'row', 'col'), may hold values from -4 to 4
Outputs:
- relaxed_flow: float32 [2, 40, 128], P(None, 'row', 'col')
- runner: float32 [40, 128], P('row', 'col')
Inputs may be any that keep to these rules, and one draw needn't show every extreme that they name: No owner is named by more than 8 nodes of one device; some owner is named by exactly 8 nodes of one device; owners are unevenly loaded. `a_window`: pixel intensities. `b_section`: pixel intensities.
All inputs are finite; a program needn't handle non-finite values.
Results may differ from a plain program's by a relative error of at most 0.0057.
Values may be sent and summed in bfloat16 or wider, within the bound.
No kernel may reach another device: no remote copies, remote signals or barrier semaphores. Data moves between devices by JAX's collectives and lax.ppermute only.
A program may use at most 128 MiB of HBM per device.

v0:
```python
import math

import jax
import jax.numpy as jnp
from jax import lax
from jax.sharding import PartitionSpec as P

PATCH = 160
STRIDE = 8
RELAX = 2


sharpness = 80.0
epsilon = 1e-06
stiffness = 0.24
centre_reach = 2


def padded(block, sides, width):
    for axis, dim in sides:
        count = lax.axis_size(axis)
        forward = [(i, i + 1) for i in range(count - 1)]
        backward = [(target, source) for source, target in forward]
        low = lax.ppermute(
            lax.slice_in_dim(block, block.shape[dim] - width, None, axis=dim), axis, forward
        )
        high = lax.ppermute(lax.slice_in_dim(block, 0, width, axis=dim), axis, backward)
        block = jnp.concatenate([low, block, high], axis=dim)
    return block


def dft_tables(extent):
    indices = jnp.arange(extent, dtype=jnp.int32)
    product = indices[:, None] * indices[None, :] % extent
    angles = product.astype(jnp.float32) * (2.0 * math.pi / extent)
    return (jnp.cos(angles).astype(jnp.bfloat16), jnp.sin(angles).astype(jnp.bfloat16))


def batched(left_fourier_table, stacked_pairs):
    return jnp.einsum(
        "dr,xre->xde", left_fourier_table, stacked_pairs, preferred_element_type=jnp.float32
    )


def spectrum(patch_stack, right_table, left_fourier_table):
    shift_magnitude, extent = (patch_stack.shape[0], patch_stack.shape[1])
    halves = jnp.dot(
        patch_stack.reshape(shift_magnitude * extent, extent),
        right_table,
        preferred_element_type=jnp.float32,
    )
    halves = halves.astype(jnp.bfloat16).reshape(shift_magnitude, extent, 2 * extent)
    real_part = halves[:, :, :extent]
    imag_part = halves[:, :, extent:]
    stacked_pairs = jnp.concatenate(
        [halves, jnp.concatenate([imag_part, -real_part], axis=2)], axis=1
    )
    return batched(left_fourier_table, stacked_pairs)


def correlate(first, second, peak_rows, peak_cols):
    shift_magnitude, extent = (first.shape[0], first.shape[1])
    cosine, sine = dft_tables(extent)
    right_table = jnp.concatenate([cosine, -sine], axis=1)
    left_fourier_table = jnp.concatenate([cosine, sine], axis=1)
    back_table = jnp.concatenate([cosine, -sine], axis=0)
    spec_first = spectrum(first, right_table, left_fourier_table)
    spec_second = spectrum(second, right_table, left_fourier_table)
    first_real = spec_first[:, :, :extent]
    first_spectrum_imaginary = spec_first[:, :, extent:]
    second_real = spec_second[:, :, :extent]
    second_imag = spec_second[:, :, extent:]
    cross_real = first_real * second_real + first_spectrum_imaginary * second_imag
    cross_imag = first_real * second_imag - first_spectrum_imaginary * second_real
    cross = jnp.concatenate([cross_real, cross_imag], axis=2).astype(jnp.bfloat16)
    cross_real_b = cross[:, :, :extent]
    cross_imag_b = cross[:, :, extent:]
    stacked_pairs = jnp.concatenate(
        [cross, jnp.concatenate([-cross_imag_b, cross_real_b], axis=2)], axis=1
    )
    inverse_half = batched(left_fourier_table, stacked_pairs).astype(jnp.bfloat16)
    correlation = jnp.dot(
        inverse_half.reshape(shift_magnitude * extent, 2 * extent),
        back_table,
        preferred_element_type=jnp.float32,
    )
    correlation = correlation.reshape(shift_magnitude, extent, extent)
    energy_first = jnp.mean(jnp.square(first.astype(jnp.float32)), axis=(1, 2))
    energy_second = jnp.mean(jnp.square(second.astype(jnp.float32)), axis=(1, 2))
    scaling = (
        float(extent * extent * extent * extent)
        * jnp.sqrt(energy_first + epsilon)
        * jnp.sqrt(energy_second + epsilon)
    )
    score = correlation / scaling[:, None, None]
    positions = jnp.arange(extent, dtype=jnp.int32)
    shift_rows = (positions[None, :] - peak_rows[:, None] + extent // 2) % extent - extent // 2
    shift_cols = (positions[None, :] - peak_cols[:, None] + extent // 2) % extent - extent // 2
    near = (jnp.abs(shift_rows) <= centre_reach)[:, :, None] & (
        jnp.abs(shift_cols) <= centre_reach
    )[:, None, :]
    weights = jnp.where(near, jnp.exp(sharpness * score), 0.0)
    total = jnp.sum(weights, axis=(1, 2))
    moment_rows = jnp.sum(weights * shift_rows[:, :, None].astype(jnp.float32), axis=(1, 2))
    moment_cols = jnp.sum(weights * shift_cols[:, None, :].astype(jnp.float32), axis=(1, 2))
    flow_rows = peak_rows.astype(jnp.float32) + moment_rows / total
    flow_cols = peak_cols.astype(jnp.float32) + moment_cols / total
    runner = jnp.max(jnp.where(near, -2.0, score), axis=(1, 2))
    return (flow_rows, flow_cols, runner)


def neighbours(padded_image):
    return (
        padded_image[:, 2:, 1:-1]
        + padded_image[:, :-2, 1:-1]
        + padded_image[:, 1:-1, 2:]
        + padded_image[:, 1:-1, :-2]
    )


def per_device(a_window, b_section, owners, pos_rows, pos_cols, peaks):
    node_rows, node_cols = pos_rows.shape
    nodes = node_rows * node_cols
    mesh_row_extent = lax.axis_size("row")
    mesh_breadth = lax.axis_size("col")
    devices = mesh_row_extent * mesh_breadth
    capacity = max(2, (nodes * 8 // 5 + devices - 1) // devices)
    half_patch = PATCH // 2
    widened = padded(a_window, (("row", 0), ("col", 1)), half_patch)
    owner_list = owners.reshape(nodes)
    node_order = jnp.arange(nodes, dtype=jnp.int32)
    earlier = (owner_list[None, :] == owner_list[:, None]) & (
        node_order[None, :] < node_order[:, None]
    )
    ranks = jnp.sum(earlier.astype(jnp.int32), axis=1)
    slots = owner_list * capacity + ranks
    slot_order = jnp.arange(devices * capacity, dtype=jnp.int32)
    table = slots[None, :] == slot_order[:, None]
    filled = jnp.any(table, axis=1)
    target_rows = jnp.sum(
        jnp.where(table, pos_rows.reshape(nodes)[None, :], 0), axis=1
    ) + jnp.where(filled, 0, half_patch)
    target_cols = jnp.sum(
        jnp.where(table, pos_cols.reshape(nodes)[None, :], 0), axis=1
    ) + jnp.where(filled, 0, half_patch)
    requests = jnp.stack([target_rows, target_cols], axis=1).reshape(devices, capacity, 2)
    received = lax.all_to_all(requests, ("row", "col"), split_axis=0, concat_axis=0, tiled=True)
    flat_requests = received.reshape(devices * capacity, 2)
    pieces = jax.vmap(
        lambda corner_row, corner_col: lax.dynamic_slice(
            b_section, (corner_row - half_patch, corner_col - half_patch), (PATCH, PATCH)
        )
    )(flat_requests[:, 0], flat_requests[:, 1])
    returned = lax.all_to_all(
        pieces.reshape(devices, capacity, PATCH, PATCH),
        ("row", "col"),
        split_axis=0,
        concat_axis=0,
        tiled=True,
    )
    returned = returned.reshape(devices * capacity, PATCH, PATCH)
    centre_rows = jnp.arange(node_rows, dtype=jnp.int32) * STRIDE + STRIDE // 2
    centre_cols = jnp.arange(node_cols, dtype=jnp.int32) * STRIDE + STRIDE // 2
    a_top = jnp.broadcast_to(centre_rows[:, None], (node_rows, node_cols)).reshape(nodes)
    a_left = jnp.broadcast_to(centre_cols[None, :], (node_rows, node_cols)).reshape(nodes)
    block_size = math.gcd(nodes, 16)
    blocks = nodes // block_size

    def per_block(items):
        a_rows, a_cols, slot_block, peak_rows, peak_cols = items
        first = jax.vmap(
            lambda corner_row, corner_col: lax.dynamic_slice(
                widened, (corner_row, corner_col), (PATCH, PATCH)
            )
        )(a_rows, a_cols)
        second = jnp.take(returned, slot_block, axis=0)
        return correlate(first, second, peak_rows, peak_cols)

    flow_rows, flow_cols, runner = lax.map(
        per_block,
        (
            a_top.reshape(blocks, block_size),
            a_left.reshape(blocks, block_size),
            slots.reshape(blocks, block_size),
            peaks[0],
            peaks[1],
        ),
    )
    field = jnp.stack([flow_rows, flow_cols])
    for relax_step in range(RELAX):
        padded_field = padded(field, (("row", 1), ("col", 2)), 1)
        field = field + stiffness * (neighbours(padded_field) - 4.0 * field)
    return (field, runner)


def solution(mesh):
    placed = (
        P("row", "col"),
        P("row", "col"),
        P("row", "col", None, None, None),
        P("row", "col"),
        P("row", "col"),
        P(None, "row", "col"),
    )
    return jax.shard_map(
        per_device,
        mesh=mesh,
        in_specs=placed,
        out_specs=(P(None, "row", "col"), P("row", "col")),
        check_vma=False,
    )
```

profile of v0, /device:TPU:0, one launch (start us, length us, event | category | flops | bytes accessed | tf_op | source)
XLA Modules:
  0.0 2207.1 jit_solution(6662911707013275782)
XLA Ops:
  18.9 879.2 %while.22 = (s32[]{:T(128)}, bf16[1024,1024]{1,0:T(8,128)(2,1)}, s32[256,2]{0,1:T(2,128)S(1)}, bf16[256,160,160]{2,1,0:T(8,128)(2,1)}, s32[]{:T(128)}) while((s32[]{:T(128)}, bf16[1024,1024]{1,0:T(8,128)(2,1)}, s32[256,2]{0,1:T(2,128)S(1)}, bf16[256,160,160]{2,1,0:T(8,128)(2,1)}, s32[]{:T(128)}) %tuple.107), condition=%wide.while_cond.1, body=%wide.while_body.1.sunk | while | flops 2 | bytes 165473 | solution.py:150
  913.2 155.5 %collective-permute-done.2 = bf16[240,80]{1,0:T(8,128)(2,1)S(1)} collective-permute-done((bf16[240,80]{1,0:T(8,128)(2,1)S(1)}, bf16[240,80]{1,0:T(8,128)(2,1)S(1)}, u32[]{:S(2)}, u32[]{:S(2)}) %collective-permute-start.2) | collective-permute-done | bytes 38432 | tf_op jit(solution)/shard_map/ppermute | solution.py:24
  1068.9 290.0 %all-to-all-done.1 = bf16[32,8,160,160]{3,2,1,0:T(8,128)(2,1)} async-done(((bf16[32,8,160,160]{3,2,1,0:T(8,128)(2,1)}), bf16[32,8,160,160]{3,2,1,0:T(8,128)(2,1)}, u32[]{:S(2)}, u32[]{:S(2)}) %all-to-all-start.1) | async-done | bytes 13107232 | tf_op jit(solution)/shard_map/all_to_all | solution.py:154
  1360.2 790.6 %while.21 = (s32[]{:T(128)}, f32[10,16]{1,0:T(8,128)S(1)}, f32[10,16]{1,0:T(8,128)}, f32[10,16]{1,0:T(8,128)}, s32[10,16]{1,0:T(8,128)}, /*index=5*/s32[10,16]{1...) while((s32[]{:T(128)}, f32[10,16]{1,0:T(8,128)S(1)}, ...), condition=%wide.region_11.12_spmd, body=%wide.region_4.11_spmd.sunk | while | flops 2408761600 | bytes 75701576 | solution.py:179
  1360.9 32.3 %while.23 = (s32[]{:T(128)}, bf16[240,288]{1,0:T(8,128)(2,1)S(1)}, s32[16,2]{0,1:T(2,128)S(1)}, bf16[16,160,160]{2,1,0:T(8,128)(2,1)S(1)}, s32[]{:T(128)}) while((s32[]{:T(128)}, bf16[240,288]{1,0:T(8,128)(2,1)S(1)}, s32[16,2]{0,1:T(2,128)S(1)}, bf16[16,160,160]{2,1,0:T(8,128)(2,1)S(1)}, s32[]{:T(128)}) %tuple.104), condition=%wide.while_cond, body=%wide.while_body.sunk | while | flops 2 | bytes 163949 | solution.py:172
  1404.5 7.6 gather_fusion
  1440.0 32.3 %while.23 = (s32[]{:T(128)}, bf16[240,288]{1,0:T(8,128)(2,1)S(1)}, s32[16,2]{0,1:T(2,128)S(1)}, bf16[16,160,160]{2,1,0:T(8,128)(2,1)S(1)}, s32[]{:T(128)}) while((s32[]{:T(128)}, bf16[240,288]{1,0:T(8,128)(2,1)S(1)}, s32[16,2]{0,1:T(2,128)S(1)}, bf16[16,160,160]{2,1,0:T(8,128)(2,1)S(1)}, s32[]{:T(128)}) %tuple.104), condition=%wide.while_cond, body=%wide.while_body.sunk | while | flops 2 | bytes 163949 | solution.py:172
  1483.5 7.6 gather_fusion
  1519.0 32.3 %while.23 = (s32[]{:T(128)}, bf16[240,288]{1,0:T(8,128)(2,1)S(1)}, s32[16,2]{0,1:T(2,128)S(1)}, bf16[16,160,160]{2,1,0:T(8,128)(2,1)S(1)}, s32[]{:T(128)}) while((s32[]{:T(128)}, bf16[240,288]{1,0:T(8,128)(2,1)S(1)}, s32[16,2]{0,1:T(2,128)S(1)}, bf16[16,160,160]{2,1,0:T(8,128)(2,1)S(1)}, s32[]{:T(128)}) %tuple.104), condition=%wide.while_cond, body=%wide.while_body.sunk | while | flops 2 | bytes 163949 | solution.py:172
  1562.6 7.6 gather_fusion
  1598.1 32.3 %while.23 = (s32[]{:T(128)}, bf16[240,288]{1,0:T(8,128)(2,1)S(1)}, s32[16,2]{0,1:T(2,128)S(1)}, bf16[16,160,160]{2,1,0:T(8,128)(2,1)S(1)}, s32[]{:T(128)}) while((s32[]{:T(128)}, bf16[240,288]{1,0:T(8,128)(2,1)S(1)}, s32[16,2]{0,1:T(2,128)S(1)}, bf16[16,160,160]{2,1,0:T(8,128)(2,1)S(1)}, s32[]{:T(128)}) %tuple.104), condition=%wide.while_cond, body=%wide.while_body.sunk | while | flops 2 | bytes 163949 | solution.py:172
  1641.7 7.6 gather_fusion
  1677.1 32.3 %while.23 = (s32[]{:T(128)}, bf16[240,288]{1,0:T(8,128)(2,1)S(1)}, s32[16,2]{0,1:T(2,128)S(1)}, bf16[16,160,160]{2,1,0:T(8,128)(2,1)S(1)}, s32[]{:T(128)}) while((s32[]{:T(128)}, bf16[240,288]{1,0:T(8,128)(2,1)S(1)}, s32[16,2]{0,1:T(2,128)S(1)}, bf16[16,160,160]{2,1,0:T(8,128)(2,1)S(1)}, s32[]{:T(128)}) %tuple.104), condition=%wide.while_cond, body=%wide.while_body.sunk | while | flops 2 | bytes 163949 | solution.py:172
  1720.7 7.6 gather_fusion
  1756.2 32.3 %while.23 = (s32[]{:T(128)}, bf16[240,288]{1,0:T(8,128)(2,1)S(1)}, s32[16,2]{0,1:T(2,128)S(1)}, bf16[16,160,160]{2,1,0:T(8,128)(2,1)S(1)}, s32[]{:T(128)}) while((s32[]{:T(128)}, bf16[240,288]{1,0:T(8,128)(2,1)S(1)}, s32[16,2]{0,1:T(2,128)S(1)}, bf16[16,160,160]{2,1,0:T(8,128)(2,1)S(1)}, s32[]{:T(128)}) %tuple.104), condition=%wide.while_cond, body=%wide.while_body.sunk | while | flops 2 | bytes 163949 | solution.py:172
  1799.8 7.6 gather_fusion
  1835.3 32.3 %while.23 = (s32[]{:T(128)}, bf16[240,288]{1,0:T(8,128)(2,1)S(1)}, s32[16,2]{0,1:T(2,128)S(1)}, bf16[16,160,160]{2,1,0:T(8,128)(2,1)S(1)}, s32[]{:T(128)}) while((s32[]{:T(128)}, bf16[240,288]{1,0:T(8,128)(2,1)S(1)}, s32[16,2]{0,1:T(2,128)S(1)}, bf16[16,160,160]{2,1,0:T(8,128)(2,1)S(1)}, s32[]{:T(128)}) %tuple.104), condition=%wide.while_cond, body=%wide.while_body.sunk | while | flops 2 | bytes 163949 | solution.py:172
  1878.8 7.6 gather_fusion
  1914.3 32.3 %while.23 = (s32[]{:T(128)}, bf16[240,288]{1,0:T(8,128)(2,1)S(1)}, s32[16,2]{0,1:T(2,128)S(1)}, bf16[16,160,160]{2,1,0:T(8,128)(2,1)S(1)}, s32[]{:T(128)}) while((s32[]{:T(128)}, bf16[240,288]{1,0:T(8,128)(2,1)S(1)}, s32[16,2]{0,1:T(2,128)S(1)}, bf16[16,160,160]{2,1,0:T(8,128)(2,1)S(1)}, s32[]{:T(128)}) %tuple.104), condition=%wide.while_cond, body=%wide.while_body.sunk | while | flops 2 | bytes 163949 | solution.py:172
  1957.9 7.6 gather_fusion
  1993.4 32.3 %while.23 = (s32[]{:T(128)}, bf16[240,288]{1,0:T(8,128)(2,1)S(1)}, s32[16,2]{0,1:T(2,128)S(1)}, bf16[16,160,160]{2,1,0:T(8,128)(2,1)S(1)}, s32[]{:T(128)}) while((s32[]{:T(128)}, bf16[240,288]{1,0:T(8,128)(2,1)S(1)}, s32[16,2]{0,1:T(2,128)S(1)}, bf16[16,160,160]{2,1,0:T(8,128)(2,1)S(1)}, s32[]{:T(128)}) %tuple.104), condition=%wide.while_cond, body=%wide.while_body.sunk | while | flops 2 | bytes 163949 | solution.py:172
  2072.4 32.3 %while.23 = (s32[]{:T(128)}, bf16[240,288]{1,0:T(8,128)(2,1)S(1)}, s32[16,2]{0,1:T(2,128)S(1)}, bf16[16,160,160]{2,1,0:T(8,128)(2,1)S(1)}, s32[]{:T(128)}) while((s32[]{:T(128)}, bf16[240,288]{1,0:T(8,128)(2,1)S(1)}, s32[16,2]{0,1:T(2,128)S(1)}, bf16[16,160,160]{2,1,0:T(8,128)(2,1)S(1)}, s32[]{:T(128)}) %tuple.104), condition=%wide.while_cond, body=%wide.while_body.sunk | while | flops 2 | bytes 163949 | solution.py:172
  2116.0 7.6 gather_fusion
  2158.7 31.9 %collective-permute-start.7 = (f32[2,12,1]{2,1,0:T(8,128)S(1)}, f32[2,12,1]{2,1,0:T(8,128)S(1)}, u32[]{:S(2)}, u32[]{:S(2)}) collective-permute-start(f32[2,12,1]{2,1,0:T(8,128)S(1)} %get-tuple-element.269), channel_id=1, source_target_pairs={{0,1},{1,2},{2,3},{3,4},{4,5},{5,6},{6,7},{8,9},{9,10},{10,11},{11... | collective-permute-start | bytes 296 | tf_op jit(solution)/shard_map/ppermute | solution.py:24
  (1823 shorter events, 1655.2 us)
Async XLA Ops:
  4.3 14.5 all-to-all-start
  898.1 460.9 %all-to-all-start.1 = ((bf16[32,8,160,160]{3,2,1,0:T(8,128)(2,1)}), bf16[32,8,160,160]{3,2,1,0:T(8,128)(2,1)}, u32[]{:S(2)}, u32[]{:S(2)}) async-start(bf16[32,8,160,160]{3,2,1,0:T(8,128)(2,1)} %bitcast.131), calls=%async_computation.1 | async-start | bytes 41943040 | tf_op jit(solution)/shard_map/all_to_all | solution.py:154
  902.2 4.6 collective-permute-start
  904.1 4.2 collective-permute-start.1
  908.5 160.3 %collective-permute-start.2 = (bf16[240,80]{1,0:T(8,128)(2,1)S(1)}, bf16[240,80]{1,0:T(8,128)(2,1)S(1)}, u32[]{:S(2)}, u32[]{:S(2)}) collective-permute-start(bf16[240,80]{1,0:T(8,128)(2,1)S(1)} %get-tuple-element.262), channel_id=1, source_target_pairs={{0,1},{1,2},{2,3},{3,4},{4,5},{5,6},{6,7},{8,9},{9,10},{10,11},{11... | collective-permute-start | bytes 115208 | tf_op jit(solution)/shard_map/ppermute | solution.py:24
  911.9 156.9 %collective-permute-start.3 = (bf16[240,80]{1,0:T(8,128)(2,1)S(1)}, bf16[240,80]{1,0:T(8,128)(2,1)S(1)}, u32[]{:S(2)}, u32[]{:S(2)}) collective-permute-start(bf16[240,80]{1,0:T(8,128)(2,1)S(1)} %get-tuple-element.263), channel_id=1, source_target_pairs={{1,0},{2,1},{3,2},{4,3},{5,4},{6,5},{7,6},{9,8},{10,9},{11,10},{12... | collective-permute-start | bytes 115208 | tf_op jit(solution)/shard_map/ppermute | solution.py:27
  1394.5 19.8 copy-start.3
  1473.6 19.7 copy-start.3
  1552.7 19.7 copy-start.3
  1631.7 19.7 copy-start.3
  1710.8 19.7 copy-start.3
  1789.9 19.7 copy-start.3
  1868.9 19.7 copy-start.3
  1948.0 19.7 copy-start.3
  2027.0 19.7 copy-start.3
  2106.1 19.7 copy-start.3
  2151.5 4.3 collective-permute-start.4
  2152.8 3.8 collective-permute-start.5
  2157.4 33.2 %collective-permute-start.6 = (f32[2,12,1]{2,1,0:T(8,128)S(1)}, f32[2,12,1]{2,1,0:T(8,128)S(1)}, u32[]{:S(2)}, u32[]{:S(2)}) collective-permute-start(f32[2,12,1]{2,1,0:T(8,128)S(1)} %get-tuple-element.268), channel_id=1, source_target_pairs={{1,0},{2,1},{3,2},{4,3},{5,4},{6,5},{7,6},{9,8},{10,9},{11,10},{12... | collective-permute-start | bytes 296 | tf_op jit(solution)/shard_map/ppermute | solution.py:27
  2158.7 33.3 %collective-permute-start.7 = (f32[2,12,1]{2,1,0:T(8,128)S(1)}, f32[2,12,1]{2,1,0:T(8,128)S(1)}, u32[]{:S(2)}, u32[]{:S(2)}) collective-permute-start(f32[2,12,1]{2,1,0:T(8,128)S(1)} %get-tuple-element.269), channel_id=1, source_target_pairs={{0,1},{1,2},{2,3},{3,4},{4,5},{5,6},{6,7},{8,9},{9,10},{10,11},{11... | collective-permute-start | bytes 296 | tf_op jit(solution)/shard_map/ppermute | solution.py:24
  2193.0 4.6 collective-permute-start.8
  2194.3 4.1 collective-permute-start.9
  2198.5 6.5 collective-permute-start.10
  2199.8 6.6 collective-permute-start.11
  (73 other events, 197.1 us)
where the time goes:
time: 2230 us; the launch traced here: 2210 us
  local copies, waits for them, and re-layouts  1400 us (63%)
  waiting for transfers between devices  459 us (21%)
  matrix products  142 us (6%)
  other arithmetic  133 us (6%)
  starting transfers between devices  67.9 us (3%)
    gather x1248, local copies, waits for them, and re-layouts  1200 us
    all_to_all x1, waiting for transfers between devices, per_device(): lax.all_to_all(pieces.reshape(devices, capacity, PATCH, PATCH), ('row', '...  290 us
    ppermute x6, waiting for transfers between devices, padded(): lax.ppermute(lax.slice_in_dim(block, block.shape[dim] - width, None, axis...  160 us
    gather x10, local copies, waits for them, and re-layouts, per_block(): second = jnp.take(returned, slot_block, axis=0)  75.9 us
    convert_element_type x20, local copies, waits for them, and re-layouts, spectrum(): halves.astype(jnp.bfloat16).reshape(shift_magnitude, extent, 2 * extent)  72 us
    dot_general x10, matrix products, correlate(): jnp.dot(inverse_half.reshape(shift_magnitude * extent, 2 * extent), back_...  57.5 us
    ppermute x6, starting transfers between devices, padded(): lax.ppermute(lax.slice_in_dim(block, block.shape[dim] - width, None, axis...  48.7 us
  transfers between devices with their start and end apart: 14, of which 8 were waited for; matrix products, arithmetic and copies ran while one was open for 0% of the time, Pallas kernels for 0%

commit v1 on v0

v1 whole, which is shorter than its diff:
```python
import functools
import math

import jax
import jax.numpy as jnp
import numpy as np
from jax import lax
from jax.experimental import pallas as pl
from jax.experimental.pallas import tpu as pltpu
from jax.sharding import PartitionSpec as P

PATCH = 160
STRIDE = 8
RELAX = 2
WIDE = 256
HALF_LANES = 128
FREQS = PATCH // 2 + 1
GROUPS = 11
PAIRED = 16 * GROUPS
BIG = 3.0e38

sharpness = 80.0
epsilon = 1e-06
stiffness = 0.24
centre_reach = 2


def dft_tables():
    steps = np.arange(PATCH)
    angles = 2.0 * math.pi * ((steps[:, None] * steps[None, :FREQS]) % PATCH) / PATCH
    return (
        np.cos(angles).astype(jnp.bfloat16).astype(np.float32),
        np.sin(angles).astype(jnp.bfloat16).astype(np.float32),
    )


def kernel_tables():
    cosine, sine = dft_tables()
    weights = np.full((FREQS,), 2.0, np.float32)
    weights[0] = weights[-1] = 1.0
    across = np.zeros((WIDE, WIDE), np.float32)
    across[:PATCH, :FREQS] = cosine
    across[:PATCH, HALF_LANES : HALF_LANES + FREQS] = sine
    back_across = np.zeros((WIDE, WIDE), np.float32)
    back_across[:FREQS, :PATCH] = 0.5 * (cosine * weights).T
    back_across[HALF_LANES : HALF_LANES + FREQS, :PATCH] = 0.5 * (sine * weights).T
    down = np.zeros((PAIRED, PATCH), np.float32)
    back_down = np.zeros((PATCH, PAIRED), np.float32)
    for freq in range(FREQS):
        row = 16 * (freq // 8) + freq % 8
        down[row] = cosine[:, freq]
        down[row + 8] = sine[:, freq]
        back_down[:, row] = cosine[:, freq] * weights[freq]
        back_down[:, row + 8] = sine[:, freq] * weights[freq]
    caps = np.full((2 * PATCH, HALF_LANES), BIG, np.float32)
    for row in range(2 * PATCH):
        if row % PATCH <= 2 * centre_reach:
            caps[row] = -BIG
    return (
        jnp.asarray(across, jnp.bfloat16),
        jnp.asarray(down, jnp.bfloat16),
        jnp.asarray(back_down, jnp.bfloat16),
        jnp.asarray(back_across, jnp.bfloat16),
        jnp.asarray(caps, jnp.float32),
    )


B_BLOCK, B_ROW, B_ROW_REST, B_COL_REST = 0, 1, 2, 3
A_BLOCK, A_ROW, A_ROW_REST, A_COL_REST = 4, 5, 6, 7
NEAR_ROW, NEAR_COL = 8, 9
FIELDS = 10
STAGES = 6


def correlate_kernel(
    capacity,
    count_ref,
    items_ref,
    a_ref,
    b_ref,
    across_ref,
    down_ref,
    back_down_ref,
    back_across_ref,
    caps_ref,
    out_ref,
    *scratch,
):
    patches, halves, crosses, inverses, corrs, maxima = (
        scratch[0:2],
        scratch[2:4],
        scratch[4:6],
        scratch[6:8],
        scratch[8:12],
        scratch[12:14],
    )
    energies, scales, totals, row_moments, col_moments, runners = scratch[14:20]
    count = count_ref[0]

    def at(step, stage):
        return jnp.clip(step - stage, 0, capacity - 1)

    def extract(source, block, row, row_rest, col_rest, target, base):
        lanes = lax.broadcasted_iota(jnp.int32, (PATCH, WIDE), 1)
        low = source[block, pl.ds(row, PATCH), :]
        high = source[block + 1, pl.ds(row, PATCH), :]
        body = jnp.where(lanes >= col_rest, low, high)
        low = source[block, pl.ds(row + PATCH, 16), :]
        high = source[block + 1, pl.ds(row + PATCH, 16), :]
        tail = jnp.where(lanes[:16] >= col_rest, low, high)
        rows = lax.broadcasted_iota(jnp.int32, (16, WIDE), 0)
        head = jnp.where(rows >= row_rest, body[:16], tail)
        target[base : base + 16, :] = head
        target[base + 16 : base + PATCH, :] = body[16:]
        head = head.astype(jnp.float32)
        body = body[16:].astype(jnp.float32)
        total = jnp.sum((head * head).reshape(2, 8, WIDE), axis=0) + jnp.sum(
            (body * body).reshape(PATCH // 8 - 2, 8, WIDE), axis=0
        )
        return total[:, :HALF_LANES] + total[:, HALF_LANES:]

    def stage_patch(step, now):
        item = at(step, 0)
        slot = item % 8
        for which, source, base, fields in (
            (0, a_ref, 0, (A_BLOCK, A_ROW, A_ROW_REST, A_COL_REST)),
            (1, b_ref, PATCH, (B_BLOCK, B_ROW, B_ROW_REST, B_COL_REST)),
        ):
            block, row, row_rest, col_rest = (items_ref[field, item] for field in fields)
            energies[slot, which] = extract(
                source, block, pl.multiple_of(row, 16), row_rest, col_rest, patches[now], base
            )

    def stage_half(step, was, now):
        item = at(step, 1)
        slot = item % 8
        half = jnp.dot(patches[was][...], across_ref[...], preferred_element_type=jnp.float32)
        halves[now][...] = half.astype(jnp.bfloat16)
        mean_a = jnp.sum(energies[slot, 0], keepdims=True) * (1.0 / (PATCH * PATCH))
        mean_b = jnp.sum(energies[slot, 1], keepdims=True) * (1.0 / (PATCH * PATCH))
        scale = 1.0 / (
            float(PATCH**4) * jnp.sqrt(mean_a + epsilon) * jnp.sqrt(mean_b + epsilon)
        )
        scales[slot] = jnp.broadcast_to(scale, (8, HALF_LANES))

    def stage_cross(step, was, now):
        down = down_ref[...]
        spec_a = jnp.dot(down, halves[was][:PATCH, :], preferred_element_type=jnp.float32)
        spec_b = jnp.dot(down, halves[was][PATCH:, :], preferred_element_type=jnp.float32)

        def sides(spec, group):
            cc = spec[16 * group : 16 * group + 8, :HALF_LANES]
            cs = spec[16 * group : 16 * group + 8, HALF_LANES:]
            sc = spec[16 * group + 8 : 16 * group + 16, :HALF_LANES]
            ss = spec[16 * group + 8 : 16 * group + 16, HALF_LANES:]
            return cc - ss, sc + cs, cc + ss, sc - cs

        for group in range(GROUPS):
            a_pr, a_pi, a_mr, a_mi = sides(spec_a, group)
            b_pr, b_pi, b_mr, b_mi = sides(spec_b, group)
            pr = a_pr * b_pr + a_pi * b_pi
            pi = a_pr * b_pi - a_pi * b_pr
            mr = a_mr * b_mr + a_mi * b_mi
            mi = a_mr * b_mi - a_mi * b_mr
            upper = jnp.concatenate([pr + mr, pi - mi], axis=1)
            lower = jnp.concatenate([pi + mi, mr - pr], axis=1)
            crosses[now][16 * group : 16 * group + 16, :] = jnp.concatenate(
                [upper, lower], axis=0
            ).astype(jnp.bfloat16)

    def stage_inverse(step, was, now):
        inverse = jnp.dot(
            back_down_ref[...], crosses[was][...], preferred_element_type=jnp.float32
        )
        inverses[now][...] = inverse.astype(jnp.bfloat16)

    def stage_correlation(step, was, now):
        item = at(step, 4)
        corr = jnp.dot(
            inverses[was][...], back_across_ref[...], preferred_element_type=jnp.float32
        )
        for part in range(2):
            side = corr[:, part * HALF_LANES : (part + 1) * HALF_LANES]
            corrs[2 * now + part][:PATCH, :] = side
            corrs[2 * now + part][PATCH:, :] = side[:8]
        caps = caps_ref[pl.ds(PATCH - items_ref[NEAR_ROW, item], PATCH), :]
        left = jnp.max(
            jnp.minimum(corr[:, :HALF_LANES], caps).reshape(PATCH // 8, 8, HALF_LANES), axis=0
        )
        right = jnp.max(
            jnp.minimum(corr[:, HALF_LANES:], caps).reshape(PATCH // 8, 8, HALF_LANES), axis=0
        )
        lanes = lax.broadcasted_iota(jnp.int32, (8, HALF_LANES), 1)
        maxima[now][...] = jnp.maximum(
            left, jnp.where(lanes < PATCH - HALF_LANES, right, -BIG)
        )

    def stage_near(step, was):
        item = at(step, 5)
        scale = scales[item % 8]
        near_row = items_ref[NEAR_ROW, item]
        near_col = items_ref[NEAR_COL, item]
        rows = lax.broadcasted_iota(jnp.int32, (8, HALF_LANES), 0)
        lanes = lax.broadcasted_iota(jnp.int32, (8, HALF_LANES), 1)
        shift_rows = (rows - centre_reach).astype(jnp.float32)
        row_near = rows <= 2 * centre_reach
        total, row_moment, col_moment = 0.0, 0.0, 0.0
        best = maxima[was][...]
        for part in range(2):
            values = corrs[2 * was + part][pl.ds(near_row, 8), :]
            place = lanes + part * HALF_LANES
            shift = place - near_col
            shift = jnp.where(shift >= PATCH // 2, shift - PATCH, shift)
            shift = jnp.where(shift < -(PATCH // 2), shift + PATCH, shift)
            inside = row_near & (place < PATCH)
            close = jnp.abs(shift) <= centre_reach
            weight = jnp.where(
                inside & close, jnp.exp(sharpness * (values * scale)), 0.0
            )
            total = total + weight
            row_moment = row_moment + weight * shift_rows
            col_moment = col_moment + weight * shift.astype(jnp.float32)
            best = jnp.maximum(
                best, jnp.where(inside & jnp.logical_not(close), values, -BIG)
            )
        totals[pl.ds(item, 1), :] = jnp.sum(total, axis=0, keepdims=True)
        row_moments[pl.ds(item, 1), :] = jnp.sum(row_moment, axis=0, keepdims=True)
        col_moments[pl.ds(item, 1), :] = jnp.sum(col_moment, axis=0, keepdims=True)
        runners[pl.ds(item, 1), :] = jnp.max(best * scale, axis=0, keepdims=True)

    @pl.loop(0, (count + STAGES) // 2)
    def _(pair):
        for now in range(2):
            step = 2 * pair + now
            stage_near(step, 1 - now)
            stage_correlation(step, 1 - now, now)
            stage_inverse(step, 1 - now, now)
            stage_cross(step, 1 - now, now)
            stage_half(step, 1 - now, now)
            stage_patch(step, now)

    lanes = lax.broadcasted_iota(jnp.int32, (capacity, HALF_LANES), 1)
    used = lax.broadcasted_iota(jnp.int32, (capacity, HALF_LANES), 0) < count
    total = jnp.sum(totals[...], axis=1, keepdims=True)
    rows = jnp.sum(row_moments[...], axis=1, keepdims=True) / total
    cols = jnp.sum(col_moments[...], axis=1, keepdims=True) / total
    best = jnp.maximum(jnp.max(runners[...], axis=1, keepdims=True), -2.0)
    result = jnp.where(lanes == 0, rows, jnp.where(lanes == 1, cols, best))
    out_ref[...] = jnp.where(used & (lanes < 3), result, 0.0)


def correlate(count, items, a_blocks, b_blocks):
    capacity = items.shape[1]
    pair = lambda rows, dtype: [pltpu.VMEM((rows, WIDE), dtype)] * 2
    vmem = pl.BlockSpec(memory_space=pltpu.VMEM)
    smem = pl.BlockSpec(memory_space=pltpu.SMEM)
    rows = pltpu.VMEM((capacity, HALF_LANES), jnp.float32)
    return pl.pallas_call(
        functools.partial(correlate_kernel, capacity),
        out_shape=jax.ShapeDtypeStruct((capacity, HALF_LANES), jnp.float32),
        in_specs=[smem, smem] + [vmem] * 7,
        out_specs=vmem,
        scratch_shapes=pair(2 * PATCH, jnp.bfloat16)
        + pair(2 * PATCH, jnp.bfloat16)
        + pair(PAIRED, jnp.bfloat16)
        + pair(PATCH, jnp.bfloat16)
        + [pltpu.VMEM((PATCH + 8, HALF_LANES), jnp.float32)] * 4
        + [pltpu.VMEM((8, HALF_LANES), jnp.float32)] * 2
        + [
            pltpu.VMEM((8, 2, 8, HALF_LANES), jnp.float32),
            pltpu.VMEM((8, 8, HALF_LANES), jnp.float32),
        ]
        + [rows] * 4,
        compiler_params=pltpu.CompilerParams(vmem_limit_bytes=40 * 1024 * 1024),
    )(count, items, a_blocks, b_blocks, *kernel_tables())


def column_blocks(image, front, rows, blocks):
    height, breadth = image.shape
    top = rows[0]
    image = jnp.pad(
        image,
        ((top, rows[1]), (front * PATCH, (blocks - front) * PATCH - breadth)),
    )
    image = image.reshape(height + sum(rows), blocks, PATCH).transpose(1, 0, 2)
    return jnp.pad(image, ((0, 0), (0, 0), (0, WIDE - PATCH)))


def per_device(a_window, b_section, owners, pos_rows, pos_cols, peaks):
    node_rows, node_cols = pos_rows.shape
    nodes = node_rows * node_cols
    n_row, n_col = lax.axis_size("row"), lax.axis_size("col")
    devices = n_row * n_col
    me_row, me_col = lax.axis_index("row"), lax.axis_index("col")
    me = me_row * n_col + me_col
    share = max(2, (nodes * 8 // 5 + devices - 1) // devices)
    capacity = share * devices
    half_patch = PATCH // 2
    tile_rows, tile_cols = b_section.shape
    a_rows, a_cols = a_window.shape

    b_blocks = column_blocks(b_section, 0, (0, 16), -(-tile_cols // PATCH))

    fields = jnp.stack(
        [
            owners.reshape(nodes),
            pos_rows.reshape(nodes) // 16,
            pos_rows.reshape(nodes) % 16,
            pos_cols.reshape(nodes) // 16,
            pos_cols.reshape(nodes) % 16,
            peaks[0].reshape(nodes),
            peaks[1].reshape(nodes),
            jnp.zeros((nodes,), jnp.int32),
        ]
    ).astype(jnp.bfloat16)
    fields = jnp.pad(fields, ((0, 0), (0, WIDE - nodes))).reshape(16, HALF_LANES)
    sent = jnp.concatenate([a_window, fields], axis=0)
    everyone = lax.all_gather(sent, ("row", "col"))

    window = everyone[:, :a_rows].reshape(n_row, n_col, a_rows, a_cols)
    window = window.transpose(0, 2, 1, 3).reshape(n_row * a_rows, n_col * a_cols)
    a_count = (n_col * a_cols + 76) // PATCH + 2
    a_blocks = column_blocks(window, 1, (half_patch, half_patch), a_count)

    known = everyone[:, a_rows:].reshape(devices, 8, WIDE)[:, :, :nodes]
    mine = (known[:, 0] == me.astype(jnp.bfloat16)).astype(jnp.float32)
    within = jnp.dot(
        mine, jnp.triu(jnp.ones((nodes, nodes), jnp.float32), 1)
    )
    loads = jnp.sum(mine, axis=1)
    before = jnp.sum(
        jnp.where(jnp.tril(jnp.ones((devices, devices), bool), -1), loads[None, :], 0.0), axis=1
    )
    count = jnp.sum(loads).astype(jnp.int32).reshape(1)
    slots = jnp.where(mine > 0, before[:, None] + within, -1.0).astype(jnp.int32)
    slots = slots.reshape(devices * nodes)
    chosen = (
        slots[None, :] == jnp.arange(capacity, dtype=jnp.int32)[:, None]
    ).astype(jnp.bfloat16)
    device_of = jnp.broadcast_to(jnp.arange(devices)[:, None], (devices, nodes))
    node_of = jnp.broadcast_to(jnp.arange(nodes)[None, :], (devices, nodes))
    listed = jnp.concatenate(
        [
            known.transpose(1, 0, 2)[:7],
            device_of[None].astype(jnp.bfloat16),
            node_of[None].astype(jnp.bfloat16),
        ],
        axis=0,
    ).reshape(9, devices * nodes)
    taken = lax.dot_general(
        listed, chosen, (((1,), (1,)), ((), ())), preferred_element_type=jnp.float32
    ).astype(jnp.int32)
    valid = jnp.arange(capacity) < count[0]
    b_top = jnp.where(valid, taken[1] * 16 + taken[2] - half_patch, 0)
    b_left = jnp.where(valid, taken[3] * 16 + taken[4] - half_patch, 0)
    a_top = (taken[7] // n_col * node_rows + taken[8] // node_cols) * STRIDE + STRIDE // 2
    a_left = (
        (taken[7] % n_col * node_cols + taken[8] % node_cols) * STRIDE
        + STRIDE // 2
        + half_patch
    )
    near_row = (taken[5] + b_top % 16 - a_top % 16 - centre_reach + 2 * PATCH) % PATCH
    near_col = (taken[6] + b_left % PATCH - a_left % PATCH + 2 * PATCH) % PATCH
    items = jnp.stack(
        [
            b_left // PATCH,
            b_top // 16 * 16,
            b_top % 16,
            b_left % PATCH,
            a_left // PATCH,
            a_top // 16 * 16,
            a_top % 16,
            a_left % PATCH,
            near_row,
            near_col,
        ]
    )
    result = correlate(count, items, a_blocks, b_blocks)[:, :3]

    spread = lax.dot_general(
        result,
        chosen.astype(jnp.float32),
        (((0,), (0,)), ((), ())),
        precision=lax.Precision.HIGHEST,
    )
    spread = lax.psum(spread, ("row", "col"))
    spread = spread.reshape(3, n_row, n_col, node_rows, node_cols)
    runner = lax.dynamic_slice(
        spread, (2, me_row, me_col, 0, 0), (1, 1, 1, node_rows, node_cols)
    ).reshape(node_rows, node_cols)
    offsets = known[:, 5:7].astype(jnp.float32).transpose(1, 0, 2)
    field = spread[:2] + offsets.reshape(2, n_row, n_col, node_rows, node_cols)
    height, breadth = n_row * node_rows, n_col * node_cols
    field = field.transpose(0, 1, 3, 2, 4).reshape(2, height, breadth)
    field = jnp.pad(field, ((0, 0), (RELAX, RELAX), (RELAX, RELAX)))
    field = lax.dynamic_slice(
        field,
        (0, me_row * node_rows, me_col * node_cols),
        (2, node_rows + 2 * RELAX, node_cols + 2 * RELAX),
    )
    for step in range(RELAX):
        reach = RELAX - 1 - step
        centre = field[:, 1:-1, 1:-1]
        around = (
            field[:, 2:, 1:-1] + field[:, :-2, 1:-1] + field[:, 1:-1, 2:] + field[:, 1:-1, :-2]
        )
        field = centre + stiffness * (around - 4.0 * centre)
        rows = me_row * node_rows - reach + jnp.arange(node_rows + 2 * reach)
        cols = me_col * node_cols - reach + jnp.arange(node_cols + 2 * reach)
        inside = ((rows >= 0) & (rows < height))[:, None] & ((cols >= 0) & (cols < breadth))[None]
        field = jnp.where(inside[None], field, 0.0)
    return (field, runner)


def solution(mesh):
    placed = (
        P("row", "col"),
        P("row", "col"),
        P("row", "col", None, None, None),
        P("row", "col"),
        P("row", "col"),
        P(None, "row", "col"),
    )
    return jax.shard_map(
        per_device,
        mesh=mesh,
        in_specs=placed,
        out_specs=(P(None, "row", "col"), P("row", "col")),
        check_vma=False,
    )
```

time: 2230 us -> 222 us (0.10); the launches traced: 2210 us -> 222 us
  local copies, waits for them, and re-layouts: 1400 us -> 26.5 us
  waiting for transfers between devices: 459 us -> 0 us
  blocking collectives: 0 us -> 142 us
  matrix products: 142 us -> 2.77 us
  other arithmetic: 133 us -> 3.62 us
  starting transfers between devices: 67.9 us -> 0 us
  Pallas kernels: 0 us -> 45.3 us
    gather x1258 -> x0, local copies, waits for them, and re-layouts: 1270 us -> none
    all_to_all x2 -> x0, waiting for transfers between devices: 297 us -> none  [the longest x1 290 us: per_device(): lax.all_to_all(pieces.reshape(devices, capacity, PATCH, PATCH), ('row', '...]
    ppermute x12 -> x0, waiting for transfers between devices: 162 us -> none  [the longest x6 160 us: padded(): lax.ppermute(lax.slice_in_dim(block, block.shape[dim] - width, None, axis...]
    dot_general x50 -> x3, matrix products: 142 us -> 2.77 us  [the longest x1 1.71 us: per_device(): lax.dot_general(result, chosen.astype(jnp.float32), (((0,), (0,)), ((), (...]
    all_gather x0 -> x1, blocking collectives: none -> 74.2 us  [per_device(): everyone = lax.all_gather(sent, ('row', 'col'))]
    convert_element_type x20 -> x1, local copies, waits for them, and re-layouts: 72 us -> 0.1 us  [per_device(): node_of[None].astype(jnp.bfloat16)]
    psum x0 -> x1, blocking collectives: none -> 68.1 us  [per_device(): spread = lax.psum(spread, ('row', 'col'))]
    ppermute x12 -> x0, starting transfers between devices: 56.5 us -> none  [the longest x6 48.7 us: padded(): lax.ppermute(lax.slice_in_dim(block, block.shape[dim] - width, None, axis...]
  transfers between devices with their start and end apart: 14 -> 0, of which waited for: 8 -> 0; matrix products, arithmetic and copies ran while one was open for 0% -> 0% of each run, Pallas kernels for 0% -> 0%
where the time goes in v1:
time: 222 us
  blocking collectives  142 us (64%)
  Pallas kernels  45.3 us (20%)
  local copies, waits for them, and re-layouts  26.5 us (12%)
  other arithmetic  3.62 us (2%)
  matrix products  2.77 us (1%)
    all_gather x1, blocking collectives, per_device(): everyone = lax.all_gather(sent, ('row', 'col'))  74.2 us
    psum x1, blocking collectives, per_device(): spread = lax.psum(spread, ('row', 'col'))  68.1 us
    pallas_call x1, Pallas kernels, correlate(): pl.pallas_call(functools.partial(correlate_kernel, capacity), out_shape=j...  45.3 us
    reshape x2, local copies, waits for them, and re-layouts, column_blocks(): image = image.reshape(height + sum(rows), blocks, PATCH).transpose(1, 0, 2)  7.97 us
    unnamed x14, local copies, waits for them, and re-layouts  5.97 us
    pad x2, local copies, waits for them, and re-layouts, column_blocks(): return jnp.pad(image, ((0, 0), (0, 0), (0, WIDE - PATCH)))  4.61 us

profile of v1, /device:TPU:0, one launch (start us, length us, event | category | flops | bytes accessed | tf_op | source)
XLA Modules:
  0.0 222.0 jit_solution(10199676021712798372)
XLA Ops:
  0.6 0.8 reshape.386
  1.4 0.8 reshape.387
  2.2 0.7 convert.33
  3.2 0.7 convert_reduce_fusion.2
  4.1 0.7 pad_maximum_fusion
  4.8 74.2 %all-gather = bf16[3072,128]{1,0:T(8,128)(2,1)S(1)} all-gather(bf16[96,128]{1,0:T(8,128)(2,1)S(1)} %pad_maximum_fusion), channel_id=2, replica_groups=mesh['row'=4,'col'=8] {'row','col'}, dimensions={0}, use_global_device_ids=true | all-gather | bytes 811008 | tf_op jit(solution)/shard_map/all_gather | solution.py:318
  79.1 0.6 convert_reduce_fusion.1
  80.2 0.2 concatenate.10
  80.6 1.0 fusion.6
  82.5 0.7 copy.42
  83.2 0.7 reshape.407
  83.9 0.5 pad.25.clone
  84.3 2.6 %copy.34 = bf16[480,8,160]{2,0,1:T(8,128)(2,1)} copy(bf16[480,8,160]{0,2,1:T(8,128)(2,1)S(1)} %bitcast.30) | data formatting | bytes 2457600 | tf_op jit(solution)/shard_map/reshape | solution.py:285
  86.9 1.9 pad.26.a_ref
  88.8 4.0 %copy.35 = bf16[1024,1024]{0,1:T(8,128)(2,1)} copy(bf16[1024,1024]{1,0:T(8,128)(2,1)} %param.12) | data formatting | bytes 4194304 | tf_op args[1]
  92.8 3.3 %pad.27 = bf16[1040,1120]{0,1:T(8,128)(2,1)} pad(bf16[1024,1024]{0,1:T(8,128)(2,1)} %copy.35, bf16[]{:T(256)} %constant.202.clone.1), padding=0_16x0_96 | pad | bytes 4426754 | tf_op jit(solution)/shard_map/jit(_pad)/pad | solution.py:281
  96.0 5.4 %copy.36 = bf16[1040,7,160]{2,0,1:T(8,128)(2,1)} copy(bf16[1040,7,160]{0,2,1:T(8,128)(2,1)} %bitcast.28) | data formatting | bytes 4659200 | tf_op jit(solution)/shard_map/reshape | solution.py:285
  101.5 2.7 %pad.28.b_ref = bf16[7,1040,256]{2,1,0:T(8,128)(2,1)S(1)} pad(bf16[7,1040,160]{2,1,0:T(8,128)(2,1)} %bitcast.27, bf16[]{:T(256)} %constant.202.clone.1), padding=0_0x0_0x0_96 | pad | bytes 6056962 | tf_op jit(solution)/shard_map/jit(_pad)/pad | solution.py:286
  104.2 45.3 %shard_map.122 = f32[256,128]{1,0:T(8,128)S(1)} custom-call(s32[1]{0:T(128)} %bitcast.2.count_ref, s32[10,256]{1,0:T(8,128)S(1)} %stack.6.items_ref, bf16[8,480,256]{2,1,0:T(8,128)(2,1)S(1)} %pad.26.a_ref, bf16[7,1040,256]{2,1,0:T(8,128)(2,1)S(1)} %pad.28.b_ref, bf16[256,256]{1,0:T(8,128)(2,1)S(1)} %copy-done.1, bf16[176,160]{1,0:T(8,128)(2,1)S(1)} %copy-done.3, ...), custom_call_target="tpu_custom_call" | custom-call | tf_op jit(solution)/shard_map/pallas_call | solution.py:258
  149.5 1.7 fusion
  151.2 68.1 %psum.7 = f32[3,5120]{1,0:T(4,128)S(1)} all-reduce(f32[3,5120]{1,0:T(4,128)S(1)} %fusion), channel_id=1, replica_groups=mesh['row'=4,'col'=8] {'row','col'}, use_global_device_ids=true, to_apply=%region_3.4 | all-reduce | flops 15360 | bytes 122880 | tf_op jit(solution)/shard_map/psum | solution.py:386
  220.6 0.6 copy.39
  221.2 0.2 reshape.398
  221.4 0.6 dynamic-slice_bitcast_fusion
  (57 shorter events, 2.6 us)
Async XLA Ops:
  101.4 2.8 %copy-start = (f32[320,128]{1,0:T(8,128)S(1)}, f32[320,128]{1,0:T(8,128)}, u32[]{:S(2)}) copy-start(f32[320,128]{1,0:T(8,128)} %constant.223.clone.caps_ref) | copy-start | bytes 491524
  101.4 2.8 %copy-start.1 = (bf16[256,256]{1,0:T(8,128)(2,1)S(1)}, bf16[256,256]{1,0:T(8,128)(2,1)}, u32[]{:S(2)}) copy-start(bf16[256,256]{1,0:T(8,128)(2,1)} %constant.219.clone.across_ref) | copy-start | bytes 393220
  101.4 2.8 %copy-start.2 = (bf16[256,256]{1,0:T(8,128)(2,1)S(1)}, bf16[256,256]{1,0:T(8,128)(2,1)}, u32[]{:S(2)}) copy-start(bf16[256,256]{1,0:T(8,128)(2,1)} %constant.222.clone.back_across_ref) | copy-start | bytes 393220
  101.4 2.8 %copy-start.3 = (bf16[176,160]{1,0:T(8,128)(2,1)S(1)}, bf16[176,160]{1,0:T(8,128)(2,1)}, u32[]{:S(2)}) copy-start(bf16[176,160]{1,0:T(8,128)(2,1)} %constant.220.clone.down_ref) | copy-start | bytes 168964
  101.4 2.8 %copy-start.4 = (bf16[160,176]{1,0:T(8,128)(2,1)S(1)}, bf16[160,176]{1,0:T(8,128)(2,1)}, u32[]{:S(2)}) copy-start(bf16[160,176]{1,0:T(8,128)(2,1)} %constant.221.clone.back_down_ref) | copy-start | bytes 168964

commit v2 on v1

--- a/solution.py
+++ b/solution.py
@@ -72,12 +72,21 @@
 STAGES = 6
 
 
+def cut(strip, start):
+    if start >= strip.shape[1]:
+        return jnp.zeros((strip.shape[0], WIDE), strip.dtype)
+    piece = strip[:, start : min(start + PATCH, strip.shape[1])]
+    gap = jnp.zeros((strip.shape[0], WIDE - piece.shape[1]), strip.dtype)
+    return jnp.concatenate([piece, gap], axis=1)
+
+
 def correlate_kernel(
     capacity,
+    grid,
     count_ref,
     items_ref,
-    a_ref,
-    b_ref,
+    everyone_ref,
+    tile_ref,
     across_ref,
     down_ref,
     back_down_ref,
@@ -94,8 +103,33 @@
         scratch[8:12],
         scratch[12:14],
     )
-    energies, scales, totals, row_moments, col_moments, runners = scratch[14:20]
+    energies, scales, totals, row_moments, col_moments, runners, a_ref, b_ref = scratch[14:22]
     count = count_ref[0]
+    n_row, n_col, a_rows = grid
+
+    height = tile_ref.shape[0]
+
+    @pl.loop(0, height // 128)
+    def _(chunk):
+        place = pl.ds(pl.multiple_of(chunk * 128, 128), 128)
+        strip = tile_ref[place, :]
+        for block in range(b_ref.shape[0]):
+            b_ref[block, place, :] = cut(strip, block * PATCH)
+
+    b_ref[:, height:, :] = jnp.zeros((b_ref.shape[0], 16, WIDE), jnp.bfloat16)
+    a_ref[0] = jnp.zeros(a_ref.shape[1:], jnp.bfloat16)
+    rim = jnp.zeros((a_ref.shape[0], PATCH // 2, WIDE), jnp.bfloat16)
+    a_ref[:, : PATCH // 2, :] = rim
+    a_ref[:, a_ref.shape[1] - PATCH // 2 :, :] = rim
+
+    @pl.loop(0, n_row)
+    def _(row):
+        strip = jnp.concatenate(
+            [everyone_ref[row * n_col + col, :a_rows, :] for col in range(n_col)], axis=1
+        )
+        place = pl.ds(pl.multiple_of(PATCH // 2 + row * a_rows, 16), a_rows)
+        for block in range(1, a_ref.shape[0]):
+            a_ref[block, place, :] = cut(strip, (block - 1) * PATCH)
 
     def at(step, stage):
         return jnp.clip(step - stage, 0, capacity - 1)
@@ -249,14 +283,17 @@
     out_ref[...] = jnp.where(used & (lanes < 3), result, 0.0)
 
 
-def correlate(count, items, a_blocks, b_blocks):
+def correlate(count, items, everyone, tile, grid):
     capacity = items.shape[1]
+    n_row, n_col, a_rows = grid
+    a_blocks = (n_col * everyone.shape[2] + 76) // PATCH + 2
+    b_blocks = -(-tile.shape[1] // PATCH)
     pair = lambda rows, dtype: [pltpu.VMEM((rows, WIDE), dtype)] * 2
     vmem = pl.BlockSpec(memory_space=pltpu.VMEM)
     smem = pl.BlockSpec(memory_space=pltpu.SMEM)
     rows = pltpu.VMEM((capacity, HALF_LANES), jnp.float32)
     return pl.pallas_call(
-        functools.partial(correlate_kernel, capacity),
+        functools.partial(correlate_kernel, capacity, grid),
         out_shape=jax.ShapeDtypeStruct((capacity, HALF_LANES), jnp.float32),
         in_specs=[smem, smem] + [vmem] * 7,
         out_specs=vmem,
@@ -270,20 +307,13 @@
             pltpu.VMEM((8, 2, 8, HALF_LANES), jnp.float32),
             pltpu.VMEM((8, 8, HALF_LANES), jnp.float32),
         ]
-        + [rows] * 4,
+        + [rows] * 4
+        + [
+            pltpu.VMEM((a_blocks, n_row * a_rows + PATCH, WIDE), jnp.bfloat16),
+            pltpu.VMEM((b_blocks, tile.shape[0] + 16, WIDE), jnp.bfloat16),
+        ],
         compiler_params=pltpu.CompilerParams(vmem_limit_bytes=40 * 1024 * 1024),
-    )(count, items, a_blocks, b_blocks, *kernel_tables())
-
-
-def column_blocks(image, front, rows, blocks):
-    height, breadth = image.shape
-    top = rows[0]
-    image = jnp.pad(
-        image,
-        ((top, rows[1]), (front * PATCH, (blocks - front) * PATCH - breadth)),
-    )
-    image = image.reshape(height + sum(rows), blocks, PATCH).transpose(1, 0, 2)
-    return jnp.pad(image, ((0, 0), (0, 0), (0, WIDE - PATCH)))
+    )(count, items, everyone, tile, *kernel_tables())
 
 
 def per_device(a_window, b_section, owners, pos_rows, pos_cols, peaks):
@@ -296,10 +326,7 @@
     share = max(2, (nodes * 8 // 5 + devices - 1) // devices)
     capacity = share * devices
     half_patch = PATCH // 2
-    tile_rows, tile_cols = b_section.shape
     a_rows, a_cols = a_window.shape
-
-    b_blocks = column_blocks(b_section, 0, (0, 16), -(-tile_cols // PATCH))
 
     fields = jnp.stack(
         [
@@ -315,12 +342,8 @@
     ).astype(jnp.bfloat16)
     fields = jnp.pad(fields, ((0, 0), (0, WIDE - nodes))).reshape(16, HALF_LANES)
     sent = jnp.concatenate([a_window, fields], axis=0)
-    everyone = lax.all_gather(sent, ("row", "col"))
-
-    window = everyone[:, :a_rows].reshape(n_row, n_col, a_rows, a_cols)
-    window = window.transpose(0, 2, 1, 3).reshape(n_row * a_rows, n_col * a_cols)
-    a_count = (n_col * a_cols + 76) // PATCH + 2
-    a_blocks = column_blocks(window, 1, (half_patch, half_patch), a_count)
+    everyone = lax.all_gather(lax.all_gather(sent, "col"), "row")
+    everyone = everyone.reshape(devices, a_rows + 16, a_cols)
 
     known = everyone[:, a_rows:].reshape(devices, 8, WIDE)[:, :, :nodes]
     mine = (known[:, 0] == me.astype(jnp.bfloat16)).astype(jnp.float32)
@@ -375,28 +398,37 @@
             near_col,
         ]
     )
-    result = correlate(count, items, a_blocks, b_blocks)[:, :3]
-
+    result = correlate(count, items, everyone, b_section, (n_row, n_col, a_rows))[:, :3]
+
+    height, breadth = n_row * node_rows, n_col * node_cols
+    tall, broad = node_rows + 2 * RELAX, node_cols + 2 * RELAX
+    lanes = -(-tall * broad // HALF_LANES) * HALF_LANES
+    shape = (devices, lanes)
+    device = lax.broadcasted_iota(jnp.int32, shape, 0)
+    place = lax.broadcasted_iota(jnp.int32, shape, 1)
+    row = device // n_col * node_rows + place // broad - RELAX
+    col = device % n_col * node_cols + place % broad - RELAX
+    real = (row >= 0) & (row < height) & (col >= 0) & (col < breadth) & (place < tall * broad)
+    wanted = jnp.where(real, row * breadth + col, -1).reshape(devices * lanes)
+    node = (taken[7] // n_col * node_rows + taken[8] // node_cols) * breadth + (
+        taken[7] % n_col * node_cols + taken[8] % node_cols
+    )
+    node = jnp.where(valid, node, -2)
     spread = lax.dot_general(
         result,
-        chosen.astype(jnp.float32),
+        (node[:, None] == wanted[None, :]).astype(jnp.float32),
         (((0,), (0,)), ((), ())),
         precision=lax.Precision.HIGHEST,
     )
-    spread = lax.psum(spread, ("row", "col"))
-    spread = spread.reshape(3, n_row, n_col, node_rows, node_cols)
-    runner = lax.dynamic_slice(
-        spread, (2, me_row, me_col, 0, 0), (1, 1, 1, node_rows, node_cols)
-    ).reshape(node_rows, node_cols)
-    offsets = known[:, 5:7].astype(jnp.float32).transpose(1, 0, 2)
-    field = spread[:2] + offsets.reshape(2, n_row, n_col, node_rows, node_cols)
-    height, breadth = n_row * node_rows, n_col * node_cols
-    field = field.transpose(0, 1, 3, 2, 4).reshape(2, height, breadth)
-    field = jnp.pad(field, ((0, 0), (RELAX, RELAX), (RELAX, RELAX)))
-    field = lax.dynamic_slice(
-        field,
-        (0, me_row * node_rows, me_col * node_cols),
-        (2, node_rows + 2 * RELAX, node_cols + 2 * RELAX),
+    spread = spread.reshape(3, devices, lanes).transpose(1, 0, 2)
+    spread = lax.all_to_all(spread, ("row", "col"), split_axis=0, concat_axis=0, tiled=True)
+    spread = jnp.sum(spread, axis=0)[:, : tall * broad].reshape(3, tall, broad)
+    runner = spread[2, RELAX:-RELAX, RELAX:-RELAX]
+    offsets = known[:, 5:7].astype(jnp.float32).reshape(n_row, n_col, 2, node_rows, node_cols)
+    offsets = offsets.transpose(2, 0, 3, 1, 4).reshape(2, height, breadth)
+    offsets = jnp.pad(offsets, ((0, 0), (RELAX, RELAX), (RELAX, RELAX)))
+    field = spread[:2] + lax.dynamic_slice(
+        offsets, (0, me_row * node_rows, me_col * node_cols), (2, tall, broad)
     )
     for step in range(RELAX):
         reach = RELAX - 1 - step

time: 222 us -> 167 us (0.75)
  blocking collectives: 142 us -> 41 us
  starting transfers between devices: 0 us -> 50.2 us
  Pallas kernels: 45.3 us -> 31.8 us
  other arithmetic: 3.62 us -> 13.8 us
  local copies, waits for them, and re-layouts: 26.5 us -> 16.6 us
  waiting for transfers between devices: 0 us -> 6.95 us
  matrix products: 2.77 us -> 6.26 us
    psum x1 -> x0, blocking collectives: 68.1 us -> none  [per_device(): spread = lax.psum(spread, ('row', 'col'))]
    all_to_all x0 -> x1, starting transfers between devices: none -> 50.2 us  [per_device(): lax.all_to_all(spread, ('row', 'col'), split_axis=0, concat_axis=0, tiled...]
    all_gather x1 -> x2, blocking collectives: 74.2 us -> 41 us  [per_device(): everyone = lax.all_gather(lax.all_gather(sent, 'col'), 'row')]
    pallas_call x1, Pallas kernels: 45.3 us -> 31.8 us  [correlate(): pl.pallas_call(functools.partial(correlate_kernel, capacity, grid), out_s...]
    reshape x7 -> x3, local copies, waits for them, and re-layouts: 9.15 us -> 0.45 us  [the longest x1 0.22 us: per_device(): known[:, 5:7].astype(jnp.float32)]
    pad x4 -> x0, local copies, waits for them, and re-layouts: 8.33 us -> none  [the longest x2 4.61 us: column_blocks(): return jnp.pad(image, ((0, 0), (0, 0), (0, WIDE - PATCH)))]
    all_to_all x0 -> x1, waiting for transfers between devices: none -> 6.95 us  [per_device(): lax.all_to_all(spread, ('row', 'col'), split_axis=0, concat_axis=0, tiled...]
    unnamed x14 -> x17, local copies, waits for them, and re-layouts: 5.97 us -> 0.64 us
  transfers between devices with their start and end apart: 0 -> 1, of which waited for: 0 -> 1; matrix products, arithmetic and copies ran while one was open for 0% -> 1% of each run, Pallas kernels for 0% -> 0%
where the time goes in v2:
time: 167 us; the launch traced here: 168 us
  starting transfers between devices  50.2 us (30%)
  blocking collectives  41 us (25%)
  Pallas kernels  31.8 us (19%)
  local copies, waits for them, and re-layouts  16.6 us (10%)
  other arithmetic  13.8 us (8%)
  waiting for transfers between devices  6.95 us (4%)
  matrix products  6.26 us (4%)
    all_to_all x1, starting transfers between devices, per_device(): lax.all_to_all(spread, ('row', 'col'), split_axis=0, concat_axis=0, tiled...  50.2 us
    all_gather x2, blocking collectives, per_device(): everyone = lax.all_gather(lax.all_gather(sent, 'col'), 'row')  41 us
    pallas_call x1, Pallas kernels, correlate(): pl.pallas_call(functools.partial(correlate_kernel, capacity, grid), out_s...  31.8 us
    all_to_all x1, waiting for transfers between devices, per_device(): lax.all_to_all(spread, ('row', 'col'), split_axis=0, concat_axis=0, tiled...  6.95 us
    dot_general x1, matrix products, per_device(): lax.dot_general(result, (node[:, None] == wanted[None, :]).astype(jnp.flo...  4.3 us
  transfers between devices with their start and end apart: 1, of which 1 were waited for; matrix products, arithmetic and copies ran while one was open for 1% of the time, Pallas kernels for 0%

profile of v2, /device:TPU:0, one launch (start us, length us, event | category | flops | bytes accessed | tf_op | source)
XLA Modules:
  0.0 168.2 jit_solution(12071617002374748045)
XLA Ops:
  0.6 0.8 reshape.628
  1.4 0.8 reshape.629
  2.3 0.7 convert.36
  3.2 0.7 convert_reduce_fusion.2
  4.1 0.7 pad_maximum_fusion
  4.8 32.4 %all-gather = bf16[768,128]{1,0:T(8,128)(2,1)S(1)} all-gather(bf16[96,128]{1,0:T(8,128)(2,1)S(1)} %pad_maximum_fusion), channel_id=2, replica_groups=mesh['row'=4,'col'=8] {'col'}, dimensions={0}, use_global_device_ids=true | all-gather | bytes 221184 | tf_op jit(solution)/shard_map/all_gather | solution.py:345
  37.2 8.6 %all-gather.1.everyone_ref = bf16[32,96,128]{2,1,0:T(8,128)(2,1)S(1)} all-gather(bf16[8,96,128]{2,1,0:T(8,128)(2,1)S(1)} %bitcast.24), channel_id=3, replica_groups=mesh['row'=4,'col'=8] {'row'}, dimensions={0}, use_global_device_ids=true | all-gather | bytes 983040 | tf_op jit(solution)/shard_map/all_gather | solution.py:345
  46.5 1.8 %reshape.632 = bf16[32,8,256]{2,1,0:T(8,128)(2,1)} reshape(bf16[32,16,128]{2,1,0:T(8,128)(2,1)} %slice.133) | data formatting | bytes 262144 | tf_op jit(solution)/shard_map/reshape | solution.py:348
  48.3 0.9 slice.134
  49.2 1.6 slice_bitcast_fusion
  56.3 1.6 copy.30
  57.8 1.7 %concatenate.10 = bf16[7,5120]{1,0:T(8,128)(2,1)} reshape(bf16[7,32,160]{2,1,0:T(8,128)(2,1)} %copy.30) | data formatting | bytes 143360 | tf_op jit(solution)/shard_map/concatenate | solution.py:365
  60.2 0.7 broadcast_in_dim_broadcast_in_dim.13
  61.6 1.9 %fusion.8 = s32[9,256]{1,0:T(8,128)S(1)} fusion(s32[5120]{0:T(1024)S(1)} %eq.61, bf16[1,5120]{1,0:T(2,128)(2,1)S(1)} %convert_element_type.52, bf16[1,5120]{1,0:T(2,128)(2,1)} %broadcast_in_dim_broadcast_in_dim.13, bf16[7,5120]{1,0:T(8,128)(2,1)} %concatenate.10), kind=kOutput, calls=%fused_computation.10 | convolution fusion | flops 25182464 | bytes 121856 | tf_op jit(solution)/shard_map/dot_general | solution.py:373
  65.3 0.9 add_select_fusion
  66.7 0.7 fusion.56
  67.4 1.2 fusion.55
  68.7 1.3 compare_select_fusion.20
  69.9 1.4 stack.6.items_ref
  71.4 31.8 %shard_map.122 = f32[256,128]{1,0:T(8,128)S(1)} custom-call(s32[1]{0:T(128)} %bitcast.2.count_ref, s32[10,256]{1,0:T(8,128)S(1)} %stack.6.items_ref, bf16[32,96,128]{2,1,0:T(8,128)(2,1)S(1)} %all-gather.1.everyone_ref, bf16[1024,1024]{1,0:T(8,128)(2,1)S(1)} %copy-done, bf16[256,256]{1,0:T(8,128)(2,1)S(1)} %copy-done.2, bf16[176,160]{1,0:T(8,128)(2,1)S(1)} %copy-done.4, ...), custom_call_target="tpu_custom_call" | custom-call | tf_op jit(solution)/shard_map/pallas_call | solution.py:295
  103.3 4.3 %fusion = f32[3,12288]{1,0:T(4,128)} fusion(s32[12288]{0:T(1024)S(1)} %copy-done.6, s32[256]{0:T(256)S(1)} %copy-done.7, f32[256,128]{1,0:T(8,128)S(1)} %shard_map.122), kind=kOutput, calls=%fused_computation | convolution fusion | flops 116391936 | bytes 328704 | tf_op jit(solution)/shard_map/dot_general | solution.py:417
  107.6 50.2 %all-to-all-start = ((f32[32,3,384]{2,1,0:T(4,128)}), f32[32,3,384]{2,1,0:T(4,128)S(1)}, u32[]{:S(2)}, u32[]{:S(2)}) async-start(f32[32,3,384]{2,1,0:T(4,128)} %bitcast.7), calls=%async_computation | async-start | bytes 393216 | tf_op jit(solution)/shard_map/all_to_all | solution.py:424
  157.8 0.9 slice.147
  159.4 6.9 %all-to-all-done = f32[32,3,384]{2,1,0:T(4,128)S(1)} async-done(((f32[32,3,384]{2,1,0:T(4,128)}), f32[32,3,384]{2,1,0:T(4,128)S(1)}, u32[]{:S(2)}, u32[]{:S(2)}) %all-to-all-start) | async-done | bytes 147488 | tf_op jit(solution)/shard_map/all_to_all | solution.py:424
  (67 shorter events, 12.1 us)
Async XLA Ops:
  45.8 25.6 %copy-start = (bf16[1024,1024]{1,0:T(8,128)(2,1)S(1)}, bf16[1024,1024]{1,0:T(8,128)(2,1)}, u32[]{:S(2)}) copy-start(bf16[1024,1024]{1,0:T(8,128)(2,1)} %tile_ref.1) | copy-start | bytes 6291460
  45.8 25.6 %copy-start.1 = (f32[320,128]{1,0:T(8,128)S(1)}, f32[320,128]{1,0:T(8,128)}, u32[]{:S(2)}) copy-start(f32[320,128]{1,0:T(8,128)} %constant.283.clone.caps_ref) | copy-start | bytes 491524
  45.8 25.6 %copy-start.2 = (bf16[256,256]{1,0:T(8,128)(2,1)S(1)}, bf16[256,256]{1,0:T(8,128)(2,1)}, u32[]{:S(2)}) copy-start(bf16[256,256]{1,0:T(8,128)(2,1)} %constant.279.clone.across_ref) | copy-start | bytes 393220
  45.8 25.6 %copy-start.3 = (bf16[256,256]{1,0:T(8,128)(2,1)S(1)}, bf16[256,256]{1,0:T(8,128)(2,1)}, u32[]{:S(2)}) copy-start(bf16[256,256]{1,0:T(8,128)(2,1)} %constant.282.clone.back_across_ref) | copy-start | bytes 393220
  45.8 25.6 %copy-start.4 = (bf16[176,160]{1,0:T(8,128)(2,1)S(1)}, bf16[176,160]{1,0:T(8,128)(2,1)}, u32[]{:S(2)}) copy-start(bf16[176,160]{1,0:T(8,128)(2,1)} %constant.280.clone.down_ref) | copy-start | bytes 168964
  45.8 25.6 %copy-start.5 = (bf16[160,176]{1,0:T(8,128)(2,1)S(1)}, bf16[160,176]{1,0:T(8,128)(2,1)}, u32[]{:S(2)}) copy-start(bf16[160,176]{1,0:T(8,128)(2,1)} %constant.281.clone.back_down_ref) | copy-start | bytes 168964
  66.7 36.5 %copy-start.6 = (s32[12288]{0:T(1024)S(1)}, s32[12288]{0:T(1024)}, u32[]{:S(2)}) copy-start(s32[12288]{0:T(1024)} %reshape.663) | copy-start | bytes 147460
  69.9 33.3 %copy-start.7 = (s32[256]{0:T(256)S(1)}, s32[256]{0:T(256)}, u32[]{:S(2)}) copy-start(s32[256]{0:T(256)} %compare_select_fusion.20) | copy-start | bytes 3076
  107.6 58.8 %all-to-all-start = ((f32[32,3,384]{2,1,0:T(4,128)}), f32[32,3,384]{2,1,0:T(4,128)S(1)}, u32[]{:S(2)}, u32[]{:S(2)}) async-start(f32[32,3,384]{2,1,0:T(4,128)} %bitcast.7), calls=%async_computation | async-start | bytes 393216 | tf_op jit(solution)/shard_map/all_to_all | solution.py:424

commit v3 on v2

--- a/solution.py
+++ b/solution.py
@@ -69,7 +69,8 @@
 A_BLOCK, A_ROW, A_ROW_REST, A_COL_REST = 4, 5, 6, 7
 NEAR_ROW, NEAR_COL = 8, 9
 FIELDS = 10
-STAGES = 6
+BATCH = 4
+RING = 16
 
 
 def cut(strip, start):
@@ -95,15 +96,9 @@
     out_ref,
     *scratch,
 ):
-    patches, halves, crosses, inverses, corrs, maxima = (
-        scratch[0:2],
-        scratch[2:4],
-        scratch[4:6],
-        scratch[6:8],
-        scratch[8:12],
-        scratch[12:14],
-    )
-    energies, scales, totals, row_moments, col_moments, runners, a_ref, b_ref = scratch[14:22]
+    patches, halves, crosses, inverses = scratch[:4]
+    corrs = scratch[4:6]
+    energies, totals, row_moments, col_moments, runners, a_ref, b_ref = scratch[6:]
     count = count_ref[0]
     n_row, n_col, a_rows = grid
 
@@ -131,147 +126,141 @@
         for block in range(1, a_ref.shape[0]):
             a_ref[block, place, :] = cut(strip, (block - 1) * PATCH)
 
-    def at(step, stage):
-        return jnp.clip(step - stage, 0, capacity - 1)
-
-    def extract(source, block, row, row_rest, col_rest, target, base):
-        lanes = lax.broadcasted_iota(jnp.int32, (PATCH, WIDE), 1)
-        low = source[block, pl.ds(row, PATCH), :]
-        high = source[block + 1, pl.ds(row, PATCH), :]
-        body = jnp.where(lanes >= col_rest, low, high)
-        low = source[block, pl.ds(row + PATCH, 16), :]
-        high = source[block + 1, pl.ds(row + PATCH, 16), :]
-        tail = jnp.where(lanes[:16] >= col_rest, low, high)
-        rows = lax.broadcasted_iota(jnp.int32, (16, WIDE), 0)
-        head = jnp.where(rows >= row_rest, body[:16], tail)
-        target[base : base + 16, :] = head
-        target[base + 16 : base + PATCH, :] = body[16:]
-        head = head.astype(jnp.float32)
-        body = body[16:].astype(jnp.float32)
-        total = jnp.sum((head * head).reshape(2, 8, WIDE), axis=0) + jnp.sum(
-            (body * body).reshape(PATCH // 8 - 2, 8, WIDE), axis=0
+    def at(step, stage, part):
+        return jnp.clip(BATCH * (step - stage) + part, 0, capacity - 1)
+
+    def extract(source, block, row, row_rest, col_rest, base):
+        lanes = lax.broadcasted_iota(jnp.int32, (16, WIDE), 1) >= col_rest
+        rows = lax.broadcasted_iota(jnp.int32, (16, WIDE), 0) >= row_rest
+
+        def group(place):
+            here = pl.ds(pl.multiple_of(row + 16 * place, 16), 16)
+            return jnp.where(lanes, source[block, here, :], source[block + 1, here, :])
+
+        total = jnp.zeros((8, WIDE), jnp.float32)
+        for place in range(PATCH // 16):
+            values = group(place)
+            if place == 0:
+                values = jnp.where(rows, values, group(PATCH // 16))
+            patches[base + 16 * place : base + 16 * place + 16, :] = values
+            values = values.astype(jnp.float32)
+            values = values * values
+            total = total + (values[:8] + values[8:])
+        return total[:, :HALF_LANES] + total[:, HALF_LANES:]
+
+    def stage_half(step):
+        for part in range(BATCH):
+            item = at(step, 0, part)
+            for which, source, fields in (
+                (0, a_ref, (A_BLOCK, A_ROW, A_ROW_REST, A_COL_REST)),
+                (1, b_ref, (B_BLOCK, B_ROW, B_ROW_REST, B_COL_REST)),
+            ):
+                block, row, row_rest, col_rest = (items_ref[field, item] for field in fields)
+                energies[item % RING, which] = extract(
+                    source, block, row, row_rest, col_rest, (2 * part + which) * PATCH
+                )
+        half = jnp.dot(patches[...], across_ref[...], preferred_element_type=jnp.float32)
+        halves[...] = half.astype(jnp.bfloat16)
+
+    def sides(spec, group):
+        cc = spec[16 * group : 16 * group + 8, :HALF_LANES]
+        cs = spec[16 * group : 16 * group + 8, HALF_LANES:]
+        sc = spec[16 * group + 8 : 16 * group + 16, :HALF_LANES]
+        ss = spec[16 * group + 8 : 16 * group + 16, HALF_LANES:]
+        return cc - ss, sc + cs, cc + ss, sc - cs
+
+    def stage_inverse():
+        down = down_ref[...]
+        for part in range(BATCH):
+            base = 2 * part * PATCH
+            spec_a = jnp.dot(
+                down, halves[base : base + PATCH, :], preferred_element_type=jnp.float32
+            )
+            base = base + PATCH
+            spec_b = jnp.dot(
+                down, halves[base : base + PATCH, :], preferred_element_type=jnp.float32
+            )
+            for group in range(GROUPS):
+                a_pr, a_pi, a_mr, a_mi = sides(spec_a, group)
+                b_pr, b_pi, b_mr, b_mi = sides(spec_b, group)
+                pr = a_pr * b_pr + a_pi * b_pi
+                pi = a_pr * b_pi - a_pi * b_pr
+                mr = a_mr * b_mr + a_mi * b_mi
+                mi = a_mr * b_mi - a_mi * b_mr
+                upper = jnp.concatenate([pr + mr, pi - mi], axis=1)
+                lower = jnp.concatenate([pi + mi, mr - pr], axis=1)
+                crosses[part, 16 * group : 16 * group + 16, :] = jnp.concatenate(
+                    [upper, lower], axis=0
+                ).astype(jnp.bfloat16)
+        for part in range(BATCH):
+            inverse = jnp.dot(
+                back_down_ref[...], crosses[part], preferred_element_type=jnp.float32
+            )
+            inverses[PATCH * part : PATCH * (part + 1), :] = inverse.astype(jnp.bfloat16)
+
+    def stage_score(step):
+        corr_all = jnp.dot(
+            inverses[...], back_across_ref[...], preferred_element_type=jnp.float32
         )
-        return total[:, :HALF_LANES] + total[:, HALF_LANES:]
-
-    def stage_patch(step, now):
-        item = at(step, 0)
-        slot = item % 8
-        for which, source, base, fields in (
-            (0, a_ref, 0, (A_BLOCK, A_ROW, A_ROW_REST, A_COL_REST)),
-            (1, b_ref, PATCH, (B_BLOCK, B_ROW, B_ROW_REST, B_COL_REST)),
-        ):
-            block, row, row_rest, col_rest = (items_ref[field, item] for field in fields)
-            energies[slot, which] = extract(
-                source, block, pl.multiple_of(row, 16), row_rest, col_rest, patches[now], base
-            )
-
-    def stage_half(step, was, now):
-        item = at(step, 1)
-        slot = item % 8
-        half = jnp.dot(patches[was][...], across_ref[...], preferred_element_type=jnp.float32)
-        halves[now][...] = half.astype(jnp.bfloat16)
-        mean_a = jnp.sum(energies[slot, 0], keepdims=True) * (1.0 / (PATCH * PATCH))
-        mean_b = jnp.sum(energies[slot, 1], keepdims=True) * (1.0 / (PATCH * PATCH))
-        scale = 1.0 / (
-            float(PATCH**4) * jnp.sqrt(mean_a + epsilon) * jnp.sqrt(mean_b + epsilon)
-        )
-        scales[slot] = jnp.broadcast_to(scale, (8, HALF_LANES))
-
-    def stage_cross(step, was, now):
-        down = down_ref[...]
-        spec_a = jnp.dot(down, halves[was][:PATCH, :], preferred_element_type=jnp.float32)
-        spec_b = jnp.dot(down, halves[was][PATCH:, :], preferred_element_type=jnp.float32)
-
-        def sides(spec, group):
-            cc = spec[16 * group : 16 * group + 8, :HALF_LANES]
-            cs = spec[16 * group : 16 * group + 8, HALF_LANES:]
-            sc = spec[16 * group + 8 : 16 * group + 16, :HALF_LANES]
-            ss = spec[16 * group + 8 : 16 * group + 16, HALF_LANES:]
-            return cc - ss, sc + cs, cc + ss, sc - cs
-
-        for group in range(GROUPS):
-            a_pr, a_pi, a_mr, a_mi = sides(spec_a, group)
-            b_pr, b_pi, b_mr, b_mi = sides(spec_b, group)
-            pr = a_pr * b_pr + a_pi * b_pi
-            pi = a_pr * b_pi - a_pi * b_pr
-            mr = a_mr * b_mr + a_mi * b_mi
-            mi = a_mr * b_mi - a_mi * b_mr
-            upper = jnp.concatenate([pr + mr, pi - mi], axis=1)
-            lower = jnp.concatenate([pi + mi, mr - pr], axis=1)
-            crosses[now][16 * group : 16 * group + 16, :] = jnp.concatenate(
-                [upper, lower], axis=0
-            ).astype(jnp.bfloat16)
-
-    def stage_inverse(step, was, now):
-        inverse = jnp.dot(
-            back_down_ref[...], crosses[was][...], preferred_element_type=jnp.float32
-        )
-        inverses[now][...] = inverse.astype(jnp.bfloat16)
-
-    def stage_correlation(step, was, now):
-        item = at(step, 4)
-        corr = jnp.dot(
-            inverses[was][...], back_across_ref[...], preferred_element_type=jnp.float32
-        )
-        for part in range(2):
-            side = corr[:, part * HALF_LANES : (part + 1) * HALF_LANES]
-            corrs[2 * now + part][:PATCH, :] = side
-            corrs[2 * now + part][PATCH:, :] = side[:8]
-        caps = caps_ref[pl.ds(PATCH - items_ref[NEAR_ROW, item], PATCH), :]
-        left = jnp.max(
-            jnp.minimum(corr[:, :HALF_LANES], caps).reshape(PATCH // 8, 8, HALF_LANES), axis=0
-        )
-        right = jnp.max(
-            jnp.minimum(corr[:, HALF_LANES:], caps).reshape(PATCH // 8, 8, HALF_LANES), axis=0
-        )
-        lanes = lax.broadcasted_iota(jnp.int32, (8, HALF_LANES), 1)
-        maxima[now][...] = jnp.maximum(
-            left, jnp.where(lanes < PATCH - HALF_LANES, right, -BIG)
-        )
-
-    def stage_near(step, was):
-        item = at(step, 5)
-        scale = scales[item % 8]
-        near_row = items_ref[NEAR_ROW, item]
-        near_col = items_ref[NEAR_COL, item]
         rows = lax.broadcasted_iota(jnp.int32, (8, HALF_LANES), 0)
         lanes = lax.broadcasted_iota(jnp.int32, (8, HALF_LANES), 1)
         shift_rows = (rows - centre_reach).astype(jnp.float32)
         row_near = rows <= 2 * centre_reach
-        total, row_moment, col_moment = 0.0, 0.0, 0.0
-        best = maxima[was][...]
-        for part in range(2):
-            values = corrs[2 * was + part][pl.ds(near_row, 8), :]
-            place = lanes + part * HALF_LANES
-            shift = place - near_col
-            shift = jnp.where(shift >= PATCH // 2, shift - PATCH, shift)
-            shift = jnp.where(shift < -(PATCH // 2), shift + PATCH, shift)
-            inside = row_near & (place < PATCH)
-            close = jnp.abs(shift) <= centre_reach
-            weight = jnp.where(
-                inside & close, jnp.exp(sharpness * (values * scale)), 0.0
+        for part in range(BATCH):
+            item = at(step, 2, part)
+            near_row = items_ref[NEAR_ROW, item]
+            near_col = items_ref[NEAR_COL, item]
+            ring = item % RING
+            mean_a = jnp.sum(energies[ring, 0], keepdims=True) * (1.0 / (PATCH * PATCH))
+            mean_b = jnp.sum(energies[ring, 1], keepdims=True) * (1.0 / (PATCH * PATCH))
+            scale = 1.0 / (
+                float(PATCH**4) * jnp.sqrt(mean_a + epsilon) * jnp.sqrt(mean_b + epsilon)
             )
-            total = total + weight
-            row_moment = row_moment + weight * shift_rows
-            col_moment = col_moment + weight * shift.astype(jnp.float32)
-            best = jnp.maximum(
-                best, jnp.where(inside & jnp.logical_not(close), values, -BIG)
-            )
-        totals[pl.ds(item, 1), :] = jnp.sum(total, axis=0, keepdims=True)
-        row_moments[pl.ds(item, 1), :] = jnp.sum(row_moment, axis=0, keepdims=True)
-        col_moments[pl.ds(item, 1), :] = jnp.sum(col_moment, axis=0, keepdims=True)
-        runners[pl.ds(item, 1), :] = jnp.max(best * scale, axis=0, keepdims=True)
-
-    @pl.loop(0, (count + STAGES) // 2)
-    def _(pair):
-        for now in range(2):
-            step = 2 * pair + now
-            stage_near(step, 1 - now)
-            stage_correlation(step, 1 - now, now)
-            stage_inverse(step, 1 - now, now)
-            stage_cross(step, 1 - now, now)
-            stage_half(step, 1 - now, now)
-            stage_patch(step, now)
+            caps = caps_ref[pl.ds(PATCH - near_row, PATCH), :]
+            total, row_moment, col_moment = 0.0, 0.0, 0.0
+            best = None
+            for half in range(2):
+                corr = corr_all[
+                    PATCH * part : PATCH * (part + 1),
+                    half * HALF_LANES : (half + 1) * HALF_LANES,
+                ]
+                corrs[half][part, :PATCH, :] = corr
+                corrs[half][part, PATCH:, :] = corr[:8]
+                far = jnp.max(
+                    jnp.minimum(corr, caps).reshape(PATCH // 8, 8, HALF_LANES), axis=0
+                )
+                if half == 0:
+                    best = far
+                else:
+                    far = jnp.where(lanes < PATCH - HALF_LANES, far, -BIG)
+                    best = jnp.maximum(best, far)
+            for half in range(2):
+                values = corrs[half][part, pl.ds(near_row, 8), :]
+                place = lanes + half * HALF_LANES
+                shift = place - near_col
+                shift = jnp.where(shift >= PATCH // 2, shift - PATCH, shift)
+                shift = jnp.where(shift < -(PATCH // 2), shift + PATCH, shift)
+                inside = row_near & (place < PATCH)
+                close = jnp.abs(shift) <= centre_reach
+                weight = jnp.where(
+                    inside & close, jnp.exp(sharpness * (values * scale)), 0.0
+                )
+                total = total + weight
+                row_moment = row_moment + weight * shift_rows
+                col_moment = col_moment + weight * shift.astype(jnp.float32)
+                best = jnp.maximum(
+                    best, jnp.where(inside & jnp.logical_not(close), values, -BIG)
+                )
+            totals[pl.ds(item, 1), :] = jnp.sum(total, axis=0, keepdims=True)
+            row_moments[pl.ds(item, 1), :] = jnp.sum(row_moment, axis=0, keepdims=True)
+            col_moments[pl.ds(item, 1), :] = jnp.sum(col_moment, axis=0, keepdims=True)
+            runners[pl.ds(item, 1), :] = jnp.max(best * scale, axis=0, keepdims=True)
+
+    @pl.loop(0, (count + BATCH - 1) // BATCH + 2)
+    def _(step):
+        stage_score(step)
+        stage_inverse()
+        stage_half(step)
 
     lanes = lax.broadcasted_iota(jnp.int32, (capacity, HALF_LANES), 1)
     used = lax.broadcasted_iota(jnp.int32, (capacity, HALF_LANES), 0) < count
@@ -288,7 +277,6 @@
     n_row, n_col, a_rows = grid
     a_blocks = (n_col * everyone.shape[2] + 76) // PATCH + 2
     b_blocks = -(-tile.shape[1] // PATCH)
-    pair = lambda rows, dtype: [pltpu.VMEM((rows, WIDE), dtype)] * 2
     vmem = pl.BlockSpec(memory_space=pltpu.VMEM)
     smem = pl.BlockSpec(memory_space=pltpu.SMEM)
     rows = pltpu.VMEM((capacity, HALF_LANES), jnp.float32)
@@ -297,15 +285,14 @@
         out_shape=jax.ShapeDtypeStruct((capacity, HALF_LANES), jnp.float32),
         in_specs=[smem, smem] + [vmem] * 7,
         out_specs=vmem,
-        scratch_shapes=pair(2 * PATCH, jnp.bfloat16)
-        + pair(2 * PATCH, jnp.bfloat16)
-        + pair(PAIRED, jnp.bfloat16)
-        + pair(PATCH, jnp.bfloat16)
-        + [pltpu.VMEM((PATCH + 8, HALF_LANES), jnp.float32)] * 4
-        + [pltpu.VMEM((8, HALF_LANES), jnp.float32)] * 2
-        + [
-            pltpu.VMEM((8, 2, 8, HALF_LANES), jnp.float32),
-            pltpu.VMEM((8, 8, HALF_LANES), jnp.float32),
+        scratch_shapes=[
+            pltpu.VMEM((2 * BATCH * PATCH, WIDE), jnp.bfloat16),
+            pltpu.VMEM((2 * BATCH * PATCH, WIDE), jnp.bfloat16),
+            pltpu.VMEM((BATCH, PAIRED, WIDE), jnp.bfloat16),
+            pltpu.VMEM((BATCH * PATCH, WIDE), jnp.bfloat16),
+            pltpu.VMEM((BATCH, PATCH + 8, HALF_LANES), jnp.float32),
+            pltpu.VMEM((BATCH, PATCH + 8, HALF_LANES), jnp.float32),
+            pltpu.VMEM((RING, 2, 8, HALF_LANES), jnp.float32),
         ]
         + [rows] * 4
         + [
@@ -342,7 +329,9 @@
     ).astype(jnp.bfloat16)
     fields = jnp.pad(fields, ((0, 0), (0, WIDE - nodes))).reshape(16, HALF_LANES)
     sent = jnp.concatenate([a_window, fields], axis=0)
-    everyone = lax.all_gather(lax.all_gather(sent, "col"), "row")
+    sent = jnp.broadcast_to(sent[None], (n_col,) + sent.shape)
+    sent = lax.all_to_all(sent, "col", split_axis=0, concat_axis=0, tiled=True)
+    everyone = lax.all_gather(sent, "row")
     everyone = everyone.reshape(devices, a_rows + 16, a_cols)
 
     known = everyone[:, a_rows:].reshape(devices, 8, WIDE)[:, :, :nodes]

time: 167 us -> 121 us (0.72); the launches traced: 168 us -> 120 us
  blocking collectives: 41 us -> 8.82 us
  starting transfers between devices: 50.2 us -> 35.3 us
  other arithmetic: 13.8 us -> 7.76 us
  waiting for transfers between devices: 6.95 us -> 12.7 us
  Pallas kernels: 31.8 us -> 29.3 us
    all_gather x2 -> x1, blocking collectives: 41 us -> 8.82 us  [per_device(): everyone = lax.all_gather(sent, 'row')]
    all_to_all x1, starting transfers between devices: 50.2 us -> 28 us  [per_device(): lax.all_to_all(spread, ('row', 'col'), split_axis=0, concat_axis=0, tiled...]
    all_to_all x0 -> x1, starting transfers between devices: none -> 7.25 us  [per_device(): sent = lax.all_to_all(sent, 'col', split_axis=0, concat_axis=0, tiled=True)]
    all_to_all x0 -> x1, waiting for transfers between devices: none -> 5.66 us  [per_device(): sent = lax.all_to_all(sent, 'col', split_axis=0, concat_axis=0, tiled=True)]
    pallas_call x1, Pallas kernels: 31.8 us -> 29.3 us  [correlate(): pl.pallas_call(functools.partial(correlate_kernel, capacity, grid), out_s...]
  transfers between devices with their start and end apart: 1 -> 2, of which waited for: 1 -> 2; matrix products, arithmetic and copies ran while one was open for 1% -> 3% of each run, Pallas kernels for 0% -> 0%
where the time goes in v3:
time: 121 us; the launch traced here: 120 us
  starting transfers between devices  35.3 us (29%)
  Pallas kernels  29.3 us (24%)
  local copies, waits for them, and re-layouts  17.8 us (15%)
  waiting for transfers between devices  12.7 us (10%)
  blocking collectives  8.82 us (7%)
  other arithmetic  7.76 us (6%)
  matrix products  6.93 us (6%)
  between operations  1.58 us (1%)
    pallas_call x1, Pallas kernels, correlate(): pl.pallas_call(functools.partial(correlate_kernel, capacity, grid), out_s...  29.3 us
    all_to_all x1, starting transfers between devices, per_device(): lax.all_to_all(spread, ('row', 'col'), split_axis=0, concat_axis=0, tiled...  28 us
    all_gather x1, blocking collectives, per_device(): everyone = lax.all_gather(sent, 'row')  8.82 us
    all_to_all x1, starting transfers between devices, per_device(): sent = lax.all_to_all(sent, 'col', split_axis=0, concat_axis=0, tiled=True)  7.25 us
    all_to_all x1, waiting for transfers between devices, per_device(): lax.all_to_all(spread, ('row', 'col'), split_axis=0, concat_axis=0, tiled...  7.06 us
    all_to_all x1, waiting for transfers between devices, per_device(): sent = lax.all_to_all(sent, 'col', split_axis=0, concat_axis=0, tiled=True)  5.66 us
    dot_general x1, matrix products, per_device(): lax.dot_general(result, (node[:, None] == wanted[None, :]).astype(jnp.flo...  4.29 us
  transfers between devices with their start and end apart: 2, of which 2 were waited for; matrix products, arithmetic and copies ran while one was open for 3% of the time, Pallas kernels for 0%

profile of v3, /device:TPU:0, one launch (start us, length us, event | category | flops | bytes accessed | tf_op | source)
XLA Modules:
  0.0 120.2 jit_solution(4747887930129830902)
XLA Ops:
  0.6 0.8 reshape.629
  1.4 0.8 reshape.630
  2.2 0.7 convert.36
  3.2 0.7 convert_reduce_fusion.2
  4.0 0.7 pad_maximum_fusion
  4.8 0.7 broadcast_in_dim.82
  5.5 7.3 %all-to-all-start = ((bf16[8,96,128]{2,1,0:T(8,128)(2,1)}), bf16[8,96,128]{2,1,0:T(8,128)(2,1)}, u32[]{:S(2)}, u32[]{:S(2)}) async-start(bf16[8,96,128]{2,1,0:T(8,128)(2,1)} %broadcast_in_dim.82), calls=%async_computation | async-start | bytes 393216 | tf_op jit(solution)/shard_map/all_to_all | solution.py:333
  13.6 0.7 broadcast_in_dim_broadcast_in_dim.13
  15.1 5.7 %all-to-all-done = bf16[8,96,128]{2,1,0:T(8,128)(2,1)} async-done(((bf16[8,96,128]{2,1,0:T(8,128)(2,1)}), bf16[8,96,128]{2,1,0:T(8,128)(2,1)}, u32[]{:S(2)}, u32[]{:S(2)}) %all-to-all-start) | async-done | bytes 196640 | tf_op jit(solution)/shard_map/all_to_all | solution.py:333
  20.8 8.8 %all-gather.everyone_ref = bf16[32,96,128]{2,1,0:T(8,128)(2,1)S(1)} all-gather(bf16[8,96,128]{2,1,0:T(8,128)(2,1)} %all-to-all-done), channel_id=2, replica_groups=mesh['row'=4,'col'=8] {'row'}, dimensions={0}, use_global_device_ids=true | all-gather | bytes 983040 | tf_op jit(solution)/shard_map/all_gather | solution.py:334
  30.3 1.6 %reshape.633 = bf16[32,8,256]{2,1,0:T(8,128)(2,1)} reshape(bf16[32,16,128]{2,1,0:T(8,128)(2,1)} %slice.133) | data formatting | bytes 262144 | tf_op jit(solution)/shard_map/reshape | solution.py:337
  31.9 0.9 slice.134
  32.8 1.5 %slice_bitcast_fusion = bf16[8,32,160]{2,0,1:T(8,128)(2,1)} fusion(bf16[32,8,256]{2,1,0:T(8,128)(2,1)} %reshape.633), kind=kLoop, calls=%fused_computation.19 | loop fusion | bytes 163840 | tf_op jit(solution)/shard_map/transpose | solution.py:356
  35.1 0.8 fusion.7
  35.9 1.4 %eq.61 = s32[5120]{0:T(1024)} reshape(s32[32,160]{1,0:T(8,128)} %fusion.7) | data formatting | bytes 40960 | tf_op jit(solution)/shard_map/eq | solution.py:350
  37.3 1.6 %copy.30 = bf16[7,32,160]{2,1,0:T(8,128)(2,1)} copy(bf16[7,32,160]{2,0,1:T(8,128)(2,1)} %bitcast.23) | data formatting | bytes 143360 | tf_op jit(solution)/shard_map/slice | solution.py:356
  38.9 1.7 %concatenate.10 = bf16[7,5120]{1,0:T(8,128)(2,1)} reshape(bf16[7,32,160]{2,1,0:T(8,128)(2,1)} %copy.30) | data formatting | bytes 143360 | tf_op jit(solution)/shard_map/concatenate | solution.py:354
  41.3 1.9 %fusion.8 = s32[9,256]{1,0:T(8,128)S(1)} fusion(s32[5120]{0:T(1024)} %eq.61, bf16[1,5120]{1,0:T(2,128)(2,1)} %convert_element_type.52, bf16[1,5120]{1,0:T(2,128)(2,1)} %broadcast_in_dim_broadcast_in_dim.13, bf16[7,5120]{1,0:T(8,128)(2,1)} %concatenate.10), kind=kOutput, calls=%fused_computation.10 | convolution fusion | flops 25182464 | bytes 121856 | tf_op jit(solution)/shard_map/dot_general | solution.py:362
  46.7 1.4 %stack.6.items_ref = s32[10,256]{1,0:T(8,128)S(1)} concatenate(s32[1,256]{1,0:T(1,128)} %and_select_fusion.13, s32[1,256]{1,0:T(1,128)} %fusion.55, s32[1,256]{1,0:T(1,128)} %get-tuple-element.23, s32[1,256]{1,0:T(1,128)} %get-tuple-element.35, s32[1,256]{1,0:T(1,128)} %and_select_fusion.7, s32[1,256]{1,0:T(1,128)} %fusion.56, s32[1,256]{1,0:T(1,128)} %get-tuple-element.20, ...), dimensions={0} | concatenate | bytes 20480 | tf_op jit(solution)/shard_map/stack | solution.py:376
  48.2 29.3 %shard_map.122 = f32[256,128]{1,0:T(8,128)S(1)} custom-call(s32[1]{0:T(128)} %bitcast.1.count_ref, s32[10,256]{1,0:T(8,128)S(1)} %stack.6.items_ref, bf16[32,96,128]{2,1,0:T(8,128)(2,1)S(1)} %all-gather.everyone_ref, bf16[1024,1024]{1,0:T(8,128)(2,1)S(1)} %copy-done, bf16[256,256]{1,0:T(8,128)(2,1)S(1)} %copy-done.2, bf16[176,160]{1,0:T(8,128)(2,1)S(1)} %copy-done.4, ...), custom_call_target="tpu_custom_call" | custom-call | tf_op jit(solution)/shard_map/pallas_call | solution.py:283
  77.5 4.3 %fusion = f32[3,12288]{1,0:T(4,128)} fusion(s32[12288]{0:T(1024)S(1)} %reshape.663, s32[256]{0:T(256)S(1)} %copy-done.6, f32[256,128]{1,0:T(8,128)S(1)} %shard_map.122), kind=kOutput, calls=%fused_computation | convolution fusion | flops 116391936 | bytes 328704 | tf_op jit(solution)/shard_map/dot_general | solution.py:406
  81.8 28.0 %all-to-all-start.1 = ((f32[32,3,384]{2,1,0:T(4,128)}), f32[32,3,384]{2,1,0:T(4,128)S(1)}, u32[]{:S(2)}, u32[]{:S(2)}) async-start(f32[32,3,384]{2,1,0:T(4,128)} %bitcast.6), calls=%async_computation.1 | async-start | bytes 393216 | tf_op jit(solution)/shard_map/all_to_all | solution.py:413
  109.9 0.9 slice.147
  111.3 7.1 %all-to-all-done.1 = f32[32,3,384]{2,1,0:T(4,128)S(1)} async-done(((f32[32,3,384]{2,1,0:T(4,128)}), f32[32,3,384]{2,1,0:T(4,128)S(1)}, u32[]{:S(2)}, u32[]{:S(2)}) %all-to-all-start.1) | async-done | bytes 147488 | tf_op jit(solution)/shard_map/all_to_all | solution.py:413
  (69 shorter events, 9.3 us)
Async XLA Ops:
  5.5 15.3 %all-to-all-start = ((bf16[8,96,128]{2,1,0:T(8,128)(2,1)}), bf16[8,96,128]{2,1,0:T(8,128)(2,1)}, u32[]{:S(2)}, u32[]{:S(2)}) async-start(bf16[8,96,128]{2,1,0:T(8,128)(2,1)} %broadcast_in_dim.82), calls=%async_computation | async-start | bytes 393216 | tf_op jit(solution)/shard_map/all_to_all | solution.py:333
  15.1 33.0 %copy-start = (bf16[1024,1024]{1,0:T(8,128)(2,1)S(1)}, bf16[1024,1024]{1,0:T(8,128)(2,1)}, u32[]{:S(2)}) copy-start(bf16[1024,1024]{1,0:T(8,128)(2,1)} %tile_ref.1) | copy-start | bytes 6291460
  15.1 33.0 %copy-start.1 = (f32[320,128]{1,0:T(8,128)S(1)}, f32[320,128]{1,0:T(8,128)}, u32[]{:S(2)}) copy-start(f32[320,128]{1,0:T(8,128)} %constant.283.clone.caps_ref) | copy-start | bytes 491524
  15.1 33.0 %copy-start.2 = (bf16[256,256]{1,0:T(8,128)(2,1)S(1)}, bf16[256,256]{1,0:T(8,128)(2,1)}, u32[]{:S(2)}) copy-start(bf16[256,256]{1,0:T(8,128)(2,1)} %constant.279.clone.across_ref) | copy-start | bytes 393220
  15.1 33.1 %copy-start.3 = (bf16[256,256]{1,0:T(8,128)(2,1)S(1)}, bf16[256,256]{1,0:T(8,128)(2,1)}, u32[]{:S(2)}) copy-start(bf16[256,256]{1,0:T(8,128)(2,1)} %constant.282.clone.back_across_ref) | copy-start | bytes 393220
  15.1 33.0 %copy-start.4 = (bf16[176,160]{1,0:T(8,128)(2,1)S(1)}, bf16[176,160]{1,0:T(8,128)(2,1)}, u32[]{:S(2)}) copy-start(bf16[176,160]{1,0:T(8,128)(2,1)} %constant.280.clone.down_ref) | copy-start | bytes 168964
  15.1 33.0 %copy-start.5 = (bf16[160,176]{1,0:T(8,128)(2,1)S(1)}, bf16[160,176]{1,0:T(8,128)(2,1)}, u32[]{:S(2)}) copy-start(bf16[160,176]{1,0:T(8,128)(2,1)} %constant.281.clone.back_down_ref) | copy-start | bytes 168964
  48.1 29.3 %copy-start.6 = (s32[256]{0:T(256)S(1)}, s32[256]{0:T(256)}, u32[]{:S(2)}) copy-start(s32[256]{0:T(256)} %compare_select_fusion.20) | copy-start | bytes 3076
  77.5 32.3 %copy-start.7 = (pred[10]{0:T(512)(128)(4,1)S(1)}, pred[10]{0:T(512)(128)(4,1)}, u32[]{:S(2)}) copy-start(pred[10]{0:T(512)(128)(4,1)} %compare_and_fusion.5) | copy-start | bytes 34
  81.8 36.6 %all-to-all-start.1 = ((f32[32,3,384]{2,1,0:T(4,128)}), f32[32,3,384]{2,1,0:T(4,128)S(1)}, u32[]{:S(2)}, u32[]{:S(2)}) async-start(f32[32,3,384]{2,1,0:T(4,128)} %bitcast.6), calls=%async_computation.1 | async-start | bytes 393216 | tf_op jit(solution)/shard_map/all_to_all | solution.py:413

commit v4 on v3

--- a/solution.py
+++ b/solution.py
@@ -10,6 +10,7 @@
 from jax.sharding import PartitionSpec as P
 
 PATCH = 160
+NODE_LANES = 16
 STRIDE = 8
 RELAX = 2
 WIDE = 256
@@ -65,6 +66,25 @@
     )
 
 
+def listing_tables():
+    lane = np.arange(HALF_LANES)
+    group, place = lane // NODE_LANES, lane % NODE_LANES
+    repeat = (lane[:, None] < NODE_LANES) & (place[None] == lane[:, None])
+    earlier = (group[:, None] == group[None]) & (place[:, None] < place[None])
+    first = np.broadcast_to(lane[:, None] < NODE_LANES, (HALF_LANES, HALF_LANES))
+    below = lane[None] < lane[:, None]
+    counting = np.concatenate([repeat, earlier, first, below, below.T, first.T], axis=1)
+    fields = np.zeros((2 * HALF_LANES, HALF_LANES), np.float32)
+    fields[lane, group] = 1.0
+    fields[HALF_LANES, MESH_ROW] = 1.0
+    return (
+        jnp.asarray(counting, jnp.bfloat16),
+        jnp.asarray(fields, jnp.bfloat16),
+        jnp.asarray(fields.T[:16], jnp.bfloat16),
+    )
+
+
+OWNER, ROW_HIGH, ROW_LOW, COL_HIGH, COL_LOW, PEAK_ROW, PEAK_COL, MESH_COL, MESH_ROW = range(9)
 B_BLOCK, B_ROW, B_ROW_REST, B_COL_REST = 0, 1, 2, 3
 A_BLOCK, A_ROW, A_ROW_REST, A_COL_REST = 4, 5, 6, 7
 NEAR_ROW, NEAR_COL = 8, 9
@@ -84,8 +104,6 @@
 def correlate_kernel(
     capacity,
     grid,
-    count_ref,
-    items_ref,
     everyone_ref,
     tile_ref,
     across_ref,
@@ -93,14 +111,29 @@
     back_down_ref,
     back_across_ref,
     caps_ref,
+    counting_ref,
+    fields_ref,
+    fields_turned_ref,
     out_ref,
     *scratch,
 ):
     patches, halves, crosses, inverses = scratch[:4]
     corrs = scratch[4:6]
-    energies, totals, row_moments, col_moments, runners, a_ref, b_ref = scratch[6:]
-    count = count_ref[0]
-    n_row, n_col, a_rows = grid
+    energies, totals, row_moments, col_moments, runners, a_ref, b_ref = scratch[6:13]
+    columns_ref, listed_ref, items_ref, semaphore = scratch[13:]
+    n_row, n_col, a_rows, node_rows = grid
+    count = list_nodes(
+        capacity,
+        grid,
+        everyone_ref,
+        counting_ref,
+        fields_ref,
+        fields_turned_ref,
+        columns_ref,
+        listed_ref,
+    )
+    to_scalars = pltpu.make_async_copy(listed_ref, items_ref, semaphore)
+    to_scalars.start()
 
     height = tile_ref.shape[0]
 
@@ -256,34 +289,161 @@
             col_moments[pl.ds(item, 1), :] = jnp.sum(col_moment, axis=0, keepdims=True)
             runners[pl.ds(item, 1), :] = jnp.max(best * scale, axis=0, keepdims=True)
 
+    to_scalars.wait()
+
     @pl.loop(0, (count + BATCH - 1) // BATCH + 2)
     def _(step):
         stage_score(step)
         stage_inverse()
         stage_half(step)
 
+    used = lax.broadcasted_iota(jnp.int32, (capacity, 1), 0) < count
+    total = jnp.sum(totals[...], axis=1, keepdims=True)
+    peak_row = columns_ref[:, PEAK_ROW : PEAK_ROW + 1]
+    peak_col = columns_ref[:, PEAK_COL : PEAK_COL + 1]
+    results = (
+        peak_row + jnp.sum(row_moments[...], axis=1, keepdims=True) / total,
+        peak_col + jnp.sum(col_moments[...], axis=1, keepdims=True) / total,
+        jnp.maximum(jnp.max(runners[...], axis=1, keepdims=True), -2.0),
+    )
     lanes = lax.broadcasted_iota(jnp.int32, (capacity, HALF_LANES), 1)
-    used = lax.broadcasted_iota(jnp.int32, (capacity, HALF_LANES), 0) < count
-    total = jnp.sum(totals[...], axis=1, keepdims=True)
-    rows = jnp.sum(row_moments[...], axis=1, keepdims=True) / total
-    cols = jnp.sum(col_moments[...], axis=1, keepdims=True) / total
-    best = jnp.maximum(jnp.max(runners[...], axis=1, keepdims=True), -2.0)
-    result = jnp.where(lanes == 0, rows, jnp.where(lanes == 1, cols, best))
-    out_ref[...] = jnp.where(used & (lanes < 3), result, 0.0)
-
-
-def correlate(count, items, everyone, tile, grid):
-    capacity = items.shape[1]
-    n_row, n_col, a_rows = grid
+    terms = jnp.zeros((capacity, HALF_LANES), jnp.float32)
+    for value, rest in enumerate(results):
+        rest = jnp.where(used, rest, 0.0)
+        for term in range(3):
+            here = rest.astype(jnp.bfloat16).astype(jnp.float32)
+            terms = jnp.where(lanes == 8 * term + value, here, terms)
+            rest = rest - here
+    square = (32, HALF_LANES)
+    pick = lax.broadcasted_iota(jnp.int32, square, 0) == lax.broadcasted_iota(jnp.int32, square, 1)
+    terms = lax.dot_general(
+        jnp.where(pick, 1.0, 0.0).astype(jnp.bfloat16),
+        terms.astype(jnp.bfloat16),
+        (((1,), (1,)), ((), ())),
+        preferred_element_type=jnp.float32,
+    ).astype(jnp.bfloat16)
+
+    height, breadth = n_row * node_rows, n_col * NODE_LANES
+    tall, broad = node_rows + 2 * RELAX, NODE_LANES + 2 * RELAX
+    width = out_ref.shape[2]
+    node = columns_ref[:, MESH_ROW : MESH_ROW + 1] * float(breadth)
+    node = node + columns_ref[:, MESH_COL : MESH_COL + 1]
+    node = jnp.where(used, node, -2.0)
+    place = lax.broadcasted_iota(jnp.int32, (8, width), 1).astype(jnp.float32)
+    local_row = jnp.floor((place + 0.5) * (1.0 / broad))
+    local_col = place - local_row * broad
+
+    @pl.loop(0, n_row * n_col)
+    def _(device):
+        row = local_row + ((device // n_col) * node_rows - RELAX).astype(jnp.float32)
+        col = local_col + ((device % n_col) * NODE_LANES - RELAX).astype(jnp.float32)
+        real = (row >= 0) & (row < height) & (col >= 0) & (col < breadth) & (local_row < tall)
+        wanted = jnp.where(real, row * float(breadth) + col, -1.0)[:1]
+        chosen = jnp.where(node == wanted, 1.0, 0.0).astype(jnp.bfloat16)
+        sent = jnp.dot(terms, chosen, preferred_element_type=jnp.float32)
+        sent = sent[0:8] + sent[8:16] + sent[16:24]
+        out_ref[device] = sent[:3]
+
+
+def list_nodes(
+    capacity,
+    grid,
+    everyone_ref,
+    counting_ref,
+    fields_ref,
+    fields_turned_ref,
+    columns_ref,
+    listed_ref,
+):
+    n_row, n_col, a_rows, node_rows = grid
+    me = (lax.axis_index("row") * n_col + lax.axis_index("col")).astype(jnp.float32)
+    exact = functools.partial(lax.dot_general, preferred_element_type=jnp.float32)
+    plain = (((1,), (0,)), ((), ()))
+    turned = (((1,), (1,)), ((), ()))
+
+    def table(index, many=1):
+        return counting_ref[:, index * HALF_LANES : (index + many) * HALF_LANES]
+
+    slot = lax.broadcasted_iota(jnp.int32, (capacity, HALF_LANES), 0).astype(jnp.float32)
+    before = jnp.zeros((1, HALF_LANES), jnp.float32)
+    found = jnp.zeros((capacity, 3 * HALF_LANES), jnp.float32)
+    for block in range(n_row * n_col // 8):
+        records = everyone_ref[8 * block : 8 * block + 8, a_rows : a_rows + 16, :]
+        records = records.reshape(HALF_LANES, HALF_LANES)
+        mine = exact(records, table(0), plain) == me
+        ones = jnp.where(mine, 1.0, 0.0).astype(jnp.bfloat16)
+        counts = exact(ones, table(1, 2), plain)
+        within, loads = counts[:, :HALF_LANES], counts[:, HALF_LANES:]
+        base = exact(table(3), loads.astype(jnp.bfloat16), plain) + before
+        slots = jnp.where(mine, within + base, -1.0)
+        row_loads = exact(table(5)[:16], ones, turned)
+        row_base = exact(row_loads.astype(jnp.bfloat16), table(4), plain)[:1] + before
+        holds = (slot >= row_base) & (slot < row_base + row_loads[:1])
+        local = lax.broadcasted_iota(jnp.int32, (HALF_LANES, HALF_LANES), 0) % 16
+        mesh_row = (local + 8 * block // n_col * node_rows).astype(jnp.float32)
+        found = found + exact(
+            jnp.where(holds, 1.0, 0.0).astype(jnp.bfloat16),
+            jnp.concatenate(
+                [records, slots.astype(jnp.bfloat16), mesh_row.astype(jnp.bfloat16)], axis=1
+            ),
+            plain,
+        )
+        before = before + jnp.sum(loads, axis=0, keepdims=True)
+
+    same = found[:, HALF_LANES : 2 * HALF_LANES] == slot
+    taken = jnp.concatenate(
+        [jnp.where(same, found[:, :HALF_LANES], 0.0), found[:, 2 * HALF_LANES :]], axis=1
+    ).astype(jnp.bfloat16)
+    columns_ref[...] = exact(taken, fields_ref[...], plain)
+    rows = exact(fields_turned_ref[...], taken, turned)
+
+    def field(index):
+        return rows[index : index + 1, :]
+
+    def divide(value, by):
+        whole = jnp.floor((value + 0.5) * (1.0 / by))
+        return whole, value - whole * by
+
+    half = float(PATCH // 2)
+    b_top = jnp.maximum(16.0 * field(ROW_HIGH) + field(ROW_LOW) - half, 0.0)
+    b_left = jnp.maximum(16.0 * field(COL_HIGH) + field(COL_LOW) - half, 0.0)
+    a_top = STRIDE * field(MESH_ROW) + STRIDE // 2
+    a_left = STRIDE * field(MESH_COL) + (STRIDE // 2 + half)
+    b_group, b_row_rest = divide(b_top, 16)
+    b_block, b_col_rest = divide(b_left, PATCH)
+    a_group, a_row_rest = divide(a_top, 16)
+    a_block, a_col_rest = divide(a_left, PATCH)
+    near_row = divide(field(PEAK_ROW) + b_row_rest - a_row_rest - centre_reach, PATCH)[1]
+    near_col = divide(field(PEAK_COL) + b_col_rest - a_col_rest, PATCH)[1]
+    for index, value in (
+        (B_BLOCK, b_block),
+        (B_ROW, 16.0 * b_group),
+        (B_ROW_REST, b_row_rest),
+        (B_COL_REST, b_col_rest),
+        (A_BLOCK, a_block),
+        (A_ROW, 16.0 * a_group),
+        (A_ROW_REST, a_row_rest),
+        (A_COL_REST, a_col_rest),
+        (NEAR_ROW, near_row),
+        (NEAR_COL, near_col),
+    ):
+        listed_ref[index : index + 1, :] = value.astype(jnp.int32)
+    listed_ref[FIELDS:, :] = jnp.zeros((16 - FIELDS, capacity), jnp.int32)
+    return jnp.max(before).astype(jnp.int32)
+
+
+def correlate(capacity, everyone, tile, grid):
+    n_row, n_col, a_rows, node_rows = grid
+    tall, broad = node_rows + 2 * RELAX, NODE_LANES + 2 * RELAX
+    width = -(-tall * broad // HALF_LANES) * HALF_LANES
     a_blocks = (n_col * everyone.shape[2] + 76) // PATCH + 2
     b_blocks = -(-tile.shape[1] // PATCH)
     vmem = pl.BlockSpec(memory_space=pltpu.VMEM)
-    smem = pl.BlockSpec(memory_space=pltpu.SMEM)
     rows = pltpu.VMEM((capacity, HALF_LANES), jnp.float32)
     return pl.pallas_call(
         functools.partial(correlate_kernel, capacity, grid),
-        out_shape=jax.ShapeDtypeStruct((capacity, HALF_LANES), jnp.float32),
-        in_specs=[smem, smem] + [vmem] * 7,
+        out_shape=jax.ShapeDtypeStruct((n_row * n_col, 3, width), jnp.float32),
+        in_specs=[vmem] * 10,
         out_specs=vmem,
         scratch_shapes=[
             pltpu.VMEM((2 * BATCH * PATCH, WIDE), jnp.bfloat16),
@@ -298,9 +458,13 @@
         + [
             pltpu.VMEM((a_blocks, n_row * a_rows + PATCH, WIDE), jnp.bfloat16),
             pltpu.VMEM((b_blocks, tile.shape[0] + 16, WIDE), jnp.bfloat16),
+            rows,
+            pltpu.VMEM((16, capacity), jnp.int32),
+            pltpu.SMEM((16, capacity), jnp.int32),
+            pltpu.SemaphoreType.DMA,
         ],
         compiler_params=pltpu.CompilerParams(vmem_limit_bytes=40 * 1024 * 1024),
-    )(count, items, everyone, tile, *kernel_tables())
+    )(everyone, tile, *kernel_tables(), *listing_tables())
 
 
 def per_device(a_window, b_section, owners, pos_rows, pos_cols, peaks):
@@ -309,116 +473,37 @@
     n_row, n_col = lax.axis_size("row"), lax.axis_size("col")
     devices = n_row * n_col
     me_row, me_col = lax.axis_index("row"), lax.axis_index("col")
-    me = me_row * n_col + me_col
     share = max(2, (nodes * 8 // 5 + devices - 1) // devices)
-    capacity = share * devices
-    half_patch = PATCH // 2
     a_rows, a_cols = a_window.shape
-
-    fields = jnp.stack(
+    height, breadth = n_row * node_rows, n_col * node_cols
+
+    mesh_col = me_col * node_cols + lax.broadcasted_iota(jnp.int32, pos_rows.shape, 1)
+    records = jnp.concatenate(
         [
-            owners.reshape(nodes),
-            pos_rows.reshape(nodes) // 16,
-            pos_rows.reshape(nodes) % 16,
-            pos_cols.reshape(nodes) // 16,
-            pos_cols.reshape(nodes) % 16,
-            peaks[0].reshape(nodes),
-            peaks[1].reshape(nodes),
-            jnp.zeros((nodes,), jnp.int32),
-        ]
+            owners.reshape(node_rows, node_cols),
+            pos_rows // 16,
+            pos_rows % 16,
+            pos_cols // 16,
+            pos_cols % 16,
+            peaks[0],
+            peaks[1],
+            mesh_col,
+        ],
+        axis=1,
     ).astype(jnp.bfloat16)
-    fields = jnp.pad(fields, ((0, 0), (0, WIDE - nodes))).reshape(16, HALF_LANES)
-    sent = jnp.concatenate([a_window, fields], axis=0)
+    records = jnp.pad(records, ((0, 16 - node_rows), (0, 0)), constant_values=-1)
+    sent = jnp.concatenate([a_window, records], axis=0)
     sent = jnp.broadcast_to(sent[None], (n_col,) + sent.shape)
     sent = lax.all_to_all(sent, "col", split_axis=0, concat_axis=0, tiled=True)
-    everyone = lax.all_gather(sent, "row")
-    everyone = everyone.reshape(devices, a_rows + 16, a_cols)
-
-    known = everyone[:, a_rows:].reshape(devices, 8, WIDE)[:, :, :nodes]
-    mine = (known[:, 0] == me.astype(jnp.bfloat16)).astype(jnp.float32)
-    within = jnp.dot(
-        mine, jnp.triu(jnp.ones((nodes, nodes), jnp.float32), 1)
-    )
-    loads = jnp.sum(mine, axis=1)
-    before = jnp.sum(
-        jnp.where(jnp.tril(jnp.ones((devices, devices), bool), -1), loads[None, :], 0.0), axis=1
-    )
-    count = jnp.sum(loads).astype(jnp.int32).reshape(1)
-    slots = jnp.where(mine > 0, before[:, None] + within, -1.0).astype(jnp.int32)
-    slots = slots.reshape(devices * nodes)
-    chosen = (
-        slots[None, :] == jnp.arange(capacity, dtype=jnp.int32)[:, None]
-    ).astype(jnp.bfloat16)
-    device_of = jnp.broadcast_to(jnp.arange(devices)[:, None], (devices, nodes))
-    node_of = jnp.broadcast_to(jnp.arange(nodes)[None, :], (devices, nodes))
-    listed = jnp.concatenate(
-        [
-            known.transpose(1, 0, 2)[:7],
-            device_of[None].astype(jnp.bfloat16),
-            node_of[None].astype(jnp.bfloat16),
-        ],
-        axis=0,
-    ).reshape(9, devices * nodes)
-    taken = lax.dot_general(
-        listed, chosen, (((1,), (1,)), ((), ())), preferred_element_type=jnp.float32
-    ).astype(jnp.int32)
-    valid = jnp.arange(capacity) < count[0]
-    b_top = jnp.where(valid, taken[1] * 16 + taken[2] - half_patch, 0)
-    b_left = jnp.where(valid, taken[3] * 16 + taken[4] - half_patch, 0)
-    a_top = (taken[7] // n_col * node_rows + taken[8] // node_cols) * STRIDE + STRIDE // 2
-    a_left = (
-        (taken[7] % n_col * node_cols + taken[8] % node_cols) * STRIDE
-        + STRIDE // 2
-        + half_patch
-    )
-    near_row = (taken[5] + b_top % 16 - a_top % 16 - centre_reach + 2 * PATCH) % PATCH
-    near_col = (taken[6] + b_left % PATCH - a_left % PATCH + 2 * PATCH) % PATCH
-    items = jnp.stack(
-        [
-            b_left // PATCH,
-            b_top // 16 * 16,
-            b_top % 16,
-            b_left % PATCH,
-            a_left // PATCH,
-            a_top // 16 * 16,
-            a_top % 16,
-            a_left % PATCH,
-            near_row,
-            near_col,
-        ]
-    )
-    result = correlate(count, items, everyone, b_section, (n_row, n_col, a_rows))[:, :3]
-
-    height, breadth = n_row * node_rows, n_col * node_cols
+    everyone = lax.all_gather(sent, "row").reshape(devices, a_rows + 16, a_cols)
+
+    grid = (n_row, n_col, a_rows, node_rows)
+    spread = correlate(share * devices, everyone, b_section, grid)
+    spread = lax.all_to_all(spread, ("row", "col"), split_axis=0, concat_axis=0, tiled=True)
     tall, broad = node_rows + 2 * RELAX, node_cols + 2 * RELAX
-    lanes = -(-tall * broad // HALF_LANES) * HALF_LANES
-    shape = (devices, lanes)
-    device = lax.broadcasted_iota(jnp.int32, shape, 0)
-    place = lax.broadcasted_iota(jnp.int32, shape, 1)
-    row = device // n_col * node_rows + place // broad - RELAX
-    col = device % n_col * node_cols + place % broad - RELAX
-    real = (row >= 0) & (row < height) & (col >= 0) & (col < breadth) & (place < tall * broad)
-    wanted = jnp.where(real, row * breadth + col, -1).reshape(devices * lanes)
-    node = (taken[7] // n_col * node_rows + taken[8] // node_cols) * breadth + (
-        taken[7] % n_col * node_cols + taken[8] % node_cols
-    )
-    node = jnp.where(valid, node, -2)
-    spread = lax.dot_general(
-        result,
-        (node[:, None] == wanted[None, :]).astype(jnp.float32),
-        (((0,), (0,)), ((), ())),
-        precision=lax.Precision.HIGHEST,
-    )
-    spread = spread.reshape(3, devices, lanes).transpose(1, 0, 2)
-    spread = lax.all_to_all(spread, ("row", "col"), split_axis=0, concat_axis=0, tiled=True)
     spread = jnp.sum(spread, axis=0)[:, : tall * broad].reshape(3, tall, broad)
     runner = spread[2, RELAX:-RELAX, RELAX:-RELAX]
-    offsets = known[:, 5:7].astype(jnp.float32).reshape(n_row, n_col, 2, node_rows, node_cols)
-    offsets = offsets.transpose(2, 0, 3, 1, 4).reshape(2, height, breadth)
-    offsets = jnp.pad(offsets, ((0, 0), (RELAX, RELAX), (RELAX, RELAX)))
-    field = spread[:2] + lax.dynamic_slice(
-        offsets, (0, me_row * node_rows, me_col * node_cols), (2, tall, broad)
-    )
+    field = spread[:2]
     for step in range(RELAX):
         reach = RELAX - 1 - step
         centre = field[:, 1:-1, 1:-1]

time: 121 us -> 115 us (0.950); the launches traced: 120 us -> 115 us
  Pallas kernels: 29.3 us -> 65.8 us
  starting transfers between devices: 35.3 us -> 9.85 us
  local copies, waits for them, and re-layouts: 17.8 us -> 10.8 us
  matrix products: 6.93 us -> 0 us
  other arithmetic: 7.76 us -> 3.3 us
  waiting for transfers between devices: 12.7 us -> 16.3 us
    pallas_call x1, Pallas kernels: 29.3 us -> 65.8 us  [correlate(): pl.pallas_call(functools.partial(correlate_kernel, capacity, grid), out_s...]
    all_to_all x1, starting transfers between devices: 28 us -> 2.6 us  [per_device(): lax.all_to_all(spread, ('row', 'col'), split_axis=0, concat_axis=0, tiled...]
    unnamed x17 -> x19, local copies, waits for them, and re-layouts: 0.64 us -> 9.16 us
    dot_general x3 -> x0, matrix products: 6.93 us -> none  [the longest x1 4.29 us: per_device(): lax.dot_general(result, (node[:, None] == wanted[None, :]).astype(jnp.flo...]
    slice x8 -> x2, local copies, waits for them, and re-layouts: 4.22 us -> 0.09 us  [per_device(): field = spread[:2]]
    reshape x6 -> x0, local copies, waits for them, and re-layouts: 3.53 us -> none  [the longest x1 1.6 us: per_device(): known = everyone[:, a_rows:].reshape(devices, 8, WIDE)[:, :, :nodes]]
    another operation x8 -> x0, local copies, waits for them, and re-layouts: 2.5 us -> none  [the longest x1 1.42 us: per_device(): jnp.stack([b_left // PATCH, b_top // 16 * 16, b_top % 16, b_left % PATCH,...]
    select_n x5 -> x0, other arithmetic: 2.49 us -> none  [the longest x1 0.64 us: per_device(): (taken[5] + b_top % 16 - a_top % 16 - centre_reach + 2 * PATCH) % PATCH]
  transfers between devices with their start and end apart: 2 -> 2, of which waited for: 2 -> 2; matrix products, arithmetic and copies ran while one was open for 3% -> 0% of each run, Pallas kernels for 0% -> 0%
where the time goes in v4:
time: 115 us
  Pallas kernels  65.8 us (57%)
  waiting for transfers between devices  16.3 us (14%)
  local copies, waits for them, and re-layouts  10.8 us (9%)
  starting transfers between devices  9.85 us (9%)
  blocking collectives  8.61 us (7%)
  other arithmetic  3.3 us (3%)
    pallas_call x1, Pallas kernels, correlate(): pl.pallas_call(functools.partial(correlate_kernel, capacity, grid), out_s...  65.8 us
    unnamed x19, local copies, waits for them, and re-layouts  9.16 us
    all_gather x1, blocking collectives, per_device(): everyone = lax.all_gather(sent, 'row').reshape(devices, a_rows + 16, a_cols)  8.61 us
    all_to_all x1, waiting for transfers between devices, per_device(): lax.all_to_all(spread, ('row', 'col'), split_axis=0, concat_axis=0, tiled...  8.46 us
    all_to_all x1, waiting for transfers between devices, per_device(): sent = lax.all_to_all(sent, 'col', split_axis=0, concat_axis=0, tiled=True)  7.83 us
    all_to_all x1, starting transfers between devices, per_device(): sent = lax.all_to_all(sent, 'col', split_axis=0, concat_axis=0, tiled=True)  7.25 us
    all_to_all x1, starting transfers between devices, per_device(): lax.all_to_all(spread, ('row', 'col'), split_axis=0, concat_axis=0, tiled...  2.6 us
  transfers between devices with their start and end apart: 2, of which 2 were waited for; matrix products, arithmetic and copies ran while one was open for 0% of the time, Pallas kernels for 0%

profile of v4, /device:TPU:0, one launch (start us, length us, event | category | flops | bytes accessed | tf_op | source)
XLA Modules:
  0.0 115.4 jit_solution(7309435021541742562)
XLA Ops:
  0.6 0.7 copy_convert_fusion
  1.4 0.7 fusion.18
  2.1 0.7 fusion.11
  2.8 0.1 concatenate.7
  2.9 0.7 fusion.1
  3.6 0.7 broadcast_in_dim.38
  4.3 7.3 %all-to-all-start = ((bf16[8,96,128]{2,1,0:T(8,128)(2,1)}), bf16[8,96,128]{2,1,0:T(8,128)(2,1)S(1)}, u32[]{:S(2)}, u32[]{:S(2)}) async-start(bf16[8,96,128]{2,1,0:T(8,128)(2,1)} %broadcast_in_dim.38), calls=%async_computation | async-start | bytes 393216 | tf_op jit(solution)/shard_map/all_to_all | solution.py:497
  11.7 7.8 %all-to-all-done = bf16[8,96,128]{2,1,0:T(8,128)(2,1)S(1)} async-done(((bf16[8,96,128]{2,1,0:T(8,128)(2,1)}), bf16[8,96,128]{2,1,0:T(8,128)(2,1)S(1)}, u32[]{:S(2)}, u32[]{:S(2)}) %all-to-all-start) | async-done | bytes 196640 | tf_op jit(solution)/shard_map/all_to_all | solution.py:497
  19.5 8.6 %all-gather.everyone_ref = bf16[32,96,128]{2,1,0:T(8,128)(2,1)S(1)} all-gather(bf16[8,96,128]{2,1,0:T(8,128)(2,1)S(1)} %all-to-all-done), channel_id=2, replica_groups=mesh['row'=4,'col'=8] {'row'}, dimensions={0}, use_global_device_ids=true | all-gather | bytes 983040 | tf_op jit(solution)/shard_map/all_gather | solution.py:498
  28.2 1.6 %copy-done = bf16[1024,1024]{1,0:T(8,128)(2,1)S(1)} copy-done((bf16[1024,1024]{1,0:T(8,128)(2,1)S(1)}, bf16[1024,1024]{1,0:T(8,128)(2,1)}, u32[]{:S(2)}) %copy-start) | copy-done | bytes 2097176
  29.8 0.9 copy-done.1
  30.7 0.9 copy-done.2
  31.6 0.9 copy-done.3
  32.5 0.9 copy-done.4
  33.4 0.9 copy-done.5
  34.3 0.9 copy-done.6
  35.2 0.8 copy-done.7
  36.0 0.7 copy-done.8
  36.7 65.8 %shard_map.149 = f32[32,3,384]{2,1,0:T(4,128)} custom-call(bf16[32,96,128]{2,1,0:T(8,128)(2,1)S(1)} %all-gather.everyone_ref, bf16[1024,1024]{1,0:T(8,128)(2,1)S(1)} %copy-done, bf16[256,256]{1,0:T(8,128)(2,1)S(1)} %copy-done.3, bf16[176,160]{1,0:T(8,128)(2,1)S(1)} %copy-done.5, bf16[160,176]{1,0:T(8,128)(2,1)S(1)} %copy-done.6, ...), custom_call_target="tpu_custom_call" | custom-call | tf_op jit(solution)/shard_map/pallas_call | solution.py:443
  102.5 2.6 %all-to-all-start.1 = ((f32[32,3,384]{2,1,0:T(4,128)}), f32[32,3,384]{2,1,0:T(4,128)S(1)}, u32[]{:S(2)}, u32[]{:S(2)}) async-start(f32[32,3,384]{2,1,0:T(4,128)} %shard_map.149), calls=%async_computation.1 | async-start | bytes 393216 | tf_op jit(solution)/shard_map/all_to_all | solution.py:502
  105.2 8.5 %all-to-all-done.1 = f32[32,3,384]{2,1,0:T(4,128)S(1)} async-done(((f32[32,3,384]{2,1,0:T(4,128)}), f32[32,3,384]{2,1,0:T(4,128)S(1)}, u32[]{:S(2)}, u32[]{:S(2)}) %all-to-all-start.1) | async-done | bytes 147488 | tf_op jit(solution)/shard_map/all_to_all | solution.py:502
  113.8 0.1 fusion.9
  114.0 0.6 copy.23
  114.7 0.7 slice_bitcast_fusion
  (23 shorter events, 0.5 us)
Async XLA Ops:
  4.3 15.2 %all-to-all-start = ((bf16[8,96,128]{2,1,0:T(8,128)(2,1)}), bf16[8,96,128]{2,1,0:T(8,128)(2,1)S(1)}, u32[]{:S(2)}, u32[]{:S(2)}) async-start(bf16[8,96,128]{2,1,0:T(8,128)(2,1)} %broadcast_in_dim.38), calls=%async_computation | async-start | bytes 393216 | tf_op jit(solution)/shard_map/all_to_all | solution.py:497
  28.2 1.6 %copy-start = (bf16[1024,1024]{1,0:T(8,128)(2,1)S(1)}, bf16[1024,1024]{1,0:T(8,128)(2,1)}, u32[]{:S(2)}) copy-start(bf16[1024,1024]{1,0:T(8,128)(2,1)} %tile_ref.1) | copy-start | bytes 6291460
  29.8 0.9 copy-start.1
  30.7 0.9 copy-start.2
  31.6 0.9 copy-start.3
  32.5 0.9 copy-start.4
  33.4 0.9 copy-start.5
  34.3 0.9 copy-start.6
  35.2 0.8 copy-start.7
  36.0 0.7 copy-start.8
  102.5 11.2 %all-to-all-start.1 = ((f32[32,3,384]{2,1,0:T(4,128)}), f32[32,3,384]{2,1,0:T(4,128)S(1)}, u32[]{:S(2)}, u32[]{:S(2)}) async-start(f32[32,3,384]{2,1,0:T(4,128)} %shard_map.149), calls=%async_computation.1 | async-start | bytes 393216 | tf_op jit(solution)/shard_map/all_to_all | solution.py:502

commit v5 on v4

--- a/solution.py
+++ b/solution.py
@@ -11,6 +11,8 @@
 
 PATCH = 160
 NODE_LANES = 16
+SPREAD_LANES = 32
+SPREAD_ROWS = 16
 STRIDE = 8
 RELAX = 2
 WIDE = 256
@@ -53,17 +55,7 @@
         down[row + 8] = sine[:, freq]
         back_down[:, row] = cosine[:, freq] * weights[freq]
         back_down[:, row + 8] = sine[:, freq] * weights[freq]
-    caps = np.full((2 * PATCH, HALF_LANES), BIG, np.float32)
-    for row in range(2 * PATCH):
-        if row % PATCH <= 2 * centre_reach:
-            caps[row] = -BIG
-    return (
-        jnp.asarray(across, jnp.bfloat16),
-        jnp.asarray(down, jnp.bfloat16),
-        jnp.asarray(back_down, jnp.bfloat16),
-        jnp.asarray(back_across, jnp.bfloat16),
-        jnp.asarray(caps, jnp.float32),
-    )
+    return across, down, back_down, back_across
 
 
 def listing_tables():
@@ -73,15 +65,26 @@
     earlier = (group[:, None] == group[None]) & (place[:, None] < place[None])
     first = np.broadcast_to(lane[:, None] < NODE_LANES, (HALF_LANES, HALF_LANES))
     below = lane[None] < lane[:, None]
-    counting = np.concatenate([repeat, earlier, first, below, below.T, first.T], axis=1)
     fields = np.zeros((2 * HALF_LANES, HALF_LANES), np.float32)
     fields[lane, group] = 1.0
     fields[HALF_LANES, MESH_ROW] = 1.0
-    return (
-        jnp.asarray(counting, jnp.bfloat16),
-        jnp.asarray(fields, jnp.bfloat16),
-        jnp.asarray(fields.T[:16], jnp.bfloat16),
+    return repeat, np.concatenate([earlier, first], axis=1), below, below.T, first.T[:16], fields, (
+        fields.T[:16]
     )
+
+
+def all_tables():
+    names = ("across", "down", "back_down", "back_across", "repeat", "within")
+    names += ("below", "above", "count", "fields", "turned")
+    places, parts, start = {}, [], 0
+    for name, part in zip(names, kernel_tables() + listing_tables()):
+        rows, lanes = part.shape
+        places[name] = (start, rows, lanes)
+        rows_up = -(-rows // 16) * 16
+        parts.append(np.zeros((rows_up, WIDE), np.float32))
+        parts[-1][:rows, :lanes] = part
+        start += rows_up
+    return jnp.asarray(np.concatenate(parts), jnp.bfloat16), places
 
 
 OWNER, ROW_HIGH, ROW_LOW, COL_HIGH, COL_LOW, PEAK_ROW, PEAK_COL, MESH_COL, MESH_ROW = range(9)
@@ -104,34 +107,34 @@
 def correlate_kernel(
     capacity,
     grid,
+    places,
     everyone_ref,
     tile_ref,
-    across_ref,
-    down_ref,
-    back_down_ref,
-    back_across_ref,
-    caps_ref,
-    counting_ref,
-    fields_ref,
-    fields_turned_ref,
+    tables_ref,
     out_ref,
     *scratch,
 ):
     patches, halves, crosses, inverses = scratch[:4]
     corrs = scratch[4:6]
     energies, totals, row_moments, col_moments, runners, a_ref, b_ref = scratch[6:13]
-    columns_ref, listed_ref, items_ref, semaphore = scratch[13:]
+    columns_ref, listed_ref, items_ref, semaphore, caps_ref, rows_ref = scratch[13:]
+
+    def table(name):
+        start, rows, lanes = places[name]
+        return tables_ref[start : start + rows, :lanes]
+
     n_row, n_col, a_rows, node_rows = grid
     count = list_nodes(
         capacity,
         grid,
         everyone_ref,
-        counting_ref,
-        fields_ref,
-        fields_turned_ref,
+        table,
         columns_ref,
+        rows_ref,
         listed_ref,
     )
+    caps_row = lax.broadcasted_iota(jnp.int32, caps_ref.shape, 0) % PATCH
+    caps_ref[...] = jnp.where(caps_row <= 2 * centre_reach, -BIG, BIG)
     to_scalars = pltpu.make_async_copy(listed_ref, items_ref, semaphore)
     to_scalars.start()
 
@@ -192,7 +195,7 @@
                 energies[item % RING, which] = extract(
                     source, block, row, row_rest, col_rest, (2 * part + which) * PATCH
                 )
-        half = jnp.dot(patches[...], across_ref[...], preferred_element_type=jnp.float32)
+        half = jnp.dot(patches[...], table("across"), preferred_element_type=jnp.float32)
         halves[...] = half.astype(jnp.bfloat16)
 
     def sides(spec, group):
@@ -203,7 +206,7 @@
         return cc - ss, sc + cs, cc + ss, sc - cs
 
     def stage_inverse():
-        down = down_ref[...]
+        down = table("down")
         for part in range(BATCH):
             base = 2 * part * PATCH
             spec_a = jnp.dot(
@@ -227,13 +230,13 @@
                 ).astype(jnp.bfloat16)
         for part in range(BATCH):
             inverse = jnp.dot(
-                back_down_ref[...], crosses[part], preferred_element_type=jnp.float32
+                table("back_down"), crosses[part], preferred_element_type=jnp.float32
             )
             inverses[PATCH * part : PATCH * (part + 1), :] = inverse.astype(jnp.bfloat16)
 
     def stage_score(step):
         corr_all = jnp.dot(
-            inverses[...], back_across_ref[...], preferred_element_type=jnp.float32
+            inverses[...], table("back_across"), preferred_element_type=jnp.float32
         )
         rows = lax.broadcasted_iota(jnp.int32, (8, HALF_LANES), 0)
         lanes = lax.broadcasted_iota(jnp.int32, (8, HALF_LANES), 1)
@@ -307,52 +310,41 @@
         jnp.maximum(jnp.max(runners[...], axis=1, keepdims=True), -2.0),
     )
     lanes = lax.broadcasted_iota(jnp.int32, (capacity, HALF_LANES), 1)
-    terms = jnp.zeros((capacity, HALF_LANES), jnp.float32)
+    terms = [jnp.zeros((capacity, HALF_LANES), jnp.float32)] * 3
     for value, rest in enumerate(results):
         rest = jnp.where(used, rest, 0.0)
         for term in range(3):
             here = rest.astype(jnp.bfloat16).astype(jnp.float32)
-            terms = jnp.where(lanes == 8 * term + value, here, terms)
+            terms[term] = jnp.where(lanes // SPREAD_LANES == value, here, terms[term])
             rest = rest - here
-    square = (32, HALF_LANES)
-    pick = lax.broadcasted_iota(jnp.int32, square, 0) == lax.broadcasted_iota(jnp.int32, square, 1)
-    terms = lax.dot_general(
-        jnp.where(pick, 1.0, 0.0).astype(jnp.bfloat16),
-        terms.astype(jnp.bfloat16),
-        (((1,), (1,)), ((), ())),
-        preferred_element_type=jnp.float32,
-    ).astype(jnp.bfloat16)
-
-    height, breadth = n_row * node_rows, n_col * NODE_LANES
-    tall, broad = node_rows + 2 * RELAX, NODE_LANES + 2 * RELAX
-    width = out_ref.shape[2]
-    node = columns_ref[:, MESH_ROW : MESH_ROW + 1] * float(breadth)
-    node = node + columns_ref[:, MESH_COL : MESH_COL + 1]
-    node = jnp.where(used, node, -2.0)
-    place = lax.broadcasted_iota(jnp.int32, (8, width), 1).astype(jnp.float32)
-    local_row = jnp.floor((place + 0.5) * (1.0 / broad))
-    local_col = place - local_row * broad
-
-    @pl.loop(0, n_row * n_col)
-    def _(device):
-        row = local_row + ((device // n_col) * node_rows - RELAX).astype(jnp.float32)
-        col = local_col + ((device % n_col) * NODE_LANES - RELAX).astype(jnp.float32)
-        real = (row >= 0) & (row < height) & (col >= 0) & (col < breadth) & (local_row < tall)
-        wanted = jnp.where(real, row * float(breadth) + col, -1.0)[:1]
-        chosen = jnp.where(node == wanted, 1.0, 0.0).astype(jnp.bfloat16)
-        sent = jnp.dot(terms, chosen, preferred_element_type=jnp.float32)
-        sent = sent[0:8] + sent[8:16] + sent[16:24]
-        out_ref[device] = sent[:3]
+    slot_row = rows_ref[MESH_ROW : MESH_ROW + 1, :]
+    slot_col = columns_ref[:, MESH_COL : MESH_COL + 1]
+    offset = (lanes % SPREAD_LANES - RELAX).astype(jnp.float32)
+    shape = (n_row * SPREAD_ROWS, capacity)
+    place = lax.broadcasted_iota(jnp.int32, shape, 0)
+    row = place // SPREAD_ROWS * node_rows + place % SPREAD_ROWS - RELAX
+    rows_picked = jnp.where(slot_row == row.astype(jnp.float32), 1.0, 0.0).astype(jnp.bfloat16)
+    for col in range(n_col):
+        here = slot_col == offset + float(col * NODE_LANES)
+        sent = sum(
+            jnp.dot(
+                rows_picked,
+                jnp.where(here, term, 0.0).astype(jnp.bfloat16),
+                preferred_element_type=jnp.float32,
+            )
+            for term in terms
+        )
+        for row in range(n_row):
+            out_ref[row * n_col + col] = sent[SPREAD_ROWS * row : SPREAD_ROWS * (row + 1)]
 
 
 def list_nodes(
     capacity,
     grid,
     everyone_ref,
-    counting_ref,
-    fields_ref,
-    fields_turned_ref,
+    table,
     columns_ref,
+    rows_ref,
     listed_ref,
 ):
     n_row, n_col, a_rows, node_rows = grid
@@ -361,23 +353,20 @@
     plain = (((1,), (0,)), ((), ()))
     turned = (((1,), (1,)), ((), ()))
 
-    def table(index, many=1):
-        return counting_ref[:, index * HALF_LANES : (index + many) * HALF_LANES]
-
     slot = lax.broadcasted_iota(jnp.int32, (capacity, HALF_LANES), 0).astype(jnp.float32)
     before = jnp.zeros((1, HALF_LANES), jnp.float32)
     found = jnp.zeros((capacity, 3 * HALF_LANES), jnp.float32)
     for block in range(n_row * n_col // 8):
         records = everyone_ref[8 * block : 8 * block + 8, a_rows : a_rows + 16, :]
         records = records.reshape(HALF_LANES, HALF_LANES)
-        mine = exact(records, table(0), plain) == me
+        mine = exact(records, table("repeat"), plain) == me
         ones = jnp.where(mine, 1.0, 0.0).astype(jnp.bfloat16)
-        counts = exact(ones, table(1, 2), plain)
+        counts = exact(ones, table("within"), plain)
         within, loads = counts[:, :HALF_LANES], counts[:, HALF_LANES:]
-        base = exact(table(3), loads.astype(jnp.bfloat16), plain) + before
+        base = exact(table("below"), loads.astype(jnp.bfloat16), plain) + before
         slots = jnp.where(mine, within + base, -1.0)
-        row_loads = exact(table(5)[:16], ones, turned)
-        row_base = exact(row_loads.astype(jnp.bfloat16), table(4), plain)[:1] + before
+        row_loads = exact(table("count"), ones, turned)
+        row_base = exact(row_loads.astype(jnp.bfloat16), table("above"), plain)[:1] + before
         holds = (slot >= row_base) & (slot < row_base + row_loads[:1])
         local = lax.broadcasted_iota(jnp.int32, (HALF_LANES, HALF_LANES), 0) % 16
         mesh_row = (local + 8 * block // n_col * node_rows).astype(jnp.float32)
@@ -394,8 +383,9 @@
     taken = jnp.concatenate(
         [jnp.where(same, found[:, :HALF_LANES], 0.0), found[:, 2 * HALF_LANES :]], axis=1
     ).astype(jnp.bfloat16)
-    columns_ref[...] = exact(taken, fields_ref[...], plain)
-    rows = exact(fields_turned_ref[...], taken, turned)
+    columns_ref[...] = exact(taken, table("fields"), plain)
+    rows = exact(table("turned"), taken, turned)
+    rows_ref[...] = rows
 
     def field(index):
         return rows[index : index + 1, :]
@@ -434,16 +424,17 @@
 
 def correlate(capacity, everyone, tile, grid):
     n_row, n_col, a_rows, node_rows = grid
-    tall, broad = node_rows + 2 * RELAX, NODE_LANES + 2 * RELAX
-    width = -(-tall * broad // HALF_LANES) * HALF_LANES
+    tables, places = all_tables()
     a_blocks = (n_col * everyone.shape[2] + 76) // PATCH + 2
     b_blocks = -(-tile.shape[1] // PATCH)
     vmem = pl.BlockSpec(memory_space=pltpu.VMEM)
     rows = pltpu.VMEM((capacity, HALF_LANES), jnp.float32)
     return pl.pallas_call(
-        functools.partial(correlate_kernel, capacity, grid),
-        out_shape=jax.ShapeDtypeStruct((n_row * n_col, 3, width), jnp.float32),
-        in_specs=[vmem] * 10,
+        functools.partial(correlate_kernel, capacity, grid, places),
+        out_shape=jax.ShapeDtypeStruct(
+            (n_row * n_col, SPREAD_ROWS, HALF_LANES), jnp.float32
+        ),
+        in_specs=[vmem] * 3,
         out_specs=vmem,
         scratch_shapes=[
             pltpu.VMEM((2 * BATCH * PATCH, WIDE), jnp.bfloat16),
@@ -462,9 +453,11 @@
             pltpu.VMEM((16, capacity), jnp.int32),
             pltpu.SMEM((16, capacity), jnp.int32),
             pltpu.SemaphoreType.DMA,
+            pltpu.VMEM((2 * PATCH, HALF_LANES), jnp.float32),
+            pltpu.VMEM((16, capacity), jnp.float32),
         ],
         compiler_params=pltpu.CompilerParams(vmem_limit_bytes=40 * 1024 * 1024),
-    )(everyone, tile, *kernel_tables(), *listing_tables())
+    )(everyone, tile, tables)
 
 
 def per_device(a_window, b_section, owners, pos_rows, pos_cols, peaks):
@@ -501,9 +494,10 @@
     spread = correlate(share * devices, everyone, b_section, grid)
     spread = lax.all_to_all(spread, ("row", "col"), split_axis=0, concat_axis=0, tiled=True)
     tall, broad = node_rows + 2 * RELAX, node_cols + 2 * RELAX
-    spread = jnp.sum(spread, axis=0)[:, : tall * broad].reshape(3, tall, broad)
-    runner = spread[2, RELAX:-RELAX, RELAX:-RELAX]
-    field = spread[:2]
+    spread = jnp.sum(spread, axis=0)[:tall]
+    spread = [spread[:, SPREAD_LANES * value :][:, :broad] for value in range(3)]
+    runner = spread[2][RELAX:-RELAX, RELAX:-RELAX]
+    field = jnp.stack(spread[:2])
     for step in range(RELAX):
         reach = RELAX - 1 - step
         centre = field[:, 1:-1, 1:-1]

time: 115 us -> 103 us (0.90)
  Pallas kernels: 65.8 us -> 58.3 us
  local copies, waits for them, and re-layouts: 10.8 us -> 3.75 us
  waiting for transfers between devices: 16.3 us -> 18.4 us
    pallas_call x1, Pallas kernels: 65.8 us -> 58.3 us  [correlate(): pl.pallas_call(functools.partial(correlate_kernel, capacity, grid, places...]
    unnamed x19 -> x5, local copies, waits for them, and re-layouts: 9.16 us -> 2.2 us
    all_to_all x1, waiting for transfers between devices: 8.46 us -> 10.5 us  [per_device(): lax.all_to_all(spread, ('row', 'col'), split_axis=0, concat_axis=0, tiled...]
where the time goes in v5:
time: 103 us
  Pallas kernels  58.3 us (57%)
  waiting for transfers between devices  18.4 us (18%)
  starting transfers between devices  9.85 us (10%)
  blocking collectives  8.61 us (8%)
  local copies, waits for them, and re-layouts  3.75 us (4%)
  other arithmetic  3.35 us (3%)
    pallas_call x1, Pallas kernels, correlate(): pl.pallas_call(functools.partial(correlate_kernel, capacity, grid, places...  58.3 us
    all_to_all x1, waiting for transfers between devices, per_device(): lax.all_to_all(spread, ('row', 'col'), split_axis=0, concat_axis=0, tiled...  10.5 us
    all_gather x1, blocking collectives, per_device(): everyone = lax.all_gather(sent, 'row').reshape(devices, a_rows + 16, a_cols)  8.61 us
    all_to_all x1, waiting for transfers between devices, per_device(): sent = lax.all_to_all(sent, 'col', split_axis=0, concat_axis=0, tiled=True)  7.91 us
    all_to_all x1, starting transfers between devices, per_device(): sent = lax.all_to_all(sent, 'col', split_axis=0, concat_axis=0, tiled=True)  7.25 us
    all_to_all x1, starting transfers between devices, per_device(): lax.all_to_all(spread, ('row', 'col'), split_axis=0, concat_axis=0, tiled...  2.6 us
    unnamed x5, local copies, waits for them, and re-layouts  2.2 us
  transfers between devices with their start and end apart: 2, of which 2 were waited for; matrix products, arithmetic and copies ran while one was open for 0% of the time, Pallas kernels for 0%

profile of v5, /device:TPU:0, one launch (start us, length us, event | category | flops | bytes accessed | tf_op | source)
XLA Modules:
  0.0 103.0 jit_solution(18313615882041174842)
XLA Ops:
  0.6 0.0 copy-start.1
  0.7 0.8 copy_convert_fusion
  1.4 0.7 fusion.25
  2.1 0.7 fusion.18
  2.9 0.1 concatenate.7
  3.0 0.7 fusion.1
  3.7 0.7 broadcast_in_dim.38
  4.4 7.3 %all-to-all-start = ((bf16[8,96,128]{2,1,0:T(8,128)(2,1)}), bf16[8,96,128]{2,1,0:T(8,128)(2,1)S(1)}, u32[]{:S(2)}, u32[]{:S(2)}) async-start(bf16[8,96,128]{2,1,0:T(8,128)(2,1)} %broadcast_in_dim.38), calls=%async_computation | async-start | bytes 393216 | tf_op jit(solution)/shard_map/all_to_all | solution.py:490
  11.7 7.9 %all-to-all-done = bf16[8,96,128]{2,1,0:T(8,128)(2,1)S(1)} async-done(((bf16[8,96,128]{2,1,0:T(8,128)(2,1)}), bf16[8,96,128]{2,1,0:T(8,128)(2,1)S(1)}, u32[]{:S(2)}, u32[]{:S(2)}) %all-to-all-start) | async-done | bytes 196640 | tf_op jit(solution)/shard_map/all_to_all | solution.py:490
  19.6 8.6 %all-gather.everyone_ref = bf16[32,96,128]{2,1,0:T(8,128)(2,1)S(1)} all-gather(bf16[8,96,128]{2,1,0:T(8,128)(2,1)S(1)} %all-to-all-done), channel_id=2, replica_groups=mesh['row'=4,'col'=8] {'row'}, dimensions={0}, use_global_device_ids=true | all-gather | bytes 983040 | tf_op jit(solution)/shard_map/all_gather | solution.py:491
  28.2 0.0 copy-done.1
  28.2 0.0 copy-start
  28.2 1.6 %copy-done = bf16[1024,1024]{1,0:T(8,128)(2,1)S(1)} copy-done((bf16[1024,1024]{1,0:T(8,128)(2,1)S(1)}, bf16[1024,1024]{1,0:T(8,128)(2,1)}, u32[]{:S(2)}) %copy-start) | copy-done | bytes 2097176
  29.8 58.3 %shard_map.86 = f32[32,16,128]{2,1,0:T(8,128)} custom-call(bf16[32,96,128]{2,1,0:T(8,128)(2,1)S(1)} %all-gather.everyone_ref, bf16[1024,1024]{1,0:T(8,128)(2,1)S(1)} %copy-done, bf16[1648,256]{1,0:T(8,128)(2,1)S(1)} %copy-done.1), custom_call_target="tpu_custom_call" | custom-call | tf_op jit(solution)/shard_map/pallas_call | solution.py:432
  88.2 2.6 %all-to-all-start.1 = ((f32[32,16,128]{2,1,0:T(8,128)}), f32[32,16,128]{2,1,0:T(8,128)S(1)}, u32[]{:S(2)}, u32[]{:S(2)}) async-start(f32[32,16,128]{2,1,0:T(8,128)} %shard_map.86), calls=%async_computation.1 | async-start | bytes 524288 | tf_op jit(solution)/shard_map/all_to_all | solution.py:495
  90.8 0.1 broadcast_and_fusion
  90.9 0.1 broadcast_and_fusion.1
  91.0 10.5 %all-to-all-done.1 = f32[32,16,128]{2,1,0:T(8,128)S(1)} async-done(((f32[32,16,128]{2,1,0:T(8,128)}), f32[32,16,128]{2,1,0:T(8,128)S(1)}, u32[]{:S(2)}, u32[]{:S(2)}) %all-to-all-start.1) | async-done | bytes 262176 | tf_op jit(solution)/shard_map/all_to_all | solution.py:495
  101.5 0.1 slice_bitcast_fusion
  101.6 0.7 slice.89
  102.2 0.1 fusion.8
  102.3 0.1 fusion.16
  102.4 0.6 copy.17
  (8 shorter events, 0.1 us)
Async XLA Ops:
  0.6 27.6 %copy-start.1 = (bf16[1648,256]{1,0:T(8,128)(2,1)S(1)}, bf16[1648,256]{1,0:T(8,128)(2,1)}, u32[]{:S(2)}) copy-start(bf16[1648,256]{1,0:T(8,128)(2,1)} %constant.76.clone.tables_ref) | copy-start | bytes 2531332
  4.4 15.2 %all-to-all-start = ((bf16[8,96,128]{2,1,0:T(8,128)(2,1)}), bf16[8,96,128]{2,1,0:T(8,128)(2,1)S(1)}, u32[]{:S(2)}, u32[]{:S(2)}) async-start(bf16[8,96,128]{2,1,0:T(8,128)(2,1)} %broadcast_in_dim.38), calls=%async_computation | async-start | bytes 393216 | tf_op jit(solution)/shard_map/all_to_all | solution.py:490
  28.2 1.6 %copy-start = (bf16[1024,1024]{1,0:T(8,128)(2,1)S(1)}, bf16[1024,1024]{1,0:T(8,128)(2,1)}, u32[]{:S(2)}) copy-start(bf16[1024,1024]{1,0:T(8,128)(2,1)} %tile_ref.1) | copy-start | bytes 6291460
  88.2 13.3 %all-to-all-start.1 = ((f32[32,16,128]{2,1,0:T(8,128)}), f32[32,16,128]{2,1,0:T(8,128)S(1)}, u32[]{:S(2)}, u32[]{:S(2)}) async-start(f32[32,16,128]{2,1,0:T(8,128)} %shard_map.86), calls=%async_computation.1 | async-start | bytes 524288 | tf_op jit(solution)/shard_map/all_to_all | solution.py:495

commit v6 on v5

--- a/solution.py
+++ b/solution.py
@@ -11,7 +11,7 @@
 
 PATCH = 160
 NODE_LANES = 16
-SPREAD_LANES = 32
+SPREAD_LANES = 20
 SPREAD_ROWS = 16
 STRIDE = 8
 RELAX = 2
@@ -92,8 +92,11 @@
 A_BLOCK, A_ROW, A_ROW_REST, A_COL_REST = 4, 5, 6, 7
 NEAR_ROW, NEAR_COL = 8, 9
 FIELDS = 10
-BATCH = 4
-RING = 16
+BATCH = 6
+RING = 32
+TRIO = 3
+SECOND = FREQS
+THIRD = 2 * FREQS - HALF_LANES
 
 
 def cut(strip, start):
@@ -109,7 +112,7 @@
     grid,
     places,
     everyone_ref,
-    tile_ref,
+    blocks_ref,
     tables_ref,
     out_ref,
     *scratch,
@@ -117,7 +120,9 @@
     patches, halves, crosses, inverses = scratch[:4]
     corrs = scratch[4:6]
     energies, totals, row_moments, col_moments, runners, a_ref, b_ref = scratch[6:13]
-    columns_ref, listed_ref, items_ref, semaphore, caps_ref, rows_ref = scratch[13:]
+    columns_ref, listed_ref, items_ref, semaphores, caps_ref, rows_ref = scratch[13:]
+    to_blocks = pltpu.make_async_copy(blocks_ref, b_ref, semaphores.at[0])
+    to_blocks.start()
 
     def table(name):
         start, rows, lanes = places[name]
@@ -135,19 +140,9 @@
     )
     caps_row = lax.broadcasted_iota(jnp.int32, caps_ref.shape, 0) % PATCH
     caps_ref[...] = jnp.where(caps_row <= 2 * centre_reach, -BIG, BIG)
-    to_scalars = pltpu.make_async_copy(listed_ref, items_ref, semaphore)
+    to_scalars = pltpu.make_async_copy(listed_ref, items_ref, semaphores.at[1])
     to_scalars.start()
 
-    height = tile_ref.shape[0]
-
-    @pl.loop(0, height // 128)
-    def _(chunk):
-        place = pl.ds(pl.multiple_of(chunk * 128, 128), 128)
-        strip = tile_ref[place, :]
-        for block in range(b_ref.shape[0]):
-            b_ref[block, place, :] = cut(strip, block * PATCH)
-
-    b_ref[:, height:, :] = jnp.zeros((b_ref.shape[0], 16, WIDE), jnp.bfloat16)
     a_ref[0] = jnp.zeros(a_ref.shape[1:], jnp.bfloat16)
     rim = jnp.zeros((a_ref.shape[0], PATCH // 2, WIDE), jnp.bfloat16)
     a_ref[:, : PATCH // 2, :] = rim
@@ -184,6 +179,10 @@
             total = total + (values[:8] + values[8:])
         return total[:, :HALF_LANES] + total[:, HALF_LANES:]
 
+    def patch_base(part, which):
+        trio, place = divmod(part, TRIO)
+        return ((2 * trio + which) * TRIO + place) * PATCH
+
     def stage_half(step):
         for part in range(BATCH):
             item = at(step, 0, part)
@@ -193,10 +192,25 @@
             ):
                 block, row, row_rest, col_rest = (items_ref[field, item] for field in fields)
                 energies[item % RING, which] = extract(
-                    source, block, row, row_rest, col_rest, (2 * part + which) * PATCH
+                    source, block, row, row_rest, col_rest, patch_base(part, which)
                 )
         half = jnp.dot(patches[...], table("across"), preferred_element_type=jnp.float32)
-        halves[...] = half.astype(jnp.bfloat16)
+        lanes = lax.broadcasted_iota(jnp.int32, (PATCH, HALF_LANES), 1)
+        for trio in range(BATCH // TRIO):
+            for which in range(2):
+                for side in (slice(0, HALF_LANES), slice(HALF_LANES, WIDE)):
+                    first, second, third = (
+                        half[base : base + PATCH, side]
+                        for base in (patch_base(TRIO * trio + n, which) for n in range(TRIO))
+                    )
+                    second = pltpu.roll(second, SECOND, axis=1)
+                    third = pltpu.roll(third, THIRD, axis=1)
+                    halves[trio, which, 0, :, side] = jnp.where(
+                        lanes < SECOND, first, second
+                    ).astype(jnp.bfloat16)
+                    halves[trio, which, 1, :, side] = jnp.where(
+                        lanes < THIRD, second, third
+                    ).astype(jnp.bfloat16)
 
     def sides(spec, group):
         cc = spec[16 * group : 16 * group + 8, :HALF_LANES]
@@ -207,15 +221,10 @@
 
     def stage_inverse():
         down = table("down")
-        for part in range(BATCH):
-            base = 2 * part * PATCH
-            spec_a = jnp.dot(
-                down, halves[base : base + PATCH, :], preferred_element_type=jnp.float32
-            )
-            base = base + PATCH
-            spec_b = jnp.dot(
-                down, halves[base : base + PATCH, :], preferred_element_type=jnp.float32
-            )
+        for pair in range(2 * (BATCH // TRIO)):
+            trio, tile = divmod(pair, 2)
+            spec_a = jnp.dot(down, halves[trio, 0, tile], preferred_element_type=jnp.float32)
+            spec_b = jnp.dot(down, halves[trio, 1, tile], preferred_element_type=jnp.float32)
             for group in range(GROUPS):
                 a_pr, a_pi, a_mr, a_mi = sides(spec_a, group)
                 b_pr, b_pi, b_mr, b_mi = sides(spec_b, group)
@@ -225,14 +234,25 @@
                 mi = a_mr * b_mi - a_mi * b_mr
                 upper = jnp.concatenate([pr + mr, pi - mi], axis=1)
                 lower = jnp.concatenate([pi + mi, mr - pr], axis=1)
-                crosses[part, 16 * group : 16 * group + 16, :] = jnp.concatenate(
+                crosses[pair, 16 * group : 16 * group + 16, :] = jnp.concatenate(
                     [upper, lower], axis=0
                 ).astype(jnp.bfloat16)
-        for part in range(BATCH):
-            inverse = jnp.dot(
-                table("back_down"), crosses[part], preferred_element_type=jnp.float32
+        lanes = lax.broadcasted_iota(jnp.int32, (PATCH, HALF_LANES), 1)
+        for trio in range(BATCH // TRIO):
+            low, high = (
+                jnp.dot(
+                    table("back_down"), crosses[2 * trio + tile], preferred_element_type=jnp.float32
+                )
+                for tile in range(2)
             )
-            inverses[PATCH * part : PATCH * (part + 1), :] = inverse.astype(jnp.bfloat16)
+            for side in (slice(0, HALF_LANES), slice(HALF_LANES, WIDE)):
+                first = low[:, side]
+                second = jnp.where(lanes >= SECOND, first, high[:, side])
+                second = pltpu.roll(second, HALF_LANES - SECOND, axis=1)
+                third = pltpu.roll(high[:, side], HALF_LANES - THIRD, axis=1)
+                for place, inverse in enumerate((first, second, third)):
+                    base = (TRIO * trio + place) * PATCH
+                    inverses[base : base + PATCH, side] = inverse.astype(jnp.bfloat16)
 
     def stage_score(step):
         corr_all = jnp.dot(
@@ -293,6 +313,7 @@
             runners[pl.ds(item, 1), :] = jnp.max(best * scale, axis=0, keepdims=True)
 
     to_scalars.wait()
+    to_blocks.wait()
 
     @pl.loop(0, (count + BATCH - 1) // BATCH + 2)
     def _(step):
@@ -335,7 +356,11 @@
             for term in terms
         )
         for row in range(n_row):
-            out_ref[row * n_col + col] = sent[SPREAD_ROWS * row : SPREAD_ROWS * (row + 1)]
+            block = sent[SPREAD_ROWS * row : SPREAD_ROWS * (row + 1)]
+            turned = pltpu.roll(block[8:], HALF_LANES // 2, axis=1)
+            out_ref[row * n_col + col] = jnp.where(
+                lanes[:8] < HALF_LANES // 2, block[:8], turned
+            )
 
 
 def list_nodes(
@@ -422,24 +447,44 @@
     return jnp.max(before).astype(jnp.int32)
 
 
-def correlate(capacity, everyone, tile, grid):
+def cut_kernel(tile_ref, out_ref):
+    strip = tile_ref[...]
+    for block in range(out_ref.shape[0]):
+        out_ref[block] = cut(strip, block * PATCH)
+
+
+def cut_tile(tile):
+    rows, cols = tile.shape
+    blocks = -(-cols // PATCH)
+    return pl.pallas_call(
+        cut_kernel,
+        grid=(rows // HALF_LANES,),
+        out_shape=jax.ShapeDtypeStruct((blocks, rows + 16, WIDE), jnp.bfloat16),
+        in_specs=[pl.BlockSpec((HALF_LANES, cols), lambda step: (step, 0))],
+        out_specs=pl.BlockSpec((blocks, HALF_LANES, WIDE), lambda step: (0, step, 0)),
+        cost_estimate=pl.CostEstimate(
+            flops=0, bytes_accessed=2 * rows * (cols + blocks * WIDE), transcendentals=0
+        ),
+    )(tile)
+
+
+def correlate(capacity, everyone, blocks, grid):
     n_row, n_col, a_rows, node_rows = grid
     tables, places = all_tables()
     a_blocks = (n_col * everyone.shape[2] + 76) // PATCH + 2
-    b_blocks = -(-tile.shape[1] // PATCH)
     vmem = pl.BlockSpec(memory_space=pltpu.VMEM)
     rows = pltpu.VMEM((capacity, HALF_LANES), jnp.float32)
     return pl.pallas_call(
         functools.partial(correlate_kernel, capacity, grid, places),
         out_shape=jax.ShapeDtypeStruct(
-            (n_row * n_col, SPREAD_ROWS, HALF_LANES), jnp.float32
+            (n_row * n_col, SPREAD_ROWS // 2, HALF_LANES), jnp.float32
         ),
-        in_specs=[vmem] * 3,
+        in_specs=[vmem, pl.BlockSpec(memory_space=pl.ANY), vmem],
         out_specs=vmem,
         scratch_shapes=[
             pltpu.VMEM((2 * BATCH * PATCH, WIDE), jnp.bfloat16),
-            pltpu.VMEM((2 * BATCH * PATCH, WIDE), jnp.bfloat16),
-            pltpu.VMEM((BATCH, PAIRED, WIDE), jnp.bfloat16),
+            pltpu.VMEM((BATCH // TRIO, 2, 2, PATCH, WIDE), jnp.bfloat16),
+            pltpu.VMEM((BATCH // TRIO * 2, PAIRED, WIDE), jnp.bfloat16),
             pltpu.VMEM((BATCH * PATCH, WIDE), jnp.bfloat16),
             pltpu.VMEM((BATCH, PATCH + 8, HALF_LANES), jnp.float32),
             pltpu.VMEM((BATCH, PATCH + 8, HALF_LANES), jnp.float32),
@@ -448,16 +493,16 @@
         + [rows] * 4
         + [
             pltpu.VMEM((a_blocks, n_row * a_rows + PATCH, WIDE), jnp.bfloat16),
-            pltpu.VMEM((b_blocks, tile.shape[0] + 16, WIDE), jnp.bfloat16),
+            pltpu.VMEM(blocks.shape, jnp.bfloat16),
             rows,
             pltpu.VMEM((16, capacity), jnp.int32),
             pltpu.SMEM((16, capacity), jnp.int32),
-            pltpu.SemaphoreType.DMA,
+            pltpu.SemaphoreType.DMA((2,)),
             pltpu.VMEM((2 * PATCH, HALF_LANES), jnp.float32),
             pltpu.VMEM((16, capacity), jnp.float32),
         ],
         compiler_params=pltpu.CompilerParams(vmem_limit_bytes=40 * 1024 * 1024),
-    )(everyone, tile, tables)
+    )(everyone, blocks, tables)
 
 
 def per_device(a_window, b_section, owners, pos_rows, pos_cols, peaks):
@@ -491,10 +536,12 @@
     everyone = lax.all_gather(sent, "row").reshape(devices, a_rows + 16, a_cols)
 
     grid = (n_row, n_col, a_rows, node_rows)
-    spread = correlate(share * devices, everyone, b_section, grid)
+    spread = correlate(share * devices, everyone, cut_tile(b_section), grid)
     spread = lax.all_to_all(spread, ("row", "col"), split_axis=0, concat_axis=0, tiled=True)
     tall, broad = node_rows + 2 * RELAX, node_cols + 2 * RELAX
-    spread = jnp.sum(spread, axis=0)[:tall]
+    spread = jnp.sum(spread, axis=0)
+    half_lanes = HALF_LANES // 2
+    spread = jnp.concatenate([spread[:, :half_lanes], spread[:, half_lanes:]], axis=0)[:tall]
     spread = [spread[:, SPREAD_LANES * value :][:, :broad] for value in range(3)]
     runner = spread[2][RELAX:-RELAX, RELAX:-RELAX]
     field = jnp.stack(spread[:2])

time: 103 us -> 98.8 us (0.959)
  waiting for transfers between devices: 18.4 us -> 9.08 us
  Pallas kernels: 58.3 us -> 61 us
  starting transfers between devices: 9.85 us -> 10.9 us
    all_to_all x1, waiting for transfers between devices: 7.91 us -> 1.43 us  [per_device(): sent = lax.all_to_all(sent, 'col', split_axis=0, concat_axis=0, tiled=True)]
    pallas_call x0 -> x1, Pallas kernels: none -> 6.41 us  [cut_tile(): pl.pallas_call(cut_kernel, grid=(rows // HALF_LANES,), out_shape=jax.Shap...]
    pallas_call x1, Pallas kernels: 58.3 us -> 54.6 us  [correlate(): pl.pallas_call(functools.partial(correlate_kernel, capacity, grid, places...]
    all_to_all x1, waiting for transfers between devices: 10.5 us -> 7.65 us  [per_device(): lax.all_to_all(spread, ('row', 'col'), split_axis=0, concat_axis=0, tiled...]
    all_to_all x1, starting transfers between devices: 2.6 us -> 3.67 us  [per_device(): lax.all_to_all(spread, ('row', 'col'), split_axis=0, concat_axis=0, tiled...]
  transfers between devices with their start and end apart: 2 -> 2, of which waited for: 2 -> 2; matrix products, arithmetic and copies ran while one was open for 0% -> 0% of each run, Pallas kernels for 0% -> 7%
where the time goes in v6:
time: 98.8 us; the launch traced here: 97.9 us
  Pallas kernels  61 us (62%)
  starting transfers between devices  10.9 us (11%)
  waiting for transfers between devices  9.08 us (9%)
  blocking collectives  8.61 us (9%)
  other arithmetic  4.02 us (4%)
  local copies, waits for them, and re-layouts  3.54 us (4%)
    pallas_call x1, Pallas kernels, correlate(): pl.pallas_call(functools.partial(correlate_kernel, capacity, grid, places...  54.6 us
    all_gather x1, blocking collectives, per_device(): everyone = lax.all_gather(sent, 'row').reshape(devices, a_rows + 16, a_cols)  8.61 us
    all_to_all x1, waiting for transfers between devices, per_device(): lax.all_to_all(spread, ('row', 'col'), split_axis=0, concat_axis=0, tiled...  7.65 us
    all_to_all x1, starting transfers between devices, per_device(): sent = lax.all_to_all(sent, 'col', split_axis=0, concat_axis=0, tiled=True)  7.25 us
    pallas_call x1, Pallas kernels, cut_tile(): pl.pallas_call(cut_kernel, grid=(rows // HALF_LANES,), out_shape=jax.Shap...  6.41 us
    all_to_all x1, starting transfers between devices, per_device(): lax.all_to_all(spread, ('row', 'col'), split_axis=0, concat_axis=0, tiled...  3.67 us
    unnamed x5, local copies, waits for them, and re-layouts  2.66 us
  transfers between devices with their start and end apart: 2, of which 2 were waited for; matrix products, arithmetic and copies ran while one was open for 0% of the time, Pallas kernels for 7%

profile of v6, /device:TPU:0, one launch (start us, length us, event | category | flops | bytes accessed | tf_op | source)
XLA Modules:
  0.0 97.9 jit_solution(6986750177454162438)
XLA Ops:
  0.6 0.7 copy_convert_fusion
  1.4 0.7 fusion.29
  2.1 0.7 fusion.22
  2.8 0.1 concatenate.10
  2.9 0.7 fusion.1
  3.6 0.0 copy-start.1
  3.6 0.7 broadcast_in_dim.38
  4.3 7.3 %all-to-all-start = ((bf16[8,96,128]{2,1,0:T(8,128)(2,1)}), bf16[8,96,128]{2,1,0:T(8,128)(2,1)S(1)}, u32[]{:S(2)}, u32[]{:S(2)}) async-start(bf16[8,96,128]{2,1,0:T(8,128)(2,1)} %broadcast_in_dim.38), calls=%async_computation | async-start | bytes 393216 | tf_op jit(solution)/shard_map/all_to_all | solution.py:535
  11.6 6.4 %shard_map.86.blocks_ref = bf16[7,1040,256]{2,1,0:T(8,128)(2,1)} custom-call(bf16[1024,1024]{1,0:T(8,128)(2,1)} %tile_ref.1), custom_call_target="tpu_custom_call" | custom-call | bytes 5767168 | tf_op jit(solution)/shard_map/pallas_call | solution.py:459
  18.0 0.1 broadcast_and_fusion
  18.1 1.4 %all-to-all-done = bf16[8,96,128]{2,1,0:T(8,128)(2,1)S(1)} async-done(((bf16[8,96,128]{2,1,0:T(8,128)(2,1)}), bf16[8,96,128]{2,1,0:T(8,128)(2,1)S(1)}, u32[]{:S(2)}, u32[]{:S(2)}) %all-to-all-start) | async-done | bytes 196640 | tf_op jit(solution)/shard_map/all_to_all | solution.py:535
  19.5 8.6 %all-gather.everyone_ref = bf16[32,96,128]{2,1,0:T(8,128)(2,1)S(1)} all-gather(bf16[8,96,128]{2,1,0:T(8,128)(2,1)S(1)} %all-to-all-done), channel_id=2, replica_groups=mesh['row'=4,'col'=8] {'row'}, dimensions={0}, use_global_device_ids=true | all-gather | bytes 983040 | tf_op jit(solution)/shard_map/all_gather | solution.py:536
  28.2 0.0 copy-done.1
  28.2 2.1 %copy-done = bf16[7,1040,256]{2,1,0:T(8,128)(2,1)S(1)} copy-done((bf16[7,1040,256]{2,1,0:T(8,128)(2,1)S(1)}, bf16[7,1040,256]{2,1,0:T(8,128)(2,1)}, u32[]{:S(2)}) %copy-start) | copy-done | bytes 3727384
  30.2 54.6 %shard_map.87 = f32[32,8,128]{2,1,0:T(8,128)} custom-call(bf16[32,96,128]{2,1,0:T(8,128)(2,1)S(1)} %all-gather.everyone_ref, bf16[7,1040,256]{2,1,0:T(8,128)(2,1)S(1)} %copy-done, bf16[1648,256]{1,0:T(8,128)(2,1)S(1)} %copy-done.1), custom_call_target="tpu_custom_call" | custom-call | tf_op jit(solution)/shard_map/pallas_call | solution.py:477
  84.8 3.7 %all-to-all-start.1 = ((f32[32,8,128]{2,1,0:T(8,128)}), f32[32,8,128]{2,1,0:T(8,128)S(1)}, u32[]{:S(2)}, u32[]{:S(2)}) async-start(f32[32,8,128]{2,1,0:T(8,128)} %shard_map.87), calls=%async_computation.1 | async-start | bytes 262144 | tf_op jit(solution)/shard_map/all_to_all | solution.py:540
  88.5 0.1 broadcast_and_fusion.1
  88.6 7.6 %all-to-all-done.1 = f32[32,8,128]{2,1,0:T(8,128)S(1)} async-done(((f32[32,8,128]{2,1,0:T(8,128)}), f32[32,8,128]{2,1,0:T(8,128)S(1)}, u32[]{:S(2)}, u32[]{:S(2)}) %all-to-all-start.1) | async-done | bytes 131104 | tf_op jit(solution)/shard_map/all_to_all | solution.py:540
  96.3 0.1 fusion.31
  96.4 0.1 fusion.18
  96.4 0.7 pad_maximum_fusion.1
  97.1 0.1 fusion.8
  97.2 0.1 fusion.16
  97.3 0.6 copy.17
  (9 shorter events, 0.1 us)
Async XLA Ops:
  3.6 24.5 %copy-start.1 = (bf16[1648,256]{1,0:T(8,128)(2,1)S(1)}, bf16[1648,256]{1,0:T(8,128)(2,1)}, u32[]{:S(2)}) copy-start(bf16[1648,256]{1,0:T(8,128)(2,1)} %constant.76.clone.tables_ref) | copy-start | bytes 2531332
  4.3 15.2 %all-to-all-start = ((bf16[8,96,128]{2,1,0:T(8,128)(2,1)}), bf16[8,96,128]{2,1,0:T(8,128)(2,1)S(1)}, u32[]{:S(2)}, u32[]{:S(2)}) async-start(bf16[8,96,128]{2,1,0:T(8,128)(2,1)} %broadcast_in_dim.38), calls=%async_computation | async-start | bytes 393216 | tf_op jit(solution)/shard_map/all_to_all | solution.py:535
  28.2 2.1 %copy-start = (bf16[7,1040,256]{2,1,0:T(8,128)(2,1)S(1)}, bf16[7,1040,256]{2,1,0:T(8,128)(2,1)}, u32[]{:S(2)}) copy-start(bf16[7,1040,256]{2,1,0:T(8,128)(2,1)} %shard_map.86.blocks_ref) | copy-start | bytes 11182084
  84.8 11.4 %all-to-all-start.1 = ((f32[32,8,128]{2,1,0:T(8,128)}), f32[32,8,128]{2,1,0:T(8,128)S(1)}, u32[]{:S(2)}, u32[]{:S(2)}) async-start(f32[32,8,128]{2,1,0:T(8,128)} %shard_map.87), calls=%async_computation.1 | async-start | bytes 262144 | tf_op jit(solution)/shard_map/all_to_all | solution.py:540

commit v7 on v6

--- a/solution.py
+++ b/solution.py
@@ -92,8 +92,8 @@
 A_BLOCK, A_ROW, A_ROW_REST, A_COL_REST = 4, 5, 6, 7
 NEAR_ROW, NEAR_COL = 8, 9
 FIELDS = 10
-BATCH = 6
-RING = 32
+BATCH = 3
+RING = 16
 TRIO = 3
 SECOND = FREQS
 THIRD = 2 * FREQS - HALF_LANES
@@ -168,15 +168,14 @@
             here = pl.ds(pl.multiple_of(row + 16 * place, 16), 16)
             return jnp.where(lanes, source[block, here, :], source[block + 1, here, :])
 
+        groups = [group(place) for place in range(PATCH // 16 + 1)]
+        groups[0] = jnp.where(rows, groups[0], groups.pop())
         total = jnp.zeros((8, WIDE), jnp.float32)
-        for place in range(PATCH // 16):
-            values = group(place)
-            if place == 0:
-                values = jnp.where(rows, values, group(PATCH // 16))
-            patches[base + 16 * place : base + 16 * place + 16, :] = values
+        for values in groups:
             values = values.astype(jnp.float32)
             values = values * values
             total = total + (values[:8] + values[8:])
+        patches[base : base + PATCH, :] = jnp.concatenate(groups, axis=0)
         return total[:, :HALF_LANES] + total[:, HALF_LANES:]
 
     def patch_base(part, which):
@@ -219,7 +218,7 @@
         ss = spec[16 * group + 8 : 16 * group + 16, HALF_LANES:]
         return cc - ss, sc + cs, cc + ss, sc - cs
 
-    def stage_inverse():
+    def stage_cross():
         down = table("down")
         for pair in range(2 * (BATCH // TRIO)):
             trio, tile = divmod(pair, 2)
@@ -237,6 +236,8 @@
                 crosses[pair, 16 * group : 16 * group + 16, :] = jnp.concatenate(
                     [upper, lower], axis=0
                 ).astype(jnp.bfloat16)
+
+    def stage_inverse():
         lanes = lax.broadcasted_iota(jnp.int32, (PATCH, HALF_LANES), 1)
         for trio in range(BATCH // TRIO):
             low, high = (
@@ -263,7 +264,7 @@
         shift_rows = (rows - centre_reach).astype(jnp.float32)
         row_near = rows <= 2 * centre_reach
         for part in range(BATCH):
-            item = at(step, 2, part)
+            item = at(step, 3, part)
             near_row = items_ref[NEAR_ROW, item]
             near_col = items_ref[NEAR_COL, item]
             ring = item % RING
@@ -315,11 +316,13 @@
     to_scalars.wait()
     to_blocks.wait()
 
-    @pl.loop(0, (count + BATCH - 1) // BATCH + 2)
-    def _(step):
-        stage_score(step)
-        stage_inverse()
-        stage_half(step)
+    @pl.loop(0, ((count + BATCH - 1) // BATCH + 4) // 2)
+    def _(pair):
+        for step in (2 * pair, 2 * pair + 1):
+            stage_score(step)
+            stage_inverse()
+            stage_cross()
+            stage_half(step)
 
     used = lax.broadcasted_iota(jnp.int32, (capacity, 1), 0) < count
     total = jnp.sum(totals[...], axis=1, keepdims=True)
@@ -501,7 +504,7 @@
             pltpu.VMEM((2 * PATCH, HALF_LANES), jnp.float32),
             pltpu.VMEM((16, capacity), jnp.float32),
         ],
-        compiler_params=pltpu.CompilerParams(vmem_limit_bytes=40 * 1024 * 1024),
+        compiler_params=pltpu.CompilerParams(vmem_limit_bytes=61 * 1024 * 1024),
     )(everyone, blocks, tables)
 
 

time: 98.8 us -> 105 us (1.063)
  starting transfers between devices: 10.9 us -> 41.3 us
  Pallas kernels: 61 us -> 38 us
  local copies, waits for them, and re-layouts: 3.54 us -> 1.48 us
    all_to_all x1, starting transfers between devices: 3.67 us -> 34.1 us  [per_device(): lax.all_to_all(spread, ('row', 'col'), split_axis=0, concat_axis=0, tiled...]
    pallas_call x1, Pallas kernels: 54.6 us -> 31.6 us  [correlate(): pl.pallas_call(functools.partial(correlate_kernel, capacity, grid, places...]
    unnamed x5 -> x1, local copies, waits for them, and re-layouts: 2.66 us -> 0.61 us
  transfers between devices with their start and end apart: 2 -> 2, of which waited for: 2 -> 2; matrix products, arithmetic and copies ran while one was open for 0% -> 0% of each run, Pallas kernels for 7% -> 6%
where the time goes in v7:
time: 105 us; the launch traced here: 104 us
  starting transfers between devices  41.3 us (39%)
  Pallas kernels  38 us (36%)
  waiting for transfers between devices  9.09 us (9%)
  blocking collectives  9.06 us (9%)
  other arithmetic  4.02 us (4%)
  local copies, waits for them, and re-layouts  1.48 us (1%)
    all_to_all x1, starting transfers between devices, per_device(): lax.all_to_all(spread, ('row', 'col'), split_axis=0, concat_axis=0, tiled...  34.1 us
    pallas_call x1, Pallas kernels, correlate(): pl.pallas_call(functools.partial(correlate_kernel, capacity, grid, places...  31.6 us
    all_gather x1, blocking collectives, per_device(): everyone = lax.all_gather(sent, 'row').reshape(devices, a_rows + 16, a_cols)  9.06 us
    all_to_all x1, waiting for transfers between devices, per_device(): lax.all_to_all(spread, ('row', 'col'), split_axis=0, concat_axis=0, tiled...  7.65 us
    all_to_all x1, starting transfers between devices, per_device(): sent = lax.all_to_all(sent, 'col', split_axis=0, concat_axis=0, tiled=True)  7.25 us
    pallas_call x1, Pallas kernels, cut_tile(): pl.pallas_call(cut_kernel, grid=(rows // HALF_LANES,), out_shape=jax.Shap...  6.4 us
  transfers between devices with their start and end apart: 2, of which 2 were waited for; matrix products, arithmetic and copies ran while one was open for 0% of the time, Pallas kernels for 6%

profile of v7, /device:TPU:0, one launch (start us, length us, event | category | flops | bytes accessed | tf_op | source)
XLA Modules:
  0.0 103.6 jit_solution(6499137955205413161)
XLA Ops:
  0.6 0.7 copy_convert_fusion
  1.4 0.7 fusion.29
  2.1 0.7 fusion.22
  2.8 0.1 concatenate.10
  2.9 0.7 fusion.1
  3.6 0.7 broadcast_in_dim.38
  4.3 7.3 %all-to-all-start = ((bf16[8,96,128]{2,1,0:T(8,128)(2,1)}), bf16[8,96,128]{2,1,0:T(8,128)(2,1)S(1)}, u32[]{:S(2)}, u32[]{:S(2)}) async-start(bf16[8,96,128]{2,1,0:T(8,128)(2,1)} %broadcast_in_dim.38), calls=%async_computation | async-start | bytes 393216 | tf_op jit(solution)/shard_map/all_to_all | solution.py:538
  11.6 6.4 %shard_map.86.blocks_ref = bf16[7,1040,256]{2,1,0:T(8,128)(2,1)} custom-call(bf16[1024,1024]{1,0:T(8,128)(2,1)} %tile_ref.1), custom_call_target="tpu_custom_call" | custom-call | bytes 5767168 | tf_op jit(solution)/shard_map/pallas_call | solution.py:462
  18.0 0.1 broadcast_and_fusion
  18.1 1.4 %all-to-all-done = bf16[8,96,128]{2,1,0:T(8,128)(2,1)S(1)} async-done(((bf16[8,96,128]{2,1,0:T(8,128)(2,1)}), bf16[8,96,128]{2,1,0:T(8,128)(2,1)S(1)}, u32[]{:S(2)}, u32[]{:S(2)}) %all-to-all-start) | async-done | bytes 196640 | tf_op jit(solution)/shard_map/all_to_all | solution.py:538
  19.5 9.1 %all-gather.everyone_ref = bf16[32,96,128]{2,1,0:T(8,128)(2,1)} all-gather(bf16[8,96,128]{2,1,0:T(8,128)(2,1)S(1)} %all-to-all-done), channel_id=2, replica_groups=mesh['row'=4,'col'=8] {'row'}, dimensions={0}, use_global_device_ids=true | all-gather | bytes 983040 | tf_op jit(solution)/shard_map/all_gather | solution.py:539
  28.6 31.6 %shard_map.87 = f32[32,8,128]{2,1,0:T(8,128)} custom-call(bf16[32,96,128]{2,1,0:T(8,128)(2,1)} %all-gather.everyone_ref, bf16[7,1040,256]{2,1,0:T(8,128)(2,1)} %shard_map.86.blocks_ref, bf16[1648,256]{1,0:T(8,128)(2,1)} %constant.76.clone.tables_ref), custom_call_target="tpu_custom_call" | custom-call | tf_op jit(solution)/shard_map/pallas_call | solution.py:480
  60.2 34.1 %all-to-all-start.1 = ((f32[32,8,128]{2,1,0:T(8,128)}), f32[32,8,128]{2,1,0:T(8,128)S(1)}, u32[]{:S(2)}, u32[]{:S(2)}) async-start(f32[32,8,128]{2,1,0:T(8,128)} %shard_map.87), calls=%async_computation.1 | async-start | bytes 262144 | tf_op jit(solution)/shard_map/all_to_all | solution.py:543
  94.3 0.1 broadcast_and_fusion.1
  94.3 7.6 %all-to-all-done.1 = f32[32,8,128]{2,1,0:T(8,128)S(1)} async-done(((f32[32,8,128]{2,1,0:T(8,128)}), f32[32,8,128]{2,1,0:T(8,128)S(1)}, u32[]{:S(2)}, u32[]{:S(2)}) %all-to-all-start.1) | async-done | bytes 131104 | tf_op jit(solution)/shard_map/all_to_all | solution.py:543
  102.0 0.1 fusion.31
  102.1 0.1 fusion.18
  102.2 0.7 pad_maximum_fusion.1
  102.8 0.1 fusion.8
  102.9 0.1 fusion.16
  103.0 0.6 copy.17
  (8 shorter events, 0.1 us)
Async XLA Ops:
  4.3 15.2 %all-to-all-start = ((bf16[8,96,128]{2,1,0:T(8,128)(2,1)}), bf16[8,96,128]{2,1,0:T(8,128)(2,1)S(1)}, u32[]{:S(2)}, u32[]{:S(2)}) async-start(bf16[8,96,128]{2,1,0:T(8,128)(2,1)} %broadcast_in_dim.38), calls=%async_computation | async-start | bytes 393216 | tf_op jit(solution)/shard_map/all_to_all | solution.py:538
  60.2 41.8 %all-to-all-start.1 = ((f32[32,8,128]{2,1,0:T(8,128)}), f32[32,8,128]{2,1,0:T(8,128)S(1)}, u32[]{:S(2)}, u32[]{:S(2)}) async-start(f32[32,8,128]{2,1,0:T(8,128)} %shard_map.87), calls=%async_computation.1 | async-start | bytes 262144 | tf_op jit(solution)/shard_map/all_to_all | solution.py:543

commit v8 on v6

--- a/solution.py
+++ b/solution.py
@@ -95,6 +95,9 @@
 BATCH = 6
 RING = 32
 TRIO = 3
+ABOVE = 24
+BELOW = 32
+CAP_ROWS = 64
 SECOND = FREQS
 THIRD = 2 * FREQS - HALF_LANES
 
@@ -138,8 +141,8 @@
         rows_ref,
         listed_ref,
     )
-    caps_row = lax.broadcasted_iota(jnp.int32, caps_ref.shape, 0) % PATCH
-    caps_ref[...] = jnp.where(caps_row <= 2 * centre_reach, -BIG, BIG)
+    caps_row = lax.broadcasted_iota(jnp.int32, caps_ref.shape, 0) - CAP_ROWS
+    caps_ref[...] = jnp.where((caps_row >= 0) & (caps_row <= 2 * centre_reach), -BIG, BIG)
     to_scalars = pltpu.make_async_copy(listed_ref, items_ref, semaphores.at[1])
     to_scalars.start()
 
@@ -168,11 +171,10 @@
             here = pl.ds(pl.multiple_of(row + 16 * place, 16), 16)
             return jnp.where(lanes, source[block, here, :], source[block + 1, here, :])
 
+        groups = [group(place) for place in range(PATCH // 16 + 1)]
+        groups[0] = jnp.where(rows, groups[0], groups.pop())
         total = jnp.zeros((8, WIDE), jnp.float32)
-        for place in range(PATCH // 16):
-            values = group(place)
-            if place == 0:
-                values = jnp.where(rows, values, group(PATCH // 16))
+        for place, values in enumerate(groups):
             patches[base + 16 * place : base + 16 * place + 16, :] = values
             values = values.astype(jnp.float32)
             values = values * values
@@ -272,7 +274,7 @@
             scale = 1.0 / (
                 float(PATCH**4) * jnp.sqrt(mean_a + epsilon) * jnp.sqrt(mean_b + epsilon)
             )
-            caps = caps_ref[pl.ds(PATCH - near_row, PATCH), :]
+            caps = caps_ref[pl.ds(CAP_ROWS - near_row, ABOVE + BELOW), :]
             total, row_moment, col_moment = 0.0, 0.0, 0.0
             best = None
             for half in range(2):
@@ -280,10 +282,11 @@
                     PATCH * part : PATCH * (part + 1),
                     half * HALF_LANES : (half + 1) * HALF_LANES,
                 ]
-                corrs[half][part, :PATCH, :] = corr
-                corrs[half][part, PATCH:, :] = corr[:8]
-                far = jnp.max(
-                    jnp.minimum(corr, caps).reshape(PATCH // 8, 8, HALF_LANES), axis=0
+                edge = jnp.concatenate([corr[PATCH - ABOVE :], corr[:BELOW]], axis=0)
+                corrs[half][part] = edge
+                far = jnp.maximum(
+                    jnp.max(jnp.minimum(edge, caps).reshape(-1, 8, HALF_LANES), axis=0),
+                    jnp.max(corr[BELOW : PATCH - ABOVE].reshape(-1, 8, HALF_LANES), axis=0),
                 )
                 if half == 0:
                     best = far
@@ -315,11 +318,20 @@
     to_scalars.wait()
     to_blocks.wait()
 
-    @pl.loop(0, (count + BATCH - 1) // BATCH + 2)
+    steps = jnp.maximum((count + BATCH - 1) // BATCH, 2)
+    stage_half(0)
+    stage_inverse()
+    stage_half(1)
+
+    @pl.loop(2, steps)
     def _(step):
         stage_score(step)
         stage_inverse()
         stage_half(step)
+
+    stage_score(steps)
+    stage_inverse()
+    stage_score(steps + 1)
 
     used = lax.broadcasted_iota(jnp.int32, (capacity, 1), 0) < count
     total = jnp.sum(totals[...], axis=1, keepdims=True)
@@ -428,7 +440,7 @@
     b_block, b_col_rest = divide(b_left, PATCH)
     a_group, a_row_rest = divide(a_top, 16)
     a_block, a_col_rest = divide(a_left, PATCH)
-    near_row = divide(field(PEAK_ROW) + b_row_rest - a_row_rest - centre_reach, PATCH)[1]
+    near_row = field(PEAK_ROW) + b_row_rest - a_row_rest + (ABOVE - centre_reach)
     near_col = divide(field(PEAK_COL) + b_col_rest - a_col_rest, PATCH)[1]
     for index, value in (
         (B_BLOCK, b_block),
@@ -486,8 +498,8 @@
             pltpu.VMEM((BATCH // TRIO, 2, 2, PATCH, WIDE), jnp.bfloat16),
             pltpu.VMEM((BATCH // TRIO * 2, PAIRED, WIDE), jnp.bfloat16),
             pltpu.VMEM((BATCH * PATCH, WIDE), jnp.bfloat16),
-            pltpu.VMEM((BATCH, PATCH + 8, HALF_LANES), jnp.float32),
-            pltpu.VMEM((BATCH, PATCH + 8, HALF_LANES), jnp.float32),
+            pltpu.VMEM((BATCH, ABOVE + BELOW, HALF_LANES), jnp.float32),
+            pltpu.VMEM((BATCH, ABOVE + BELOW, HALF_LANES), jnp.float32),
             pltpu.VMEM((RING, 2, 8, HALF_LANES), jnp.float32),
         ]
         + [rows] * 4
@@ -498,10 +510,10 @@
             pltpu.VMEM((16, capacity), jnp.int32),
             pltpu.SMEM((16, capacity), jnp.int32),
             pltpu.SemaphoreType.DMA((2,)),
-            pltpu.VMEM((2 * PATCH, HALF_LANES), jnp.float32),
+            pltpu.VMEM((2 * CAP_ROWS, HALF_LANES), jnp.float32),
             pltpu.VMEM((16, capacity), jnp.float32),
         ],
-        compiler_params=pltpu.CompilerParams(vmem_limit_bytes=40 * 1024 * 1024),
+        compiler_params=pltpu.CompilerParams(vmem_limit_bytes=61 * 1024 * 1024),
     )(everyone, blocks, tables)
 
 

time: 98.8 us -> 96.8 us (0.980)
  Pallas kernels: 61 us -> 30.9 us
  starting transfers between devices: 10.9 us -> 40.9 us
  local copies, waits for them, and re-layouts: 3.54 us -> 1.48 us
    pallas_call x1, Pallas kernels: 54.6 us -> 24.5 us  [correlate(): pl.pallas_call(functools.partial(correlate_kernel, capacity, grid, places...]
    all_to_all x1, starting transfers between devices: 3.67 us -> 33.7 us  [per_device(): lax.all_to_all(spread, ('row', 'col'), split_axis=0, concat_axis=0, tiled...]
    unnamed x5 -> x1, local copies, waits for them, and re-layouts: 2.66 us -> 0.61 us
where the time goes in v8:
time: 96.8 us; the launch traced here: 96.2 us
  starting transfers between devices  40.9 us (42%)
  Pallas kernels  30.9 us (32%)
  waiting for transfers between devices  9.09 us (9%)
  blocking collectives  9.06 us (9%)
  other arithmetic  4.02 us (4%)
  local copies, waits for them, and re-layouts  1.48 us (2%)
    all_to_all x1, starting transfers between devices, per_device(): lax.all_to_all(spread, ('row', 'col'), split_axis=0, concat_axis=0, tiled...  33.7 us
    pallas_call x1, Pallas kernels, correlate(): pl.pallas_call(functools.partial(correlate_kernel, capacity, grid, places...  24.5 us
    all_gather x1, blocking collectives, per_device(): everyone = lax.all_gather(sent, 'row').reshape(devices, a_rows + 16, a_cols)  9.06 us
    all_to_all x1, waiting for transfers between devices, per_device(): lax.all_to_all(spread, ('row', 'col'), split_axis=0, concat_axis=0, tiled...  7.65 us
    all_to_all x1, starting transfers between devices, per_device(): sent = lax.all_to_all(sent, 'col', split_axis=0, concat_axis=0, tiled=True)  7.25 us
    pallas_call x1, Pallas kernels, cut_tile(): pl.pallas_call(cut_kernel, grid=(rows // HALF_LANES,), out_shape=jax.Shap...  6.4 us
  transfers between devices with their start and end apart: 2, of which 2 were waited for; matrix products, arithmetic and copies ran while one was open for 0% of the time, Pallas kernels for 7%

profile of v8, /device:TPU:0, one launch (start us, length us, event | category | flops | bytes accessed | tf_op | source)
XLA Modules:
  0.0 96.2 jit_solution(7136410524819214899)
XLA Ops:
  0.6 0.7 copy_convert_fusion
  1.4 0.7 fusion.29
  2.1 0.7 fusion.22
  2.8 0.1 concatenate.10
  2.9 0.7 fusion.1
  3.6 0.7 broadcast_in_dim.38
  4.3 7.3 %all-to-all-start = ((bf16[8,96,128]{2,1,0:T(8,128)(2,1)}), bf16[8,96,128]{2,1,0:T(8,128)(2,1)S(1)}, u32[]{:S(2)}, u32[]{:S(2)}) async-start(bf16[8,96,128]{2,1,0:T(8,128)(2,1)} %broadcast_in_dim.38), calls=%async_computation | async-start | bytes 393216 | tf_op jit(solution)/shard_map/all_to_all | solution.py:547
  11.6 6.4 %shard_map.86.blocks_ref = bf16[7,1040,256]{2,1,0:T(8,128)(2,1)} custom-call(bf16[1024,1024]{1,0:T(8,128)(2,1)} %tile_ref.1), custom_call_target="tpu_custom_call" | custom-call | bytes 5767168 | tf_op jit(solution)/shard_map/pallas_call | solution.py:471
  18.0 0.1 broadcast_and_fusion
  18.1 1.4 %all-to-all-done = bf16[8,96,128]{2,1,0:T(8,128)(2,1)S(1)} async-done(((bf16[8,96,128]{2,1,0:T(8,128)(2,1)}), bf16[8,96,128]{2,1,0:T(8,128)(2,1)S(1)}, u32[]{:S(2)}, u32[]{:S(2)}) %all-to-all-start) | async-done | bytes 196640 | tf_op jit(solution)/shard_map/all_to_all | solution.py:547
  19.5 9.1 %all-gather.everyone_ref = bf16[32,96,128]{2,1,0:T(8,128)(2,1)} all-gather(bf16[8,96,128]{2,1,0:T(8,128)(2,1)S(1)} %all-to-all-done), channel_id=2, replica_groups=mesh['row'=4,'col'=8] {'row'}, dimensions={0}, use_global_device_ids=true | all-gather | bytes 983040 | tf_op jit(solution)/shard_map/all_gather | solution.py:548
  28.6 24.5 %shard_map.87 = f32[32,8,128]{2,1,0:T(8,128)} custom-call(bf16[32,96,128]{2,1,0:T(8,128)(2,1)} %all-gather.everyone_ref, bf16[7,1040,256]{2,1,0:T(8,128)(2,1)} %shard_map.86.blocks_ref, bf16[1648,256]{1,0:T(8,128)(2,1)} %constant.76.clone.tables_ref), custom_call_target="tpu_custom_call" | custom-call | tf_op jit(solution)/shard_map/pallas_call | solution.py:489
  53.1 33.7 %all-to-all-start.1 = ((f32[32,8,128]{2,1,0:T(8,128)}), f32[32,8,128]{2,1,0:T(8,128)S(1)}, u32[]{:S(2)}, u32[]{:S(2)}) async-start(f32[32,8,128]{2,1,0:T(8,128)} %shard_map.87), calls=%async_computation.1 | async-start | bytes 262144 | tf_op jit(solution)/shard_map/all_to_all | solution.py:552
  86.8 0.1 broadcast_and_fusion.1
  86.8 7.6 %all-to-all-done.1 = f32[32,8,128]{2,1,0:T(8,128)S(1)} async-done(((f32[32,8,128]{2,1,0:T(8,128)}), f32[32,8,128]{2,1,0:T(8,128)S(1)}, u32[]{:S(2)}, u32[]{:S(2)}) %all-to-all-start.1) | async-done | bytes 131104 | tf_op jit(solution)/shard_map/all_to_all | solution.py:552
  94.5 0.1 fusion.31
  94.6 0.1 fusion.18
  94.7 0.7 pad_maximum_fusion.1
  95.4 0.1 fusion.8
  95.4 0.1 fusion.16
  95.5 0.6 copy.17
  (8 shorter events, 0.1 us)
Async XLA Ops:
  4.3 15.2 %all-to-all-start = ((bf16[8,96,128]{2,1,0:T(8,128)(2,1)}), bf16[8,96,128]{2,1,0:T(8,128)(2,1)S(1)}, u32[]{:S(2)}, u32[]{:S(2)}) async-start(bf16[8,96,128]{2,1,0:T(8,128)(2,1)} %broadcast_in_dim.38), calls=%async_computation | async-start | bytes 393216 | tf_op jit(solution)/shard_map/all_to_all | solution.py:547
  53.1 41.4 %all-to-all-start.1 = ((f32[32,8,128]{2,1,0:T(8,128)}), f32[32,8,128]{2,1,0:T(8,128)S(1)}, u32[]{:S(2)}, u32[]{:S(2)}) async-start(f32[32,8,128]{2,1,0:T(8,128)} %shard_map.87), calls=%async_computation.1 | async-start | bytes 262144 | tf_op jit(solution)/shard_map/all_to_all | solution.py:552

commit v9 on v8

--- a/solution.py
+++ b/solution.py
@@ -93,7 +93,6 @@
 NEAR_ROW, NEAR_COL = 8, 9
 FIELDS = 10
 BATCH = 6
-RING = 32
 TRIO = 3
 ABOVE = 24
 BELOW = 32
@@ -123,7 +122,7 @@
     patches, halves, crosses, inverses = scratch[:4]
     corrs = scratch[4:6]
     energies, totals, row_moments, col_moments, runners, a_ref, b_ref = scratch[6:13]
-    columns_ref, listed_ref, items_ref, semaphores, caps_ref, rows_ref = scratch[13:]
+    columns_ref, listed_ref, items_ref, semaphores, caps_ref, rows_ref, shares_ref = scratch[13:]
     to_blocks = pltpu.make_async_copy(blocks_ref, b_ref, semaphores.at[0])
     to_blocks.start()
 
@@ -141,6 +140,13 @@
         rows_ref,
         listed_ref,
     )
+    for place in range(TRIO):
+        for tile in range(2):
+            freq = lax.broadcasted_iota(jnp.int32, (8, HALF_LANES), 1)
+            freq = freq + (tile * HALF_LANES - place * FREQS)
+            once = (freq == 0) | (freq == FREQS - 1)
+            twice = (freq > 0) & (freq < FREQS - 1)
+            shares_ref[place, tile] = jnp.where(twice, 4.0, jnp.where(once, 2.0, 0.0))
     caps_row = lax.broadcasted_iota(jnp.int32, caps_ref.shape, 0) - CAP_ROWS
     caps_ref[...] = jnp.where((caps_row >= 0) & (caps_row <= 2 * centre_reach), -BIG, BIG)
     to_scalars = pltpu.make_async_copy(listed_ref, items_ref, semaphores.at[1])
@@ -173,13 +179,8 @@
 
         groups = [group(place) for place in range(PATCH // 16 + 1)]
         groups[0] = jnp.where(rows, groups[0], groups.pop())
-        total = jnp.zeros((8, WIDE), jnp.float32)
         for place, values in enumerate(groups):
             patches[base + 16 * place : base + 16 * place + 16, :] = values
-            values = values.astype(jnp.float32)
-            values = values * values
-            total = total + (values[:8] + values[8:])
-        return total[:, :HALF_LANES] + total[:, HALF_LANES:]
 
     def patch_base(part, which):
         trio, place = divmod(part, TRIO)
@@ -193,9 +194,7 @@
                 (1, b_ref, (B_BLOCK, B_ROW, B_ROW_REST, B_COL_REST)),
             ):
                 block, row, row_rest, col_rest = (items_ref[field, item] for field in fields)
-                energies[item % RING, which] = extract(
-                    source, block, row, row_rest, col_rest, patch_base(part, which)
-                )
+                extract(source, block, row, row_rest, col_rest, patch_base(part, which))
         half = jnp.dot(patches[...], table("across"), preferred_element_type=jnp.float32)
         lanes = lax.broadcasted_iota(jnp.int32, (PATCH, HALF_LANES), 1)
         for trio in range(BATCH // TRIO):
@@ -219,17 +218,25 @@
         cs = spec[16 * group : 16 * group + 8, HALF_LANES:]
         sc = spec[16 * group + 8 : 16 * group + 16, :HALF_LANES]
         ss = spec[16 * group + 8 : 16 * group + 16, HALF_LANES:]
-        return cc - ss, sc + cs, cc + ss, sc - cs
+        power = (cc * cc + cs * cs) + (sc * sc + ss * ss)
+        return cc - ss, sc + cs, cc + ss, sc - cs, power
 
     def stage_inverse():
         down = table("down")
+        top = lax.broadcasted_iota(jnp.int32, (8, HALF_LANES), 0) == 0
         for pair in range(2 * (BATCH // TRIO)):
             trio, tile = divmod(pair, 2)
             spec_a = jnp.dot(down, halves[trio, 0, tile], preferred_element_type=jnp.float32)
             spec_b = jnp.dot(down, halves[trio, 1, tile], preferred_element_type=jnp.float32)
             for group in range(GROUPS):
-                a_pr, a_pi, a_mr, a_mi = sides(spec_a, group)
-                b_pr, b_pi, b_mr, b_mi = sides(spec_b, group)
+                a_pr, a_pi, a_mr, a_mi, a_power = sides(spec_a, group)
+                b_pr, b_pi, b_mr, b_mi, b_power = sides(spec_b, group)
+                if group == 0:
+                    powers = [jnp.where(top, 0.5 * power, power) for power in (a_power, b_power)]
+                elif group < GROUPS - 1:
+                    powers = [powers[0] + a_power, powers[1] + b_power]
+                else:
+                    powers = [powers[0] + 0.5 * a_power, powers[1] + 0.5 * b_power]
                 pr = a_pr * b_pr + a_pi * b_pi
                 pi = a_pr * b_pi - a_pi * b_pr
                 mr = a_mr * b_mr + a_mi * b_mi
@@ -239,6 +246,8 @@
                 crosses[pair, 16 * group : 16 * group + 16, :] = jnp.concatenate(
                     [upper, lower], axis=0
                 ).astype(jnp.bfloat16)
+            energies[trio, 0, tile] = powers[0]
+            energies[trio, 1, tile] = powers[1]
         lanes = lax.broadcasted_iota(jnp.int32, (PATCH, HALF_LANES), 1)
         for trio in range(BATCH // TRIO):
             low, high = (
@@ -268,9 +277,16 @@
             item = at(step, 2, part)
             near_row = items_ref[NEAR_ROW, item]
             near_col = items_ref[NEAR_COL, item]
-            ring = item % RING
-            mean_a = jnp.sum(energies[ring, 0], keepdims=True) * (1.0 / (PATCH * PATCH))
-            mean_b = jnp.sum(energies[ring, 1], keepdims=True) * (1.0 / (PATCH * PATCH))
+            trio, place = divmod(part, TRIO)
+            mean_a, mean_b = (
+                jnp.sum(
+                    energies[trio, which, 0] * shares_ref[place, 0]
+                    + energies[trio, which, 1] * shares_ref[place, 1],
+                    keepdims=True,
+                )
+                * (1.0 / float(PATCH**4))
+                for which in range(2)
+            )
             scale = 1.0 / (
                 float(PATCH**4) * jnp.sqrt(mean_a + epsilon) * jnp.sqrt(mean_b + epsilon)
             )
@@ -500,7 +516,7 @@
             pltpu.VMEM((BATCH * PATCH, WIDE), jnp.bfloat16),
             pltpu.VMEM((BATCH, ABOVE + BELOW, HALF_LANES), jnp.float32),
             pltpu.VMEM((BATCH, ABOVE + BELOW, HALF_LANES), jnp.float32),
-            pltpu.VMEM((RING, 2, 8, HALF_LANES), jnp.float32),
+            pltpu.VMEM((BATCH // TRIO, 2, 2, 8, HALF_LANES), jnp.float32),
         ]
         + [rows] * 4
         + [
@@ -512,6 +528,7 @@
             pltpu.SemaphoreType.DMA((2,)),
             pltpu.VMEM((2 * CAP_ROWS, HALF_LANES), jnp.float32),
             pltpu.VMEM((16, capacity), jnp.float32),
+            pltpu.VMEM((TRIO, 2, 8, HALF_LANES), jnp.float32),
         ],
         compiler_params=pltpu.CompilerParams(vmem_limit_bytes=61 * 1024 * 1024),
     )(everyone, blocks, tables)

time: 96.8 us -> 96.4 us (level)
  starting transfers between devices: 40.9 us -> 32.2 us
  Pallas kernels: 30.9 us -> 38.8 us
    all_to_all x1, starting transfers between devices: 33.7 us -> 24.9 us  [per_device(): lax.all_to_all(spread, ('row', 'col'), split_axis=0, concat_axis=0, tiled...]
    pallas_call x1, Pallas kernels: 24.5 us -> 32.4 us  [correlate(): pl.pallas_call(functools.partial(correlate_kernel, capacity, grid, places...]
where the time goes in v9:
time: 96.4 us; the launch traced here: 95.3 us
  Pallas kernels  38.8 us (40%)
  starting transfers between devices  32.2 us (33%)
  waiting for transfers between devices  9.09 us (9%)
  blocking collectives  9.06 us (9%)
  other arithmetic  4.02 us (4%)
  local copies, waits for them, and re-layouts  1.48 us (2%)
    pallas_call x1, Pallas kernels, correlate(): pl.pallas_call(functools.partial(correlate_kernel, capacity, grid, places...  32.4 us
    all_to_all x1, starting transfers between devices, per_device(): lax.all_to_all(spread, ('row', 'col'), split_axis=0, concat_axis=0, tiled...  24.9 us
    all_gather x1, blocking collectives, per_device(): everyone = lax.all_gather(sent, 'row').reshape(devices, a_rows + 16, a_cols)  9.06 us
    all_to_all x1, waiting for transfers between devices, per_device(): lax.all_to_all(spread, ('row', 'col'), split_axis=0, concat_axis=0, tiled...  7.65 us
    all_to_all x1, starting transfers between devices, per_device(): sent = lax.all_to_all(sent, 'col', split_axis=0, concat_axis=0, tiled=True)  7.25 us
    pallas_call x1, Pallas kernels, cut_tile(): pl.pallas_call(cut_kernel, grid=(rows // HALF_LANES,), out_shape=jax.Shap...  6.4 us
  transfers between devices with their start and end apart: 2, of which 2 were waited for; matrix products, arithmetic and copies ran while one was open for 0% of the time, Pallas kernels for 7%

profile of v9, /device:TPU:0, one launch (start us, length us, event | category | flops | bytes accessed | tf_op | source)
XLA Modules:
  0.0 95.3 jit_solution(14910982642827980440)
XLA Ops:
  0.6 0.7 copy_convert_fusion
  1.4 0.7 fusion.29
  2.1 0.7 fusion.22
  2.8 0.1 concatenate.10
  2.9 0.7 fusion.1
  3.6 0.7 broadcast_in_dim.38
  4.3 7.3 %all-to-all-start = ((bf16[8,96,128]{2,1,0:T(8,128)(2,1)}), bf16[8,96,128]{2,1,0:T(8,128)(2,1)S(1)}, u32[]{:S(2)}, u32[]{:S(2)}) async-start(bf16[8,96,128]{2,1,0:T(8,128)(2,1)} %broadcast_in_dim.38), calls=%async_computation | async-start | bytes 393216 | tf_op jit(solution)/shard_map/all_to_all | solution.py:564
  11.6 6.4 %shard_map.86.blocks_ref = bf16[7,1040,256]{2,1,0:T(8,128)(2,1)} custom-call(bf16[1024,1024]{1,0:T(8,128)(2,1)} %tile_ref.1), custom_call_target="tpu_custom_call" | custom-call | bytes 5767168 | tf_op jit(solution)/shard_map/pallas_call | solution.py:487
  18.0 0.1 broadcast_and_fusion
  18.1 1.4 %all-to-all-done = bf16[8,96,128]{2,1,0:T(8,128)(2,1)S(1)} async-done(((bf16[8,96,128]{2,1,0:T(8,128)(2,1)}), bf16[8,96,128]{2,1,0:T(8,128)(2,1)S(1)}, u32[]{:S(2)}, u32[]{:S(2)}) %all-to-all-start) | async-done | bytes 196640 | tf_op jit(solution)/shard_map/all_to_all | solution.py:564
  19.5 9.1 %all-gather.everyone_ref = bf16[32,96,128]{2,1,0:T(8,128)(2,1)} all-gather(bf16[8,96,128]{2,1,0:T(8,128)(2,1)S(1)} %all-to-all-done), channel_id=2, replica_groups=mesh['row'=4,'col'=8] {'row'}, dimensions={0}, use_global_device_ids=true | all-gather | bytes 983040 | tf_op jit(solution)/shard_map/all_gather | solution.py:565
  28.6 32.4 %shard_map.87 = f32[32,8,128]{2,1,0:T(8,128)} custom-call(bf16[32,96,128]{2,1,0:T(8,128)(2,1)} %all-gather.everyone_ref, bf16[7,1040,256]{2,1,0:T(8,128)(2,1)} %shard_map.86.blocks_ref, bf16[1648,256]{1,0:T(8,128)(2,1)} %constant.76.clone.tables_ref), custom_call_target="tpu_custom_call" | custom-call | tf_op jit(solution)/shard_map/pallas_call | solution.py:505
  61.0 24.9 %all-to-all-start.1 = ((f32[32,8,128]{2,1,0:T(8,128)}), f32[32,8,128]{2,1,0:T(8,128)S(1)}, u32[]{:S(2)}, u32[]{:S(2)}) async-start(f32[32,8,128]{2,1,0:T(8,128)} %shard_map.87), calls=%async_computation.1 | async-start | bytes 262144 | tf_op jit(solution)/shard_map/all_to_all | solution.py:569
  86.0 0.1 broadcast_and_fusion.1
  86.0 7.6 %all-to-all-done.1 = f32[32,8,128]{2,1,0:T(8,128)S(1)} async-done(((f32[32,8,128]{2,1,0:T(8,128)}), f32[32,8,128]{2,1,0:T(8,128)S(1)}, u32[]{:S(2)}, u32[]{:S(2)}) %all-to-all-start.1) | async-done | bytes 131104 | tf_op jit(solution)/shard_map/all_to_all | solution.py:569
  93.7 0.1 fusion.31
  93.8 0.1 fusion.18
  93.9 0.7 pad_maximum_fusion.1
  94.5 0.1 fusion.8
  94.6 0.1 fusion.16
  94.7 0.6 copy.17
  (8 shorter events, 0.1 us)
Async XLA Ops:
  4.3 15.2 %all-to-all-start = ((bf16[8,96,128]{2,1,0:T(8,128)(2,1)}), bf16[8,96,128]{2,1,0:T(8,128)(2,1)S(1)}, u32[]{:S(2)}, u32[]{:S(2)}) async-start(bf16[8,96,128]{2,1,0:T(8,128)(2,1)} %broadcast_in_dim.38), calls=%async_computation | async-start | bytes 393216 | tf_op jit(solution)/shard_map/all_to_all | solution.py:564
  61.0 32.7 %all-to-all-start.1 = ((f32[32,8,128]{2,1,0:T(8,128)}), f32[32,8,128]{2,1,0:T(8,128)S(1)}, u32[]{:S(2)}, u32[]{:S(2)}) async-start(f32[32,8,128]{2,1,0:T(8,128)} %shard_map.87), calls=%async_computation.1 | async-start | bytes 262144 | tf_op jit(solution)/shard_map/all_to_all | solution.py:569

commit v10 on v9

--- a/solution.py
+++ b/solution.py
@@ -180,11 +180,12 @@
         groups = [group(place) for place in range(PATCH // 16 + 1)]
         groups[0] = jnp.where(rows, groups[0], groups.pop())
         for place, values in enumerate(groups):
-            patches[base + 16 * place : base + 16 * place + 16, :] = values
+            start = base + 16 * TRIO * place
+            patches[start : start + 16, :] = values
 
     def patch_base(part, which):
         trio, place = divmod(part, TRIO)
-        return ((2 * trio + which) * TRIO + place) * PATCH
+        return (2 * trio + which) * TRIO * PATCH + 16 * place
 
     def stage_half(step):
         for part in range(BATCH):
@@ -196,22 +197,27 @@
                 block, row, row_rest, col_rest = (items_ref[field, item] for field in fields)
                 extract(source, block, row, row_rest, col_rest, patch_base(part, which))
         half = jnp.dot(patches[...], table("across"), preferred_element_type=jnp.float32)
-        lanes = lax.broadcasted_iota(jnp.int32, (PATCH, HALF_LANES), 1)
+        lanes = lax.broadcasted_iota(jnp.int32, (16, HALF_LANES), 1)
         for trio in range(BATCH // TRIO):
             for which in range(2):
-                for side in (slice(0, HALF_LANES), slice(HALF_LANES, WIDE)):
-                    first, second, third = (
-                        half[base : base + PATCH, side]
-                        for base in (patch_base(TRIO * trio + n, which) for n in range(TRIO))
-                    )
-                    second = pltpu.roll(second, SECOND, axis=1)
-                    third = pltpu.roll(third, THIRD, axis=1)
-                    halves[trio, which, 0, :, side] = jnp.where(
-                        lanes < SECOND, first, second
-                    ).astype(jnp.bfloat16)
-                    halves[trio, which, 1, :, side] = jnp.where(
-                        lanes < THIRD, second, third
-                    ).astype(jnp.bfloat16)
+                for group in range(PATCH // 16):
+                    rows = slice(16 * group, 16 * group + 16)
+                    for side in (slice(0, HALF_LANES), slice(HALF_LANES, WIDE)):
+                        first, second, third = (
+                            half[base : base + 16, side]
+                            for base in (
+                                patch_base(TRIO * trio + n, which) + 16 * TRIO * group
+                                for n in range(TRIO)
+                            )
+                        )
+                        second = pltpu.roll(second, SECOND, axis=1)
+                        third = pltpu.roll(third, THIRD, axis=1)
+                        halves[trio, which, 0, rows, side] = jnp.where(
+                            lanes < SECOND, first, second
+                        ).astype(jnp.bfloat16)
+                        halves[trio, which, 1, rows, side] = jnp.where(
+                            lanes < THIRD, second, third
+                        ).astype(jnp.bfloat16)
 
     def sides(spec, group):
         cc = spec[16 * group : 16 * group + 8, :HALF_LANES]

time: 96.4 us -> 97.2 us (level)
  Pallas kernels: 38.8 us -> 59.5 us
  starting transfers between devices: 32.2 us -> 12.2 us
    pallas_call x1, Pallas kernels: 32.4 us -> 53.1 us  [correlate(): pl.pallas_call(functools.partial(correlate_kernel, capacity, grid, places...]
    all_to_all x1, starting transfers between devices: 24.9 us -> 4.91 us  [per_device(): lax.all_to_all(spread, ('row', 'col'), split_axis=0, concat_axis=0, tiled...]
where the time goes in v10:
time: 97.2 us; the launch traced here: 96 us
  Pallas kernels  59.5 us (61%)
  starting transfers between devices  12.2 us (13%)
  waiting for transfers between devices  9.09 us (9%)
  blocking collectives  9.06 us (9%)
  other arithmetic  4.02 us (4%)
  local copies, waits for them, and re-layouts  1.48 us (2%)
    pallas_call x1, Pallas kernels, correlate(): pl.pallas_call(functools.partial(correlate_kernel, capacity, grid, places...  53.1 us
    all_gather x1, blocking collectives, per_device(): everyone = lax.all_gather(sent, 'row').reshape(devices, a_rows + 16, a_cols)  9.06 us
    all_to_all x1, waiting for transfers between devices, per_device(): lax.all_to_all(spread, ('row', 'col'), split_axis=0, concat_axis=0, tiled...  7.65 us
    all_to_all x1, starting transfers between devices, per_device(): sent = lax.all_to_all(sent, 'col', split_axis=0, concat_axis=0, tiled=True)  7.25 us
    pallas_call x1, Pallas kernels, cut_tile(): pl.pallas_call(cut_kernel, grid=(rows // HALF_LANES,), out_shape=jax.Shap...  6.4 us
    all_to_all x1, starting transfers between devices, per_device(): lax.all_to_all(spread, ('row', 'col'), split_axis=0, concat_axis=0, tiled...  4.91 us
  transfers between devices with their start and end apart: 2, of which 2 were waited for; matrix products, arithmetic and copies ran while one was open for 0% of the time, Pallas kernels for 7%

profile of v10, /device:TPU:0, one launch (start us, length us, event | category | flops | bytes accessed | tf_op | source)
XLA Modules:
  0.0 96.0 jit_solution(3323074727351989389)
XLA Ops:
  0.6 0.7 copy_convert_fusion
  1.4 0.7 fusion.29
  2.1 0.7 fusion.22
  2.8 0.1 concatenate.10
  2.9 0.7 fusion.1
  3.6 0.7 broadcast_in_dim.38
  4.3 7.3 %all-to-all-start = ((bf16[8,96,128]{2,1,0:T(8,128)(2,1)}), bf16[8,96,128]{2,1,0:T(8,128)(2,1)S(1)}, u32[]{:S(2)}, u32[]{:S(2)}) async-start(bf16[8,96,128]{2,1,0:T(8,128)(2,1)} %broadcast_in_dim.38), calls=%async_computation | async-start | bytes 393216 | tf_op jit(solution)/shard_map/all_to_all | solution.py:570
  11.6 6.4 %shard_map.86.blocks_ref = bf16[7,1040,256]{2,1,0:T(8,128)(2,1)} custom-call(bf16[1024,1024]{1,0:T(8,128)(2,1)} %tile_ref.1), custom_call_target="tpu_custom_call" | custom-call | bytes 5767168 | tf_op jit(solution)/shard_map/pallas_call | solution.py:493
  18.0 0.1 broadcast_and_fusion
  18.1 1.4 %all-to-all-done = bf16[8,96,128]{2,1,0:T(8,128)(2,1)S(1)} async-done(((bf16[8,96,128]{2,1,0:T(8,128)(2,1)}), bf16[8,96,128]{2,1,0:T(8,128)(2,1)S(1)}, u32[]{:S(2)}, u32[]{:S(2)}) %all-to-all-start) | async-done | bytes 196640 | tf_op jit(solution)/shard_map/all_to_all | solution.py:570
  19.5 9.1 %all-gather.everyone_ref = bf16[32,96,128]{2,1,0:T(8,128)(2,1)} all-gather(bf16[8,96,128]{2,1,0:T(8,128)(2,1)S(1)} %all-to-all-done), channel_id=2, replica_groups=mesh['row'=4,'col'=8] {'row'}, dimensions={0}, use_global_device_ids=true | all-gather | bytes 983040 | tf_op jit(solution)/shard_map/all_gather | solution.py:571
  28.6 53.1 %shard_map.87 = f32[32,8,128]{2,1,0:T(8,128)} custom-call(bf16[32,96,128]{2,1,0:T(8,128)(2,1)} %all-gather.everyone_ref, bf16[7,1040,256]{2,1,0:T(8,128)(2,1)} %shard_map.86.blocks_ref, bf16[1648,256]{1,0:T(8,128)(2,1)} %constant.76.clone.tables_ref), custom_call_target="tpu_custom_call" | custom-call | tf_op jit(solution)/shard_map/pallas_call | solution.py:511
  81.7 4.9 %all-to-all-start.1 = ((f32[32,8,128]{2,1,0:T(8,128)}), f32[32,8,128]{2,1,0:T(8,128)S(1)}, u32[]{:S(2)}, u32[]{:S(2)}) async-start(f32[32,8,128]{2,1,0:T(8,128)} %shard_map.87), calls=%async_computation.1 | async-start | bytes 262144 | tf_op jit(solution)/shard_map/all_to_all | solution.py:575
  86.6 0.1 broadcast_and_fusion.1
  86.7 7.6 %all-to-all-done.1 = f32[32,8,128]{2,1,0:T(8,128)S(1)} async-done(((f32[32,8,128]{2,1,0:T(8,128)}), f32[32,8,128]{2,1,0:T(8,128)S(1)}, u32[]{:S(2)}, u32[]{:S(2)}) %all-to-all-start.1) | async-done | bytes 131104 | tf_op jit(solution)/shard_map/all_to_all | solution.py:575
  94.3 0.1 fusion.31
  94.4 0.1 fusion.18
  94.5 0.7 pad_maximum_fusion.1
  95.2 0.1 fusion.8
  95.3 0.1 fusion.16
  95.4 0.6 copy.17
  (8 shorter events, 0.1 us)
Async XLA Ops:
  4.3 15.2 %all-to-all-start = ((bf16[8,96,128]{2,1,0:T(8,128)(2,1)}), bf16[8,96,128]{2,1,0:T(8,128)(2,1)S(1)}, u32[]{:S(2)}, u32[]{:S(2)}) async-start(bf16[8,96,128]{2,1,0:T(8,128)(2,1)} %broadcast_in_dim.38), calls=%async_computation | async-start | bytes 393216 | tf_op jit(solution)/shard_map/all_to_all | solution.py:570
  81.7 12.7 %all-to-all-start.1 = ((f32[32,8,128]{2,1,0:T(8,128)}), f32[32,8,128]{2,1,0:T(8,128)S(1)}, u32[]{:S(2)}, u32[]{:S(2)}) async-start(f32[32,8,128]{2,1,0:T(8,128)} %shard_map.87), calls=%async_computation.1 | async-start | bytes 262144 | tf_op jit(solution)/shard_map/all_to_all | solution.py:575

commit v11 on v9

--- a/solution.py
+++ b/solution.py
@@ -157,14 +157,13 @@
     a_ref[:, : PATCH // 2, :] = rim
     a_ref[:, a_ref.shape[1] - PATCH // 2 :, :] = rim
 
-    @pl.loop(0, n_row)
-    def _(row):
+    for row in range(n_row):
         strip = jnp.concatenate(
             [everyone_ref[row * n_col + col, :a_rows, :] for col in range(n_col)], axis=1
         )
-        place = pl.ds(pl.multiple_of(PATCH // 2 + row * a_rows, 16), a_rows)
+        start = PATCH // 2 + row * a_rows
         for block in range(1, a_ref.shape[0]):
-            a_ref[block, place, :] = cut(strip, (block - 1) * PATCH)
+            a_ref[block, start : start + a_rows, :] = cut(strip, (block - 1) * PATCH)
 
     def at(step, stage, part):
         return jnp.clip(BATCH * (step - stage) + part, 0, capacity - 1)
@@ -475,6 +474,45 @@
     return jnp.max(before).astype(jnp.int32)
 
 
+def pack_kernel(
+    a_ref, owners_ref, rows_ref, cols_ref, peaks_ref, sent_ref, records_ref
+):
+    node_rows, node_cols = rows_ref.shape
+    mesh_col = lax.broadcasted_iota(jnp.int32, (node_rows, node_cols), 1)
+    mesh_col = mesh_col + lax.axis_index("col") * node_cols
+    fields = (
+        owners_ref[...],
+        rows_ref[...] >> 4,
+        rows_ref[...] & 15,
+        cols_ref[...] >> 4,
+        cols_ref[...] & 15,
+        peaks_ref[0],
+        peaks_ref[1],
+        mesh_col,
+    )
+    records_ref[...] = jnp.full(records_ref.shape, -1.0, jnp.float32)
+    for index, values in enumerate(fields):
+        lanes = slice(index * NODE_LANES, (index + 1) * NODE_LANES)
+        records_ref[:node_rows, lanes] = values.astype(jnp.float32)
+    records = records_ref[...].astype(jnp.bfloat16)
+    height = a_ref.shape[0]
+    for receiver in range(sent_ref.shape[0]):
+        sent_ref[receiver, :height, :] = a_ref[...]
+        sent_ref[receiver, height:, :] = records
+
+
+def pack(a_window, owners, pos_rows, pos_cols, peaks, receivers):
+    height, lanes = a_window.shape
+    vmem = pl.BlockSpec(memory_space=pltpu.VMEM)
+    return pl.pallas_call(
+        pack_kernel,
+        out_shape=jax.ShapeDtypeStruct((receivers, height + 16, lanes), jnp.bfloat16),
+        in_specs=[vmem] * 5,
+        out_specs=vmem,
+        scratch_shapes=[pltpu.VMEM((16, lanes), jnp.float32)],
+    )(a_window, owners, pos_rows, pos_cols, peaks)
+
+
 def cut_kernel(tile_ref, out_ref):
     strip = tile_ref[...]
     for block in range(out_ref.shape[0]):
@@ -544,23 +582,9 @@
     a_rows, a_cols = a_window.shape
     height, breadth = n_row * node_rows, n_col * node_cols
 
-    mesh_col = me_col * node_cols + lax.broadcasted_iota(jnp.int32, pos_rows.shape, 1)
-    records = jnp.concatenate(
-        [
-            owners.reshape(node_rows, node_cols),
-            pos_rows // 16,
-            pos_rows % 16,
-            pos_cols // 16,
-            pos_cols % 16,
-            peaks[0],
-            peaks[1],
-            mesh_col,
-        ],
-        axis=1,
-    ).astype(jnp.bfloat16)
-    records = jnp.pad(records, ((0, 16 - node_rows), (0, 0)), constant_values=-1)
-    sent = jnp.concatenate([a_window, records], axis=0)
-    sent = jnp.broadcast_to(sent[None], (n_col,) + sent.shape)
+    sent = pack(
+        a_window, owners.reshape(node_rows, node_cols), pos_rows, pos_cols, peaks, n_col
+    )
     sent = lax.all_to_all(sent, "col", split_axis=0, concat_axis=0, tiled=True)
     everyone = lax.all_gather(sent, "row").reshape(devices, a_rows + 16, a_cols)
 

time: 96.4 us -> 96.6 us (level)
  Pallas kernels: 38.8 us -> 62.4 us
  starting transfers between devices: 32.2 us -> 9.84 us
  other arithmetic: 4.02 us -> 1.15 us
  local copies, waits for them, and re-layouts: 1.48 us -> 3.27 us
    all_to_all x1, starting transfers between devices: 24.9 us -> 2.59 us  [per_device(): lax.all_to_all(spread, ('row', 'col'), split_axis=0, concat_axis=0, tiled...]
    pallas_call x1, Pallas kernels: 32.4 us -> 54.4 us  [correlate(): pl.pallas_call(functools.partial(correlate_kernel, capacity, grid, places...]
    unnamed x1 -> x3, local copies, waits for them, and re-layouts: 0.61 us -> 3.2 us
    pallas_call x0 -> x1, Pallas kernels: none -> 1.54 us  [pack(): pl.pallas_call(pack_kernel, out_shape=jax.ShapeDtypeStruct((receivers, he...]
    another operation x3 -> x0, other arithmetic: 1.45 us -> none
where the time goes in v11:
time: 96.6 us; the launch traced here: 95.4 us
  Pallas kernels  62.4 us (65%)
  starting transfers between devices  9.84 us (10%)
  blocking collectives  9.06 us (9%)
  waiting for transfers between devices  9.04 us (9%)
  local copies, waits for them, and re-layouts  3.27 us (3%)
  other arithmetic  1.15 us (1%)
    pallas_call x1, Pallas kernels, correlate(): pl.pallas_call(functools.partial(correlate_kernel, capacity, grid, places...  54.4 us
    all_gather x1, blocking collectives, per_device(): everyone = lax.all_gather(sent, 'row').reshape(devices, a_rows + 16, a_cols)  9.06 us
    all_to_all x1, waiting for transfers between devices, per_device(): lax.all_to_all(spread, ('row', 'col'), split_axis=0, concat_axis=0, tiled...  7.65 us
    all_to_all x1, starting transfers between devices, per_device(): sent = lax.all_to_all(sent, 'col', split_axis=0, concat_axis=0, tiled=True)  7.25 us
    pallas_call x1, Pallas kernels, cut_tile(): pl.pallas_call(cut_kernel, grid=(rows // HALF_LANES,), out_shape=jax.Shap...  6.45 us
    unnamed x3, local copies, waits for them, and re-layouts  3.2 us
    all_to_all x1, starting transfers between devices, per_device(): lax.all_to_all(spread, ('row', 'col'), split_axis=0, concat_axis=0, tiled...  2.59 us
  transfers between devices with their start and end apart: 2, of which 2 were waited for; matrix products, arithmetic and copies ran while one was open for 0% of the time, Pallas kernels for 7%

profile of v11, /device:TPU:0, one launch (start us, length us, event | category | flops | bytes accessed | tf_op | source)
XLA Modules:
  0.0 95.4 jit_solution(6165932520722720564)
XLA Ops:
  0.6 1.3 %copy.15 = s32[1,1,10,16,1]{3,2,4,1,0:T(8,128)} copy(s32[1,1,10,16,1]{3,4,2,1,0:T(1,128)} %param.9) | data formatting | bytes 1280
  1.9 1.3 %copy.11.peaks_ref = s32[2,10,16]{2,1,0:T(8,128)} copy(s32[2,10,16]{2,0,1:T(2,128)} %param.12) | data formatting | bytes 2560 | tf_op args[5]
  3.2 1.5 %shard_map.86 = bf16[8,96,128]{2,1,0:T(8,128)(2,1)} custom-call(bf16[80,128]{1,0:T(8,128)(2,1)} %a_ref.1, s32[10,16]{1,0:T(8,128)} %bitcast.7, s32[10,16]{1,0:T(8,128)} %rows_ref.1, s32[10,16]{1,0:T(8,128)} %cols_ref.1, s32[2,10,16]{2,1,0:T(8,128)} %copy.11.peaks_ref), custom_call_target="tpu_custom_call" | custom-call | tf_op jit(solution)/shard_map/pallas_call | solution.py:507
  4.8 7.3 %all-to-all-start = ((bf16[8,96,128]{2,1,0:T(8,128)(2,1)}), bf16[8,96,128]{2,1,0:T(8,128)(2,1)S(1)}, u32[]{:S(2)}, u32[]{:S(2)}) async-start(bf16[8,96,128]{2,1,0:T(8,128)(2,1)} %shard_map.86), calls=%async_computation | async-start | bytes 393216 | tf_op jit(solution)/shard_map/all_to_all | solution.py:588
  12.0 6.5 %shard_map.87.blocks_ref = bf16[7,1040,256]{2,1,0:T(8,128)(2,1)} custom-call(bf16[1024,1024]{1,0:T(8,128)(2,1)} %tile_ref.1), custom_call_target="tpu_custom_call" | custom-call | bytes 5767168 | tf_op jit(solution)/shard_map/pallas_call | solution.py:525
  18.5 0.1 broadcast_and_fusion
  18.6 1.4 %all-to-all-done = bf16[8,96,128]{2,1,0:T(8,128)(2,1)S(1)} async-done(((bf16[8,96,128]{2,1,0:T(8,128)(2,1)}), bf16[8,96,128]{2,1,0:T(8,128)(2,1)S(1)}, u32[]{:S(2)}, u32[]{:S(2)}) %all-to-all-start) | async-done | bytes 196640 | tf_op jit(solution)/shard_map/all_to_all | solution.py:588
  20.0 9.1 %all-gather.everyone_ref = bf16[32,96,128]{2,1,0:T(8,128)(2,1)} all-gather(bf16[8,96,128]{2,1,0:T(8,128)(2,1)S(1)} %all-to-all-done), channel_id=2, replica_groups=mesh['row'=4,'col'=8] {'row'}, dimensions={0}, use_global_device_ids=true | all-gather | bytes 983040 | tf_op jit(solution)/shard_map/all_gather | solution.py:589
  29.0 54.4 %shard_map.88 = f32[32,8,128]{2,1,0:T(8,128)} custom-call(bf16[32,96,128]{2,1,0:T(8,128)(2,1)} %all-gather.everyone_ref, bf16[7,1040,256]{2,1,0:T(8,128)(2,1)} %shard_map.87.blocks_ref, bf16[1648,256]{1,0:T(8,128)(2,1)} %constant.9.clone.tables_ref), custom_call_target="tpu_custom_call" | custom-call | tf_op jit(solution)/shard_map/pallas_call | solution.py:543
  83.4 2.6 %all-to-all-start.1 = ((f32[32,8,128]{2,1,0:T(8,128)}), f32[32,8,128]{2,1,0:T(8,128)S(1)}, u32[]{:S(2)}, u32[]{:S(2)}) async-start(f32[32,8,128]{2,1,0:T(8,128)} %shard_map.88), calls=%async_computation.1 | async-start | bytes 262144 | tf_op jit(solution)/shard_map/all_to_all | solution.py:593
  86.0 0.1 broadcast_and_fusion.1
  86.1 7.6 %all-to-all-done.1 = f32[32,8,128]{2,1,0:T(8,128)S(1)} async-done(((f32[32,8,128]{2,1,0:T(8,128)}), f32[32,8,128]{2,1,0:T(8,128)S(1)}, u32[]{:S(2)}, u32[]{:S(2)}) %all-to-all-start.1) | async-done | bytes 131104 | tf_op jit(solution)/shard_map/all_to_all | solution.py:593
  93.8 0.1 fusion.19
  93.8 0.1 fusion.16
  93.9 0.7 pad_maximum_fusion.1
  94.6 0.1 fusion.6
  94.7 0.1 fusion.14
  94.8 0.6 copy.12
  (5 shorter events, 0.1 us)
Async XLA Ops:
  4.8 15.2 %all-to-all-start = ((bf16[8,96,128]{2,1,0:T(8,128)(2,1)}), bf16[8,96,128]{2,1,0:T(8,128)(2,1)S(1)}, u32[]{:S(2)}, u32[]{:S(2)}) async-start(bf16[8,96,128]{2,1,0:T(8,128)(2,1)} %shard_map.86), calls=%async_computation | async-start | bytes 393216 | tf_op jit(solution)/shard_map/all_to_all | solution.py:588
  83.4 10.3 %all-to-all-start.1 = ((f32[32,8,128]{2,1,0:T(8,128)}), f32[32,8,128]{2,1,0:T(8,128)S(1)}, u32[]{:S(2)}, u32[]{:S(2)}) async-start(f32[32,8,128]{2,1,0:T(8,128)} %shard_map.88), calls=%async_computation.1 | async-start | bytes 262144 | tf_op jit(solution)/shard_map/all_to_all | solution.py:593

commit v12 on v9

--- a/solution.py
+++ b/solution.py
@@ -18,7 +18,7 @@
 WIDE = 256
 HALF_LANES = 128
 FREQS = PATCH // 2 + 1
-GROUPS = 11
+GROUPS = 10
 PAIRED = 16 * GROUPS
 BIG = 3.0e38
 
@@ -49,12 +49,12 @@
     back_across[HALF_LANES : HALF_LANES + FREQS, :PATCH] = 0.5 * (sine * weights).T
     down = np.zeros((PAIRED, PATCH), np.float32)
     back_down = np.zeros((PATCH, PAIRED), np.float32)
-    for freq in range(FREQS):
+    for freq in range(FREQS - 1):
         row = 16 * (freq // 8) + freq % 8
         down[row] = cosine[:, freq]
-        down[row + 8] = sine[:, freq]
+        down[row + 8] = sine[:, freq] if freq else cosine[:, -1]
         back_down[:, row] = cosine[:, freq] * weights[freq]
-        back_down[:, row + 8] = sine[:, freq] * weights[freq]
+        back_down[:, row + 8] = sine[:, freq] * weights[freq] if freq else cosine[:, -1]
     return across, down, back_down, back_across
 
 
@@ -157,14 +157,13 @@
     a_ref[:, : PATCH // 2, :] = rim
     a_ref[:, a_ref.shape[1] - PATCH // 2 :, :] = rim
 
-    @pl.loop(0, n_row)
-    def _(row):
+    for row in range(n_row):
         strip = jnp.concatenate(
             [everyone_ref[row * n_col + col, :a_rows, :] for col in range(n_col)], axis=1
         )
-        place = pl.ds(pl.multiple_of(PATCH // 2 + row * a_rows, 16), a_rows)
+        start = PATCH // 2 + row * a_rows
         for block in range(1, a_ref.shape[0]):
-            a_ref[block, place, :] = cut(strip, (block - 1) * PATCH)
+            a_ref[block, start : start + a_rows, :] = cut(strip, (block - 1) * PATCH)
 
     def at(step, stage, part):
         return jnp.clip(BATCH * (step - stage) + part, 0, capacity - 1)
@@ -219,7 +218,7 @@
         sc = spec[16 * group + 8 : 16 * group + 16, :HALF_LANES]
         ss = spec[16 * group + 8 : 16 * group + 16, HALF_LANES:]
         power = (cc * cc + cs * cs) + (sc * sc + ss * ss)
-        return cc - ss, sc + cs, cc + ss, sc - cs, power
+        return (cc - ss, sc + cs, cc + ss, sc - cs, power), (cc, cs, sc, ss)
 
     def stage_inverse():
         down = table("down")
@@ -229,20 +228,24 @@
             spec_a = jnp.dot(down, halves[trio, 0, tile], preferred_element_type=jnp.float32)
             spec_b = jnp.dot(down, halves[trio, 1, tile], preferred_element_type=jnp.float32)
             for group in range(GROUPS):
-                a_pr, a_pi, a_mr, a_mi, a_power = sides(spec_a, group)
-                b_pr, b_pi, b_mr, b_mi, b_power = sides(spec_b, group)
+                (a_pr, a_pi, a_mr, a_mi, a_power), a_plain = sides(spec_a, group)
+                (b_pr, b_pi, b_mr, b_mi, b_power), b_plain = sides(spec_b, group)
                 if group == 0:
                     powers = [jnp.where(top, 0.5 * power, power) for power in (a_power, b_power)]
-                elif group < GROUPS - 1:
+                else:
                     powers = [powers[0] + a_power, powers[1] + b_power]
-                else:
-                    powers = [powers[0] + 0.5 * a_power, powers[1] + 0.5 * b_power]
                 pr = a_pr * b_pr + a_pi * b_pi
                 pi = a_pr * b_pi - a_pi * b_pr
                 mr = a_mr * b_mr + a_mi * b_mi
                 mi = a_mr * b_mi - a_mi * b_mr
-                upper = jnp.concatenate([pr + mr, pi - mi], axis=1)
-                lower = jnp.concatenate([pi + mi, mr - pr], axis=1)
+                outs = [pr + mr, pi - mi, pi + mi, mr - pr]
+                if group == 0:
+                    for half in (0, 2):
+                        (ar, ai), (br, bi) = a_plain[half : half + 2], b_plain[half : half + 2]
+                        outs[half] = jnp.where(top, 2.0 * (ar * br + ai * bi), outs[half])
+                        outs[half + 1] = jnp.where(top, 2.0 * (ar * bi - ai * br), outs[half + 1])
+                upper = jnp.concatenate(outs[:2], axis=1)
+                lower = jnp.concatenate(outs[2:], axis=1)
                 crosses[pair, 16 * group : 16 * group + 16, :] = jnp.concatenate(
                     [upper, lower], axis=0
                 ).astype(jnp.bfloat16)

time: 96.4 us -> 95.7 us (level)
  starting transfers between devices: 32.2 us -> 30.5 us
    all_to_all x1, starting transfers between devices: 24.9 us -> 23.2 us  [per_device(): lax.all_to_all(spread, ('row', 'col'), split_axis=0, concat_axis=0, tiled...]
where the time goes in v12:
time: 95.7 us; the launch traced here: 94.5 us
  Pallas kernels  39.7 us (41%)
  starting transfers between devices  30.5 us (32%)
  waiting for transfers between devices  9.09 us (9%)
  blocking collectives  9.06 us (9%)
  other arithmetic  4.02 us (4%)
  local copies, waits for them, and re-layouts  1.48 us (2%)
    pallas_call x1, Pallas kernels, correlate(): pl.pallas_call(functools.partial(correlate_kernel, capacity, grid, places...  33.3 us
    all_to_all x1, starting transfers between devices, per_device(): lax.all_to_all(spread, ('row', 'col'), split_axis=0, concat_axis=0, tiled...  23.2 us
    all_gather x1, blocking collectives, per_device(): everyone = lax.all_gather(sent, 'row').reshape(devices, a_rows + 16, a_cols)  9.06 us
    all_to_all x1, waiting for transfers between devices, per_device(): lax.all_to_all(spread, ('row', 'col'), split_axis=0, concat_axis=0, tiled...  7.65 us
    all_to_all x1, starting transfers between devices, per_device(): sent = lax.all_to_all(sent, 'col', split_axis=0, concat_axis=0, tiled=True)  7.25 us
    pallas_call x1, Pallas kernels, cut_tile(): pl.pallas_call(cut_kernel, grid=(rows // HALF_LANES,), out_shape=jax.Shap...  6.4 us
  transfers between devices with their start and end apart: 2, of which 2 were waited for; matrix products, arithmetic and copies ran while one was open for 0% of the time, Pallas kernels for 7%

profile of v12, /device:TPU:0, one launch (start us, length us, event | category | flops | bytes accessed | tf_op | source)
XLA Modules:
  0.0 94.5 jit_solution(10406276683157305385)
XLA Ops:
  0.6 0.7 copy_convert_fusion
  1.4 0.7 fusion.29
  2.1 0.7 fusion.22
  2.8 0.1 concatenate.10
  2.9 0.7 fusion.1
  3.6 0.7 broadcast_in_dim.38
  4.3 7.3 %all-to-all-start = ((bf16[8,96,128]{2,1,0:T(8,128)(2,1)}), bf16[8,96,128]{2,1,0:T(8,128)(2,1)S(1)}, u32[]{:S(2)}, u32[]{:S(2)}) async-start(bf16[8,96,128]{2,1,0:T(8,128)(2,1)} %broadcast_in_dim.38), calls=%async_computation | async-start | bytes 393216 | tf_op jit(solution)/shard_map/all_to_all | solution.py:567
  11.6 6.4 %shard_map.86.blocks_ref = bf16[7,1040,256]{2,1,0:T(8,128)(2,1)} custom-call(bf16[1024,1024]{1,0:T(8,128)(2,1)} %tile_ref.1), custom_call_target="tpu_custom_call" | custom-call | bytes 5767168 | tf_op jit(solution)/shard_map/pallas_call | solution.py:490
  18.0 0.1 broadcast_and_fusion
  18.1 1.4 %all-to-all-done = bf16[8,96,128]{2,1,0:T(8,128)(2,1)S(1)} async-done(((bf16[8,96,128]{2,1,0:T(8,128)(2,1)}), bf16[8,96,128]{2,1,0:T(8,128)(2,1)S(1)}, u32[]{:S(2)}, u32[]{:S(2)}) %all-to-all-start) | async-done | bytes 196640 | tf_op jit(solution)/shard_map/all_to_all | solution.py:567
  19.5 9.1 %all-gather.everyone_ref = bf16[32,96,128]{2,1,0:T(8,128)(2,1)} all-gather(bf16[8,96,128]{2,1,0:T(8,128)(2,1)S(1)} %all-to-all-done), channel_id=2, replica_groups=mesh['row'=4,'col'=8] {'row'}, dimensions={0}, use_global_device_ids=true | all-gather | bytes 983040 | tf_op jit(solution)/shard_map/all_gather | solution.py:568
  28.6 33.3 %shard_map.87 = f32[32,8,128]{2,1,0:T(8,128)} custom-call(bf16[32,96,128]{2,1,0:T(8,128)(2,1)} %all-gather.everyone_ref, bf16[7,1040,256]{2,1,0:T(8,128)(2,1)} %shard_map.86.blocks_ref, bf16[1632,256]{1,0:T(8,128)(2,1)} %constant.76.clone.tables_ref), custom_call_target="tpu_custom_call" | custom-call | tf_op jit(solution)/shard_map/pallas_call | solution.py:508
  61.9 23.2 %all-to-all-start.1 = ((f32[32,8,128]{2,1,0:T(8,128)}), f32[32,8,128]{2,1,0:T(8,128)S(1)}, u32[]{:S(2)}, u32[]{:S(2)}) async-start(f32[32,8,128]{2,1,0:T(8,128)} %shard_map.87), calls=%async_computation.1 | async-start | bytes 262144 | tf_op jit(solution)/shard_map/all_to_all | solution.py:572
  85.1 0.1 broadcast_and_fusion.1
  85.2 7.6 %all-to-all-done.1 = f32[32,8,128]{2,1,0:T(8,128)S(1)} async-done(((f32[32,8,128]{2,1,0:T(8,128)}), f32[32,8,128]{2,1,0:T(8,128)S(1)}, u32[]{:S(2)}, u32[]{:S(2)}) %all-to-all-start.1) | async-done | bytes 131104 | tf_op jit(solution)/shard_map/all_to_all | solution.py:572
  92.9 0.1 fusion.31
  92.9 0.1 fusion.18
  93.0 0.7 pad_maximum_fusion.1
  93.7 0.1 fusion.8
  93.8 0.1 fusion.16
  93.9 0.6 copy.17
  (8 shorter events, 0.1 us)
Async XLA Ops:
  4.3 15.2 %all-to-all-start = ((bf16[8,96,128]{2,1,0:T(8,128)(2,1)}), bf16[8,96,128]{2,1,0:T(8,128)(2,1)S(1)}, u32[]{:S(2)}, u32[]{:S(2)}) async-start(bf16[8,96,128]{2,1,0:T(8,128)(2,1)} %broadcast_in_dim.38), calls=%async_computation | async-start | bytes 393216 | tf_op jit(solution)/shard_map/all_to_all | solution.py:567
  61.9 30.9 %all-to-all-start.1 = ((f32[32,8,128]{2,1,0:T(8,128)}), f32[32,8,128]{2,1,0:T(8,128)S(1)}, u32[]{:S(2)}, u32[]{:S(2)}) async-start(f32[32,8,128]{2,1,0:T(8,128)} %shard_map.87), calls=%async_computation.1 | async-start | bytes 262144 | tf_op jit(solution)/shard_map/all_to_all | solution.py:572

commit v13 on v12

--- a/solution.py
+++ b/solution.py
@@ -55,7 +55,17 @@
         down[row + 8] = sine[:, freq] if freq else cosine[:, -1]
         back_down[:, row] = cosine[:, freq] * weights[freq]
         back_down[:, row + 8] = sine[:, freq] * weights[freq] if freq else cosine[:, -1]
-    return across, down, back_down, back_across
+    halves = [slice(0, HALF_LANES), slice(HALF_LANES, WIDE)]
+    turns = (0, SECOND, THIRD)
+    across = [
+        np.concatenate([np.roll(across[:, half], turn, axis=1) for half in halves], axis=1)
+        for turn in turns
+    ]
+    back_across = [
+        np.concatenate([np.roll(back_across[half], turn, axis=0) for half in halves])
+        for turn in turns
+    ]
+    return *across, *back_across, down, back_down
 
 
 def listing_tables():
@@ -74,8 +84,9 @@
 
 
 def all_tables():
-    names = ("across", "down", "back_down", "back_across", "repeat", "within")
-    names += ("below", "above", "count", "fields", "turned")
+    names = tuple(f"across{place}" for place in range(TRIO))
+    names += tuple(f"back_across{place}" for place in range(TRIO))
+    names += ("down", "back_down", "repeat", "within", "below", "above", "count", "fields", "turned")
     places, parts, start = {}, [], 0
     for name, part in zip(names, kernel_tables() + listing_tables()):
         rows, lanes = part.shape
@@ -181,9 +192,11 @@
         for place, values in enumerate(groups):
             patches[base + 16 * place : base + 16 * place + 16, :] = values
 
+    trios = BATCH // TRIO
+
     def patch_base(part, which):
         trio, place = divmod(part, TRIO)
-        return ((2 * trio + which) * TRIO + place) * PATCH
+        return ((trios * place + trio) * 2 + which) * PATCH
 
     def stage_half(step):
         for part in range(BATCH):
@@ -194,17 +207,21 @@
             ):
                 block, row, row_rest, col_rest = (items_ref[field, item] for field in fields)
                 extract(source, block, row, row_rest, col_rest, patch_base(part, which))
-        half = jnp.dot(patches[...], table("across"), preferred_element_type=jnp.float32)
+        rows = 2 * trios * PATCH
+        turned = [
+            jnp.dot(
+                patches[rows * place : rows * (place + 1), :],
+                table(f"across{place}"),
+                preferred_element_type=jnp.float32,
+            )
+            for place in range(TRIO)
+        ]
         lanes = lax.broadcasted_iota(jnp.int32, (PATCH, HALF_LANES), 1)
         for trio in range(BATCH // TRIO):
             for which in range(2):
                 for side in (slice(0, HALF_LANES), slice(HALF_LANES, WIDE)):
-                    first, second, third = (
-                        half[base : base + PATCH, side]
-                        for base in (patch_base(TRIO * trio + n, which) for n in range(TRIO))
-                    )
-                    second = pltpu.roll(second, SECOND, axis=1)
-                    third = pltpu.roll(third, THIRD, axis=1)
+                    base = (2 * trio + which) * PATCH
+                    first, second, third = (half[base : base + PATCH, side] for half in turned)
                     halves[trio, which, 0, :, side] = jnp.where(
                         lanes < SECOND, first, second
                     ).astype(jnp.bfloat16)
@@ -262,16 +279,20 @@
             for side in (slice(0, HALF_LANES), slice(HALF_LANES, WIDE)):
                 first = low[:, side]
                 second = jnp.where(lanes >= SECOND, first, high[:, side])
-                second = pltpu.roll(second, HALF_LANES - SECOND, axis=1)
-                third = pltpu.roll(high[:, side], HALF_LANES - THIRD, axis=1)
+                third = high[:, side]
                 for place, inverse in enumerate((first, second, third)):
-                    base = (TRIO * trio + place) * PATCH
+                    base = (trios * place + trio) * PATCH
                     inverses[base : base + PATCH, side] = inverse.astype(jnp.bfloat16)
 
     def stage_score(step):
-        corr_all = jnp.dot(
-            inverses[...], table("back_across"), preferred_element_type=jnp.float32
-        )
+        corr_all = [
+            jnp.dot(
+                inverses[trios * PATCH * place : trios * PATCH * (place + 1), :],
+                table(f"back_across{place}"),
+                preferred_element_type=jnp.float32,
+            )
+            for place in range(TRIO)
+        ]
         rows = lax.broadcasted_iota(jnp.int32, (8, HALF_LANES), 0)
         lanes = lax.broadcasted_iota(jnp.int32, (8, HALF_LANES), 1)
         shift_rows = (rows - centre_reach).astype(jnp.float32)
@@ -297,8 +318,8 @@
             total, row_moment, col_moment = 0.0, 0.0, 0.0
             best = None
             for half in range(2):
-                corr = corr_all[
-                    PATCH * part : PATCH * (part + 1),
+                corr = corr_all[part % TRIO][
+                    PATCH * (part // TRIO) : PATCH * (part // TRIO + 1),
                     half * HALF_LANES : (half + 1) * HALF_LANES,
                 ]
                 edge = jnp.concatenate([corr[PATCH - ABOVE :], corr[:BELOW]], axis=0)

time: 95.7 us -> 96.8 us (1.011)
  Pallas kernels: 39.7 us -> 61.4 us
  starting transfers between devices: 30.5 us -> 9.86 us
    pallas_call x1, Pallas kernels: 33.3 us -> 55 us  [correlate(): pl.pallas_call(functools.partial(correlate_kernel, capacity, grid, places...]
    all_to_all x1, starting transfers between devices: 23.2 us -> 2.6 us  [per_device(): lax.all_to_all(spread, ('row', 'col'), split_axis=0, concat_axis=0, tiled...]
where the time goes in v13:
time: 96.8 us; the launch traced here: 95.6 us
  Pallas kernels  61.4 us (63%)
  starting transfers between devices  9.86 us (10%)
  waiting for transfers between devices  9.09 us (9%)
  blocking collectives  9.06 us (9%)
  other arithmetic  4.02 us (4%)
  local copies, waits for them, and re-layouts  1.48 us (2%)
    pallas_call x1, Pallas kernels, correlate(): pl.pallas_call(functools.partial(correlate_kernel, capacity, grid, places...  55 us
    all_gather x1, blocking collectives, per_device(): everyone = lax.all_gather(sent, 'row').reshape(devices, a_rows + 16, a_cols)  9.06 us
    all_to_all x1, waiting for transfers between devices, per_device(): lax.all_to_all(spread, ('row', 'col'), split_axis=0, concat_axis=0, tiled...  7.65 us
    all_to_all x1, starting transfers between devices, per_device(): sent = lax.all_to_all(sent, 'col', split_axis=0, concat_axis=0, tiled=True)  7.25 us
    pallas_call x1, Pallas kernels, cut_tile(): pl.pallas_call(cut_kernel, grid=(rows // HALF_LANES,), out_shape=jax.Shap...  6.4 us
    all_to_all x1, starting transfers between devices, per_device(): lax.all_to_all(spread, ('row', 'col'), split_axis=0, concat_axis=0, tiled...  2.6 us
  transfers between devices with their start and end apart: 2, of which 2 were waited for; matrix products, arithmetic and copies ran while one was open for 0% of the time, Pallas kernels for 7%

profile of v13, /device:TPU:0, one launch (start us, length us, event | category | flops | bytes accessed | tf_op | source)
XLA Modules:
  0.0 95.6 jit_solution(2561147860592882323)
XLA Ops:
  0.6 0.7 copy_convert_fusion
  1.4 0.7 fusion.29
  2.1 0.7 fusion.22
  2.8 0.1 concatenate.10
  2.9 0.7 fusion.1
  3.6 0.7 broadcast_in_dim.38
  4.3 7.3 %all-to-all-start = ((bf16[8,96,128]{2,1,0:T(8,128)(2,1)}), bf16[8,96,128]{2,1,0:T(8,128)(2,1)S(1)}, u32[]{:S(2)}, u32[]{:S(2)}) async-start(bf16[8,96,128]{2,1,0:T(8,128)(2,1)} %broadcast_in_dim.38), calls=%async_computation | async-start | bytes 393216 | tf_op jit(solution)/shard_map/all_to_all | solution.py:588
  11.6 6.4 %shard_map.86.blocks_ref = bf16[7,1040,256]{2,1,0:T(8,128)(2,1)} custom-call(bf16[1024,1024]{1,0:T(8,128)(2,1)} %tile_ref.1), custom_call_target="tpu_custom_call" | custom-call | bytes 5767168 | tf_op jit(solution)/shard_map/pallas_call | solution.py:511
  18.0 0.1 broadcast_and_fusion
  18.1 1.4 %all-to-all-done = bf16[8,96,128]{2,1,0:T(8,128)(2,1)S(1)} async-done(((bf16[8,96,128]{2,1,0:T(8,128)(2,1)}), bf16[8,96,128]{2,1,0:T(8,128)(2,1)S(1)}, u32[]{:S(2)}, u32[]{:S(2)}) %all-to-all-start) | async-done | bytes 196640 | tf_op jit(solution)/shard_map/all_to_all | solution.py:588
  19.5 9.1 %all-gather.everyone_ref = bf16[32,96,128]{2,1,0:T(8,128)(2,1)} all-gather(bf16[8,96,128]{2,1,0:T(8,128)(2,1)S(1)} %all-to-all-done), channel_id=2, replica_groups=mesh['row'=4,'col'=8] {'row'}, dimensions={0}, use_global_device_ids=true | all-gather | bytes 983040 | tf_op jit(solution)/shard_map/all_gather | solution.py:589
  28.6 55.0 %shard_map.87 = f32[32,8,128]{2,1,0:T(8,128)} custom-call(bf16[32,96,128]{2,1,0:T(8,128)(2,1)} %all-gather.everyone_ref, bf16[7,1040,256]{2,1,0:T(8,128)(2,1)} %shard_map.86.blocks_ref, bf16[2656,256]{1,0:T(8,128)(2,1)} %constant.76.clone.tables_ref), custom_call_target="tpu_custom_call" | custom-call | tf_op jit(solution)/shard_map/pallas_call | solution.py:529
  83.6 2.6 %all-to-all-start.1 = ((f32[32,8,128]{2,1,0:T(8,128)}), f32[32,8,128]{2,1,0:T(8,128)S(1)}, u32[]{:S(2)}, u32[]{:S(2)}) async-start(f32[32,8,128]{2,1,0:T(8,128)} %shard_map.87), calls=%async_computation.1 | async-start | bytes 262144 | tf_op jit(solution)/shard_map/all_to_all | solution.py:593
  86.2 0.1 broadcast_and_fusion.1
  86.3 7.6 %all-to-all-done.1 = f32[32,8,128]{2,1,0:T(8,128)S(1)} async-done(((f32[32,8,128]{2,1,0:T(8,128)}), f32[32,8,128]{2,1,0:T(8,128)S(1)}, u32[]{:S(2)}, u32[]{:S(2)}) %all-to-all-start.1) | async-done | bytes 131104 | tf_op jit(solution)/shard_map/all_to_all | solution.py:593
  94.0 0.1 fusion.31
  94.1 0.1 fusion.18
  94.1 0.7 pad_maximum_fusion.1
  94.8 0.1 fusion.8
  94.9 0.1 fusion.16
  95.0 0.6 copy.17
  (8 shorter events, 0.1 us)
Async XLA Ops:
  4.3 15.2 %all-to-all-start = ((bf16[8,96,128]{2,1,0:T(8,128)(2,1)}), bf16[8,96,128]{2,1,0:T(8,128)(2,1)S(1)}, u32[]{:S(2)}, u32[]{:S(2)}) async-start(bf16[8,96,128]{2,1,0:T(8,128)(2,1)} %broadcast_in_dim.38), calls=%async_computation | async-start | bytes 393216 | tf_op jit(solution)/shard_map/all_to_all | solution.py:588
  83.6 10.4 %all-to-all-start.1 = ((f32[32,8,128]{2,1,0:T(8,128)}), f32[32,8,128]{2,1,0:T(8,128)S(1)}, u32[]{:S(2)}, u32[]{:S(2)}) async-start(f32[32,8,128]{2,1,0:T(8,128)} %shard_map.87), calls=%async_computation.1 | async-start | bytes 262144 | tf_op jit(solution)/shard_map/all_to_all | solution.py:593

commit v14 on v12

--- a/solution.py
+++ b/solution.py
@@ -92,7 +92,7 @@
 A_BLOCK, A_ROW, A_ROW_REST, A_COL_REST = 4, 5, 6, 7
 NEAR_ROW, NEAR_COL = 8, 9
 FIELDS = 10
-BATCH = 6
+BATCH = 9
 TRIO = 3
 ABOVE = 24
 BELOW = 32

time: 95.7 us -> 93.3 us (0.975)
  Pallas kernels: 39.7 us -> 29.9 us
  starting transfers between devices: 30.5 us -> 38.1 us
    pallas_call x1, Pallas kernels: 33.3 us -> 23.5 us  [correlate(): pl.pallas_call(functools.partial(correlate_kernel, capacity, grid, places...]
    all_to_all x1, starting transfers between devices: 23.2 us -> 30.8 us  [per_device(): lax.all_to_all(spread, ('row', 'col'), split_axis=0, concat_axis=0, tiled...]
where the time goes in v14:
time: 93.3 us; the launch traced here: 92.4 us
  starting transfers between devices  38.1 us (41%)
  Pallas kernels  29.9 us (32%)
  waiting for transfers between devices  9.09 us (10%)
  blocking collectives  9.06 us (10%)
  other arithmetic  4.02 us (4%)
  local copies, waits for them, and re-layouts  1.48 us (2%)
    all_to_all x1, starting transfers between devices, per_device(): lax.all_to_all(spread, ('row', 'col'), split_axis=0, concat_axis=0, tiled...  30.8 us
    pallas_call x1, Pallas kernels, correlate(): pl.pallas_call(functools.partial(correlate_kernel, capacity, grid, places...  23.5 us
    all_gather x1, blocking collectives, per_device(): everyone = lax.all_gather(sent, 'row').reshape(devices, a_rows + 16, a_cols)  9.06 us
    all_to_all x1, waiting for transfers between devices, per_device(): lax.all_to_all(spread, ('row', 'col'), split_axis=0, concat_axis=0, tiled...  7.65 us
    all_to_all x1, starting transfers between devices, per_device(): sent = lax.all_to_all(sent, 'col', split_axis=0, concat_axis=0, tiled=True)  7.25 us
    pallas_call x1, Pallas kernels, cut_tile(): pl.pallas_call(cut_kernel, grid=(rows // HALF_LANES,), out_shape=jax.Shap...  6.4 us
  transfers between devices with their start and end apart: 2, of which 2 were waited for; matrix products, arithmetic and copies ran while one was open for 0% of the time, Pallas kernels for 7%

profile of v14, /device:TPU:0, one launch (start us, length us, event | category | flops | bytes accessed | tf_op | source)
XLA Modules:
  0.0 92.4 jit_solution(16273002493474545392)
XLA Ops:
  0.6 0.7 copy_convert_fusion
  1.4 0.7 fusion.29
  2.1 0.7 fusion.22
  2.8 0.1 concatenate.10
  2.9 0.7 fusion.1
  3.6 0.7 broadcast_in_dim.38
  4.3 7.3 %all-to-all-start = ((bf16[8,96,128]{2,1,0:T(8,128)(2,1)}), bf16[8,96,128]{2,1,0:T(8,128)(2,1)S(1)}, u32[]{:S(2)}, u32[]{:S(2)}) async-start(bf16[8,96,128]{2,1,0:T(8,128)(2,1)} %broadcast_in_dim.38), calls=%async_computation | async-start | bytes 393216 | tf_op jit(solution)/shard_map/all_to_all | solution.py:567
  11.6 6.4 %shard_map.86.blocks_ref = bf16[7,1040,256]{2,1,0:T(8,128)(2,1)} custom-call(bf16[1024,1024]{1,0:T(8,128)(2,1)} %tile_ref.1), custom_call_target="tpu_custom_call" | custom-call | bytes 5767168 | tf_op jit(solution)/shard_map/pallas_call | solution.py:490
  18.0 0.1 broadcast_and_fusion
  18.1 1.4 %all-to-all-done = bf16[8,96,128]{2,1,0:T(8,128)(2,1)S(1)} async-done(((bf16[8,96,128]{2,1,0:T(8,128)(2,1)}), bf16[8,96,128]{2,1,0:T(8,128)(2,1)S(1)}, u32[]{:S(2)}, u32[]{:S(2)}) %all-to-all-start) | async-done | bytes 196640 | tf_op jit(solution)/shard_map/all_to_all | solution.py:567
  19.5 9.1 %all-gather.everyone_ref = bf16[32,96,128]{2,1,0:T(8,128)(2,1)} all-gather(bf16[8,96,128]{2,1,0:T(8,128)(2,1)S(1)} %all-to-all-done), channel_id=2, replica_groups=mesh['row'=4,'col'=8] {'row'}, dimensions={0}, use_global_device_ids=true | all-gather | bytes 983040 | tf_op jit(solution)/shard_map/all_gather | solution.py:568
  28.6 23.5 %shard_map.87 = f32[32,8,128]{2,1,0:T(8,128)} custom-call(bf16[32,96,128]{2,1,0:T(8,128)(2,1)} %all-gather.everyone_ref, bf16[7,1040,256]{2,1,0:T(8,128)(2,1)} %shard_map.86.blocks_ref, bf16[1632,256]{1,0:T(8,128)(2,1)} %constant.76.clone.tables_ref), custom_call_target="tpu_custom_call" | custom-call | tf_op jit(solution)/shard_map/pallas_call | solution.py:508
  52.1 30.8 %all-to-all-start.1 = ((f32[32,8,128]{2,1,0:T(8,128)}), f32[32,8,128]{2,1,0:T(8,128)S(1)}, u32[]{:S(2)}, u32[]{:S(2)}) async-start(f32[32,8,128]{2,1,0:T(8,128)} %shard_map.87), calls=%async_computation.1 | async-start | bytes 262144 | tf_op jit(solution)/shard_map/all_to_all | solution.py:572
  83.0 0.1 broadcast_and_fusion.1
  83.1 7.6 %all-to-all-done.1 = f32[32,8,128]{2,1,0:T(8,128)S(1)} async-done(((f32[32,8,128]{2,1,0:T(8,128)}), f32[32,8,128]{2,1,0:T(8,128)S(1)}, u32[]{:S(2)}, u32[]{:S(2)}) %all-to-all-start.1) | async-done | bytes 131104 | tf_op jit(solution)/shard_map/all_to_all | solution.py:572
  90.7 0.1 fusion.31
  90.8 0.1 fusion.18
  90.9 0.7 pad_maximum_fusion.1
  91.6 0.1 fusion.8
  91.7 0.1 fusion.16
  91.8 0.6 copy.17
  (8 shorter events, 0.1 us)
Async XLA Ops:
  4.3 15.2 %all-to-all-start = ((bf16[8,96,128]{2,1,0:T(8,128)(2,1)}), bf16[8,96,128]{2,1,0:T(8,128)(2,1)S(1)}, u32[]{:S(2)}, u32[]{:S(2)}) async-start(bf16[8,96,128]{2,1,0:T(8,128)(2,1)} %broadcast_in_dim.38), calls=%async_computation | async-start | bytes 393216 | tf_op jit(solution)/shard_map/all_to_all | solution.py:567
  52.1 38.6 %all-to-all-start.1 = ((f32[32,8,128]{2,1,0:T(8,128)}), f32[32,8,128]{2,1,0:T(8,128)S(1)}, u32[]{:S(2)}, u32[]{:S(2)}) async-start(f32[32,8,128]{2,1,0:T(8,128)} %shard_map.87), calls=%async_computation.1 | async-start | bytes 262144 | tf_op jit(solution)/shard_map/all_to_all | solution.py:572
